TPU v7x, 256 devices: a whole 4x4x8 slice. The times are simulated.
256 devices in a mesh: dp: 16 (over y_lo, z), blk: 16 (over y_hi, x, core).
Axes of the slice: x: 4, y: 4 (y_hi: 2, y_lo: 2; y = y_hi * 2 + y_lo), z: 8, core: 2. Of those that a mesh axis runs over, the one named last changes fastest.
Arguments:
- queries: bfloat16 [16, 2048, 512], P('dp', 'blk'), may hold values from -6 to 6
- history_keys: bfloat16 [16, 2048, 512], P('dp', 'blk'), may hold values from -6 to 6
- history_values: bfloat16 [16, 2048, 512], P('dp', 'blk'), may hold values from -6 to 6
- gate_inputs: bfloat16 [16, 2048, 512], P('dp', 'blk'), may hold values from -6 to 6
- frequencies: float32 [4, 128, 64], replicated, may hold values from -0.5 to 0.5
- out_weight: bfloat16 [512, 1024], replicated, may hold values from -0.25 to 0.25
- lengths: int32 [16, 8], P('dp'), may hold values from 1 to 1024, 2048 in all within a row
- cotangent: bfloat16 [16, 2048, 1024], P('dp', 'blk'), may hold values from -6 to 6
Outputs:
- layer_out: bfloat16 [16, 2048, 1024], P('dp', 'blk')
- grad_queries: bfloat16 [16, 2048, 512], P('dp', 'blk')
- grad_keys: bfloat16 [16, 2048, 512], P('dp', 'blk')
- grad_values: bfloat16 [16, 2048, 512], P('dp', 'blk')
- grad_gates: bfloat16 [16, 2048, 512], P('dp', 'blk')
- grad_weight: float32 [512, 1024], P('blk')
Inputs may be any that keep to these rules, and one draw needn't show every extreme that they name: The 8 lengths of a row sum to 2048; in every row the longest history has exactly 1024 positions.
All inputs are finite; a program needn't handle non-finite values.
Results may differ from a plain program's by a relative error of at most 0.015.
Values may be sent and summed in bfloat16 or wider, within the bound.
No kernel may reach another device: no remote copies, remote signals or barrier semaphores. Data moves between devices by JAX's collectives and lax.ppermute only.
A program may use at most 64 MiB of HBM per device.

v0:
```python
import math

import jax
import jax.numpy as jnp
from jax import lax
from jax.sharding import PartitionSpec as P

EPS = 1e-05
HIGHEST_PRECISION = lax.Precision.HIGHEST


def entering(value, axis, join, neutral):
    place = lax.axis_index(axis)
    gathered = jax.tree.map(
        lambda a, kind: lax.all_gather(a.astype(kind), axis), value, (jnp.bfloat16, jnp.bfloat16)
    )
    state = jax.tree.map(lambda a, e: jnp.zeros_like(a) + jnp.asarray(e, a.dtype), value, neutral)

    def one(turn, state):
        return join(
            state,
            jax.tree.map(
                lambda a, own: lax.dynamic_index_in_dim(a, turn, 0, False).astype(own.dtype),
                gathered,
                value,
            ),
        )

    return lax.fori_loop(0, place, one, state)


def prefix(value, axis, combine, identity):
    count, mine = (lax.axis_size(axis), lax.axis_index(axis))
    everything = jax.tree.map(
        lambda part, kind: lax.all_gather(part.astype(kind), axis),
        value,
        jax.tree.map(lambda a: jnp.bfloat16 if a.dtype == jnp.float32 else a.dtype, value),
    )
    start = jax.tree.map(
        lambda part, zero: jnp.broadcast_to(jnp.asarray(zero, part.dtype), part.shape),
        value,
        identity,
    )

    def turn(k, before):
        at = count - 1 - k
        reached = at > mine
        new = combine(
            before, jax.tree.map(lambda part, own: part[at].astype(own.dtype), everything, value)
        )
        return jax.tree.map(lambda a, b: jnp.where(reached, a, b), new, before)

    return lax.fori_loop(0, count, turn, start)


def user_index(positions, user_ends):
    return jnp.sum(
        (positions[:, None] >= user_ends[None, :]).astype(jnp.int32), axis=1, dtype=jnp.int32
    )


def user_layout(lengths_row, positions):
    user_ends = jnp.cumsum(lengths_row, dtype=jnp.int32)
    user_starts = user_ends - lengths_row
    user_ids = user_index(positions, user_ends)
    picked = (
        user_ids[:, None] == jnp.arange(lengths_row.shape[0], dtype=jnp.int32)[None, :]
    ).astype(jnp.int32)
    first_pos = jnp.sum(picked * user_starts[None, :], axis=1, dtype=jnp.int32)
    return (user_ends, user_ids, positions - first_pos + 1)


def feature_map(angles, freq_count):
    return (
        jnp.concatenate([jnp.cos(angles), jnp.sin(angles)], axis=-1) / math.sqrt(freq_count)
    ).astype(jnp.bfloat16)


def feature_grad(angles, grad_phi, frequencies):
    freq_count = frequencies.shape[2]
    grad_angles = (
        jnp.cos(angles) * grad_phi[..., freq_count:] - jnp.sin(angles) * grad_phi[..., :freq_count]
    ) / math.sqrt(freq_count)
    return jnp.einsum("thf,hdf->thd", grad_angles, frequencies, precision=HIGHEST_PRECISION)


def silu_slope(scores):
    sigma = jax.nn.sigmoid(scores)
    return sigma * (1.0 + scores * (1.0 - sigma))


def chain_combine(earlier, later):
    return (jnp.maximum(earlier[0], later[0]), later[1] + (1.0 - later[0]) * earlier[1])


def local(
    queries, history_keys, history_values, gate_inputs, frequencies, out_weight, lengths, cotangent
):
    rows = queries.shape[1]
    width = queries.shape[2]
    heads = frequencies.shape[0]
    head_dim = frequencies.shape[1]
    freq_count = frequencies.shape[2]
    blk_count = lax.axis_size("blk")
    seq_len = rows * blk_count
    score_scale = 1.0 / math.sqrt(head_dim)
    my_index = lax.axis_index("blk")
    positions = my_index * rows + jnp.arange(rows, dtype=jnp.int32)
    user_ends, user_ids, counts = user_layout(lengths[0], positions)
    count_float = counts.astype(jnp.float32)
    query_heads = queries[0].reshape(rows, heads, head_dim)
    key_local = history_keys[0].reshape(rows, heads, head_dim)
    value_local = history_values[0].reshape(rows, heads, head_dim)

    def tile_allowed(key_pos, key_users):
        return (
            (key_pos[None, :] <= positions[:, None]) & (key_users[None, :] == user_ids[:, None])
        ).astype(jnp.float32)

    zero_total = jnp.zeros((rows, heads, head_dim), jnp.float32)
    total = zero_total
    key_piece = lax.all_gather(history_keys, "blk", axis=1, tiled=True)
    value_piece = lax.all_gather(history_values, "blk", axis=1, tiled=True)
    piece_rows = key_piece.shape[1]
    fold_block_rows = math.gcd(piece_rows, 512)
    steps_count = piece_rows // fold_block_rows
    key_split = key_piece.reshape(steps_count, fold_block_rows, heads, head_dim)
    value_split = value_piece.reshape(steps_count, fold_block_rows, heads, head_dim)

    def advance(carried, inputs):
        key_blk, value_blk, block_index = inputs
        key_pos = block_index * fold_block_rows + jnp.arange(fold_block_rows, dtype=jnp.int32)
        key_users = user_index(key_pos, user_ends)
        scores = (
            jnp.einsum("thd,shd->hts", query_heads, key_blk, preferred_element_type=jnp.float32)
            * score_scale
        )
        weights = (jax.nn.silu(scores) * tile_allowed(key_pos, key_users)).astype(jnp.bfloat16)
        updated = carried + jnp.einsum(
            "hts,shd->thd", weights, value_blk, preferred_element_type=jnp.float32
        )
        return (updated, None)

    total, _ = lax.scan(
        advance, total, (key_split, value_split, jnp.arange(steps_count, dtype=jnp.int32))
    )
    value_float = value_local.astype(jnp.float32)
    query_angles = jnp.einsum(
        "thd,hdf->thf", query_heads.astype(jnp.float32), frequencies, precision=HIGHEST_PRECISION
    )
    key_angles = jnp.einsum(
        "thd,hdf->thf", key_local.astype(jnp.float32), frequencies, precision=HIGHEST_PRECISION
    )
    query_phi = feature_map(query_angles, freq_count)
    key_phi = feature_map(key_angles, freq_count)
    query_phi_float = query_phi.astype(jnp.float32)
    key_phi_float = key_phi.astype(jnp.float32)
    local_allowed = tile_allowed(positions, user_ids)
    kernel = (
        jnp.einsum("thf,shf->hts", query_phi, key_phi, preferred_element_type=jnp.float32)
        * local_allowed
    )
    recalled = jnp.einsum("hts,shd->thd", kernel, value_float, precision=HIGHEST_PRECISION)
    before_start = ((user_ids == user_ids[0]) & (counts[0] > 1)).astype(jnp.float32)
    after_last = (user_ids == user_ids[-1]).astype(jnp.float32)
    has_start = ((user_ids[0] != user_ids[-1]) | (counts[0] == 1)).astype(jnp.float32)
    state_sum = jnp.einsum(
        "shf,shd->hfd",
        key_phi * after_last[:, None, None].astype(jnp.bfloat16),
        value_local,
        preferred_element_type=jnp.float32,
    )
    identity = (jnp.zeros((), jnp.float32), jnp.zeros_like(state_sum))
    history = entering((has_start, state_sum), "blk", chain_combine, identity)[1]
    recalled = recalled + before_start[:, None, None] * jnp.einsum(
        "thf,hfd->thd", query_phi_float, history, precision=HIGHEST_PRECISION
    )
    gate_float = gate_inputs[0].astype(jnp.float32)
    gate = jax.nn.sigmoid(jnp.sum(gate_float.reshape(rows, heads, head_dim), axis=-1) * score_scale)
    mixed = ((total + gate[..., None] * recalled) / count_float[:, None, None]).reshape(rows, width)
    centered = mixed - jnp.mean(mixed, axis=1, keepdims=True)
    rstd = lax.rsqrt(jnp.mean(centered * centered, axis=1, keepdims=True) + EPS)
    normed = centered * rstd
    hidden = (normed * gate_float).astype(jnp.bfloat16)
    layer_out = jnp.dot(hidden, out_weight, preferred_element_type=jnp.float32).astype(jnp.bfloat16)
    cot_rows = cotangent[0]
    grad_hidden = jnp.dot(cot_rows, out_weight.T, preferred_element_type=jnp.float32)
    share = width // blk_count
    full_term = jnp.dot(hidden.T, cot_rows, preferred_element_type=jnp.float32)
    total_weight = lax.psum(full_term, ("dp", "blk"))
    grad_weight = lax.dynamic_slice_in_dim(total_weight, my_index * share, share, 0)
    grad_normed = grad_hidden * gate_float
    grad_mixed = rstd * (
        grad_normed
        - jnp.mean(grad_normed, axis=1, keepdims=True)
        - normed * jnp.mean(grad_normed * normed, axis=1, keepdims=True)
    )
    scaled = (grad_mixed / count_float[:, None]).reshape(rows, heads, head_dim)
    scaled_b = scaled.astype(jnp.bfloat16)
    gate_term = jnp.sum(scaled * recalled, axis=-1) * gate * (1.0 - gate) * score_scale
    grad_gates = grad_hidden * normed + jnp.broadcast_to(
        gate_term[..., None], (rows, heads, head_dim)
    ).reshape(rows, width)
    all_keys, all_values = (
        lax.all_gather(history_keys, "blk", axis=1, tiled=True),
        lax.all_gather(history_values, "blk", axis=1, tiled=True),
    )
    block_rows = math.gcd(seq_len, 512)
    steps_count = seq_len // block_rows
    key_split = all_keys.reshape(steps_count, block_rows, heads, head_dim)
    value_split = all_values.reshape(steps_count, block_rows, heads, head_dim)

    def backward_step(grad_q, inputs):
        key_blk, value_blk, block_index = inputs
        key_pos = block_index * block_rows + jnp.arange(block_rows, dtype=jnp.int32)
        key_users = user_index(key_pos, user_ends)
        allowed = tile_allowed(key_pos, key_users)
        scores = (
            jnp.einsum("thd,shd->hts", query_heads, key_blk, preferred_element_type=jnp.float32)
            * score_scale
        )
        weights = (jax.nn.silu(scores) * allowed).astype(jnp.bfloat16)
        grad_v = jnp.einsum("hts,thd->shd", weights, scaled_b, preferred_element_type=jnp.float32)
        grad_w = jnp.einsum("thd,shd->hts", scaled_b, value_blk, preferred_element_type=jnp.float32)
        grad_scores = (grad_w * silu_slope(scores) * allowed * score_scale).astype(jnp.bfloat16)
        grad_q_new = grad_q + jnp.einsum(
            "hts,shd->thd", grad_scores, key_blk, preferred_element_type=jnp.float32
        )
        grad_k = jnp.einsum(
            "hts,thd->shd", grad_scores, query_heads, preferred_element_type=jnp.float32
        )
        return (grad_q_new, (grad_k.astype(jnp.bfloat16), grad_v.astype(jnp.bfloat16)))

    grad_q_attn, key_terms = lax.scan(
        backward_step,
        zero_total,
        (key_split, value_split, jnp.arange(steps_count, dtype=jnp.int32)),
    )
    key_term = key_terms[0].reshape(seq_len, width)
    value_term = key_terms[1].reshape(seq_len, width)
    key_attn, value_attn = (
        lax.psum_scatter(
            key_term.astype(jnp.float32)[None].astype(jnp.bfloat16),
            "blk",
            scatter_dimension=1,
            tiled=True,
        ).astype(jnp.float32),
        lax.psum_scatter(
            value_term.astype(jnp.float32)[None].astype(jnp.bfloat16),
            "blk",
            scatter_dimension=1,
            tiled=True,
        ).astype(jnp.float32),
    )
    grad_recall = gate[..., None] * scaled
    grad_kernel = (
        jnp.einsum("thd,shd->hts", grad_recall, value_float, precision=HIGHEST_PRECISION)
        * local_allowed
    )
    value_recall = jnp.einsum("hts,thd->shd", kernel, grad_recall, precision=HIGHEST_PRECISION)
    grad_qphi = jnp.einsum("hts,shf->thf", grad_kernel, key_phi_float, precision=HIGHEST_PRECISION)
    grad_qphi = grad_qphi + before_start[:, None, None] * jnp.einsum(
        "thd,hfd->thf", grad_recall, history, precision=HIGHEST_PRECISION
    )
    grad_kphi = jnp.einsum(
        "hts,thf->shf", grad_kernel, query_phi_float, precision=HIGHEST_PRECISION
    )
    head_sum = jnp.einsum(
        "thf,thd->hfd",
        query_phi_float * before_start[:, None, None],
        grad_recall,
        precision=HIGHEST_PRECISION,
    )
    later = prefix((has_start, head_sum), "blk", chain_combine, identity)[1]
    grad_kphi = grad_kphi + after_last[:, None, None] * jnp.einsum(
        "shd,hfd->shf", value_float, later, precision=HIGHEST_PRECISION
    )
    value_recall = value_recall + after_last[:, None, None] * jnp.einsum(
        "shf,hfd->shd", key_phi_float, later, precision=HIGHEST_PRECISION
    )
    grad_queries = (
        (grad_q_attn + feature_grad(query_angles, grad_qphi, frequencies))
        .reshape(1, rows, width)
        .astype(jnp.bfloat16)
    )
    grad_keys = (
        key_attn + feature_grad(key_angles, grad_kphi, frequencies).reshape(1, rows, width)
    ).astype(jnp.bfloat16)
    grad_values = (value_attn + value_recall.reshape(1, rows, width)).astype(jnp.bfloat16)
    return (
        layer_out[None],
        grad_queries,
        grad_keys,
        grad_values,
        grad_gates.astype(jnp.bfloat16)[None],
        grad_weight,
    )


def solution(mesh):
    in_specs = (
        P("dp", "blk", None),
        P("dp", "blk", None),
        P("dp", "blk", None),
        P("dp", "blk", None),
        P(),
        P(),
        P("dp", None),
        P("dp", "blk", None),
    )
    out_specs = (
        P("dp", "blk", None),
        P("dp", "blk", None),
        P("dp", "blk", None),
        P("dp", "blk", None),
        P("dp", "blk", None),
        P("blk", None),
    )
    return jax.shard_map(local, mesh=mesh, in_specs=in_specs, out_specs=out_specs, check_vma=False)
```

profile of v0, /device:TPU:1, one launch (start us, length us, event | category | flops | bytes accessed | tf_op | source)
XLA Modules:
  0.0 702.3 jit_solution(12926516851324086820)
XLA Ops:
  23.0 35.9 %all-reduce = bf16[16]{0:T(256)(128)(2,1)S(1)} all-reduce(bf16[16]{0:T(256)(128)(2,1)S(1)} %dynamic-update-slice), channel_id=1, replica_groups=mesh['dp'=16,'blk'=16] {'blk'}, use_global_device_ids=true, to_apply=%add | all-reduce | flops 16 | bytes 64
  61.2 7.3 %all-gather.9.cloned.1.call-done = bf16[1,2048,512]{2,1,0:T(8,128)(2,1)} async-done(((bf16[1,128,512]{2,1,0:T(8,128)(2,1)}), bf16[1,2048,512]{2,1,0:T(8,128)(2,1)}) %all-gather.9.cloned.1.call-update) | async-done | bytes 2097168 | tf_op jit(solution)/shard_map/all_gather | solution.py:122
  68.5 2.5 reshape.369
  72.8 50.9 %all-gather.7.cloned.1.call-done = bf16[1,2048,512]{2,1,0:T(8,128)(2,1)} async-done(((bf16[1,128,512]{2,1,0:T(8,128)(2,1)}), bf16[1,2048,512]{2,1,0:T(8,128)(2,1)}) %all-gather.7.cloned.1.call-update) | async-done | bytes 2097168 | tf_op jit(solution)/shard_map/all_gather | solution.py:123
  123.7 4.0 reshape.368
  127.7 19.5 %while.55 = (s32[]{:T(128)}, f32[128,4,128]{0,2,1:T(8,128)S(1)}, bf16[4,512,4,128]{3,2,1,0:T(4,128)(2,1)}, bf16[4,512,4,128]{3,1,2,0:T(8,128)(2,1)}, bf16[128,4,...) while((s32[]{:T(128)}, f32[128,4,128]{0,2,1:T(8,128)S(1)}, ...), condition=%wide.region_4.5_spmd.clone, body=%wide.region_2.4_spmd.clone.sunk | while | flops 136458368 | bytes 4337359 | solution.py:144
  147.2 32.1 %all-gather.11.cloned.1.call-done = bf16[64,128,128]{2,1,0:T(8,128)(2,1)} async-done(((bf16[4,128,128]{2,1,0:T(8,128)(2,1)}), bf16[64,128,128]{2,1,0:T(8,128)(2,1)}) %all-gather.11.cloned.1.call-update) | async-done | bytes 2097168 | tf_op jit(solution)/shard_map/all_gather | solution.py:15
  179.4 2.3 while.54
  183.9 1.8 fusion.47
  185.8 1.8 fusion.79
  188.3 1.8 multiply_divide_fusion
  190.1 1.8 copy.129
  195.2 2.3 convolution_convert_fusion.3
  198.1 31.3 %while.56 = (s32[]{:T(128)}, f32[128,4,128]{0,2,1:T(8,128)}, bf16[4,512,4,128]{3,2,1,0:T(4,128)(2,1)}, bf16[4,512,4,128]{3,2,1,0:T(4,128)(2,1)}, bf16[4,512,4,12...) while((s32[]{:T(128)}, f32[128,4,128]{0,2,1:T(8,128)}, ...), condition=%wide.region_15.16_spmd.clone, body=%wide.region_13.15_spmd.clone.sunk | while | flops 341192832 | bytes 14954307 | solution.py:234
  204.2 1.9 copy_dynamic-update-slice_fusion.3
  219.8 1.8 copy_dynamic-update-slice_fusion.3
  227.6 1.8 copy_dynamic-update-slice_fusion.3
  229.5 4.2 reshape.377
  238.5 4.2 reshape.375
  246.4 229.3 %all-reduce.3.cloned.1.call-done = f32[512,1024]{1,0:T(8,128)} async-done(((f32[512,1024]{1,0:T(8,128)}), f32[512,1024]{1,0:T(8,128)}) %all-reduce.3.cloned.1.call-update) | async-done | bytes 2097168 | tf_op jit(solution)/shard_map/psum | solution.py:190
  477.3 55.2 %all-gather.13.cloned.1.call-done = bf16[64,128,128]{2,1,0:T(8,128)(2,1)} async-done(((bf16[4,128,128]{2,1,0:T(8,128)(2,1)}), bf16[64,128,128]{2,1,0:T(8,128)(2,1)}) %all-gather.13.cloned.1.call-update) | async-done | bytes 2097168 | tf_op jit(solution)/shard_map/all_gather | solution.py:35
  532.5 37.4 %while.57 = (s32[]{:T(128)}, f32[4,128,128]{2,1,0:T(8,128)S(1)}, s32[]{:T(128)}, bf16[16,4,128,128]{3,2,1,0:T(8,128)(2,1)}, bf16[16]{0:T(256)(128)(2,1)S(1)}, /*...) while((s32[]{:T(128)}, f32[4,128,128]{2,1,0:T(8,128)S(1)}, s32[]{:T(128)}, ...), condition=%wide.region_18.19_spmd.clone, body=%wide.region_17.18_spmd.clone.sunk | while | flops 327689 | bytes 655561 | solution.py:53
  572.0 39.8 %reduce-scatter.5.cloned.1.call-done = bf16[1,128,512]{2,1,0:T(8,128)(2,1)} async-done(((bf16[1,2048,512]{2,1,0:T(8,128)(2,1)}), bf16[1,128,512]{2,1,0:T(8,128)(2,1)}) %reduce-scatter.5.cloned.1.call-update) | async-done | bytes 131088 | tf_op jit(solution)/shard_map/reduce_scatter | solution.py:248
  613.4 80.4 %reduce-scatter.3.cloned.1.call-done = bf16[1,128,512]{2,1,0:T(8,128)(2,1)} async-done(((bf16[1,2048,512]{2,1,0:T(8,128)(2,1)}), bf16[1,128,512]{2,1,0:T(8,128)(2,1)}) %reduce-scatter.3.cloned.1.call-update) | async-done | bytes 131088 | tf_op jit(solution)/shard_map/reduce_scatter | solution.py:242
  (298 shorter events, 107.7 us)
Async XLA Ops:
  7.2 178.6 %copy-start = (bf16[512,1024]{1,0:T(8,128)(2,1)S(1)}, bf16[512,1024]{1,0:T(8,128)(2,1)}, u32[]{:S(2)}) copy-start(bf16[512,1024]{1,0:T(8,128)(2,1)} %param.21) | copy-start | bytes 3145732
  7.2 61.3 %all-gather.9.cloned.1.call-start = ((), (), s32[]{:S(2)}) async-start(), calls=%async_computation.3 | async-start | bytes 2228224 | tf_op jit(solution)/shard_map/all_gather | solution.py:122
  7.9 13.8 %copy-start.41 = (u32[256]{0:T(256)S(1)}, u32[256]{0:T(256)}, u32[]{:S(2)}) copy-start(u32[256]{0:T(256)} %constant.162) | copy-start | bytes 3076
  7.9 51.0 %copy-start.19 = (bf16[1,128,512]{2,1,0:T(8,128)(2,1)S(1)}, bf16[1,128,512]{2,1,0:T(8,128)(2,1)}, u32[]{:S(2)}) copy-start(bf16[1,128,512]{2,1,0:T(8,128)(2,1)} %param.19) | copy-start | bytes 393220
  7.9 115.7 %all-gather.7.cloned.1.call-start = ((), (), s32[]{:S(2)}) async-start(), calls=%async_computation.2 | async-start | bytes 2228224 | tf_op jit(solution)/shard_map/all_gather | solution.py:123
  8.7 170.7 %all-gather.11.cloned.1.call-start = ((), (), s32[]{:S(2)}) async-start(), calls=%async_computation.7 | async-start | bytes 2228224 | tf_op jit(solution)/shard_map/all_gather | solution.py:15
  9.7 50.3 %copy-start.7 = (bf16[128,4,128]{2,1,0:T(4,128)(2,1)}, bf16[128,4,128]{2,1,0:T(4,128)(2,1)S(1)}, u32[]{:S(2)}) copy-start(bf16[128,4,128]{2,1,0:T(4,128)(2,1)S(1)} %reshape_squeeze.11) | copy-start | bytes 393220
  13.4 168.3 %copy-start.40 = (f32[128]{0:T(128)}, f32[128]{0:T(128)S(1)}, u32[]{:S(2)}) copy-start(f32[128]{0:T(128)S(1)} %get-tuple-element.566) | copy-start | bytes 1540
  15.2 7.9 %copy-start.24 = (f32[4,64,128]{2,1,0:T(8,128)}, f32[4,64,128]{2,1,0:T(8,128)S(1)}, u32[]{:S(2)}) copy-start(f32[4,64,128]{2,1,0:T(8,128)S(1)} %fusion.94) | copy-start | bytes 393220
  17.5 43.7 %copy-start.9 = (bf16[128,4,128]{0,2,1:T(8,128)(2,1)}, bf16[128,4,128]{0,2,1:T(8,128)(2,1)S(1)}, u32[]{:S(2)}) copy-start(bf16[128,4,128]{0,2,1:T(8,128)(2,1)S(1)} %get-tuple-element.582) | copy-start | bytes 393220
  17.5 164.2 %copy-start.11 = (bf16[128,4,128]{0,2,1:T(8,128)(2,1)}, bf16[128,4,128]{0,2,1:T(8,128)(2,1)S(1)}, u32[]{:S(2)}) copy-start(bf16[128,4,128]{0,2,1:T(8,128)(2,1)S(1)} %get-tuple-element.581) | copy-start | bytes 393220
  19.3 162.5 %copy-start.37 = (f32[128]{0:T(128)}, f32[128]{0:T(128)S(1)}, u32[]{:S(2)}) copy-start(f32[128]{0:T(128)S(1)} %get-tuple-element.576) | copy-start | bytes 1540
  20.1 455.6 %all-reduce.3.cloned.1.call-start = ((), (), s32[]{:S(2)}) async-start(), calls=%async_computation.6 | async-start | bytes 4194304 | tf_op jit(solution)/shard_map/psum | solution.py:190
  21.6 39.6 %copy-start.29 = (f32[128,128]{1,0:T(8,128)}, f32[128,128]{1,0:T(8,128)S(1)}, u32[]{:S(2)}) copy-start(f32[128,128]{1,0:T(8,128)S(1)} %and_convert_fusion.2) | copy-start | bytes 196612
  72.8 54.9 %copy-start.31 = (f32[128,4,128]{0,2,1:T(8,128)S(1)}, f32[128,4,128]{0,2,1:T(8,128)}, u32[]{:S(2)}) copy-start(f32[128,4,128]{0,2,1:T(8,128)} %custom-call) | copy-start | bytes 786436
  147.2 34.5 %copy-start.28 = (f32[128,4,128]{0,2,1:T(8,128)S(1)}, f32[128,4,128]{0,2,1:T(8,128)}, u32[]{:S(2)}) copy-start(f32[128,4,128]{0,2,1:T(8,128)} %convolution_bitcast_fusion.3) | copy-start | bytes 786436
  185.7 12.4 %copy-start.1 = (bf16[4,512,4,128]{3,1,2,0:T(8,128)(2,1)S(1)}, bf16[4,512,4,128]{3,1,2,0:T(8,128)(2,1)}, u32[]{:S(2)}) copy-start(bf16[4,512,4,128]{3,1,2,0:T(8,128)(2,1)} %get-tuple-element.923) | copy-start | bytes 6291460
  185.7 346.8 %all-gather.13.cloned.1.call-start = ((), (), s32[]{:S(2)}) async-start(), calls=%async_computation.8 | async-start | bytes 2228224 | tf_op jit(solution)/shard_map/all_gather | solution.py:35
  197.6 414.3 %reduce-scatter.5.cloned.1.call-start = ((), (), s32[]{:S(2)}) async-start(), calls=%async_computation.5 | async-start | bytes 2228224 | tf_op jit(solution)/shard_map/reduce_scatter | solution.py:248
  233.7 460.1 %reduce-scatter.3.cloned.1.call-start = ((), (), s32[]{:S(2)}) async-start(), calls=%async_computation.4 | async-start | bytes 2228224 | tf_op jit(solution)/shard_map/reduce_scatter | solution.py:242
  238.5 5.4 copy-start.12
  244.1 288.4 %copy-start.43 = (bf16[16]{0:T(256)(128)(2,1)S(1)}, bf16[16]{0:T(256)(128)(2,1)}, u32[]{:S(2)}) copy-start(bf16[16]{0:T(256)(128)(2,1)} %copy-done.42) | copy-start | bytes 100
  246.4 323.6 %copy-start.39 = (f32[128]{0:T(128)S(1)}, f32[128]{0:T(128)}, u32[]{:S(2)}) copy-start(f32[128]{0:T(128)} %get-tuple-element.569) | copy-start | bytes 1540
  532.5 38.4 %copy-start.23 = (f32[4,64,128]{2,1,0:T(8,128)S(1)}, f32[4,64,128]{2,1,0:T(8,128)}, u32[]{:S(2)}) copy-start(f32[4,64,128]{2,1,0:T(8,128)} %copy-done.22) | copy-start | bytes 393220
  (36 other events, 83.0 us)
Sparse Core Ops, SparseCore 0:
  10.7 57.7 all-gather.8
  71.2 52.3 all-gather.6
  127.0 52.3 all-gather.10
  185.8 289.8 all-reduce.2
  478.3 54.1 all-gather.12
  536.6 75.1 reduce-scatter.4
  616.1 77.7 reduce-scatter.2
where the time goes:
time: 705 us; the launch traced here: 702 us
  waiting for transfers between devices  497 us (70%)
  local copies, waits for them, and re-layouts  72 us (10%)
  blocking collectives  35.9 us (5%)
  matrix products  32.1 us (5%)
  other arithmetic  31.7 us (4%)
  loops' own time  17.3 us (2%)
  between operations  16.1 us (2%)
    psum x1, waiting for transfers between devices, local(): total_weight = lax.psum(full_term, ('dp', 'blk'))  229 us
    reduce_scatter x1, waiting for transfers between devices, local(): lax.psum_scatter(key_term.astype(jnp.float32)[None].astype(jnp.bfloat16),...  80.4 us
    all_gather x1, waiting for transfers between devices, prefix(): lax.all_gather(part.astype(kind), axis)  55.2 us
    all_gather x1, waiting for transfers between devices, local(): value_piece = lax.all_gather(history_values, 'blk', axis=1, tiled=True)  50.9 us
    reduce_scatter x1, waiting for transfers between devices, local(): lax.psum_scatter(value_term.astype(jnp.float32)[None].astype(jnp.bfloat16...  39.8 us
    unnamed x1, blocking collectives  35.9 us
    all_gather x1, waiting for transfers between devices, entering(): lax.all_gather(a.astype(kind), axis)  32.1 us
    dynamic_slice x20, local copies, waits for them, and re-layouts, local(): lax.scan(advance, total, (key_split, value_split, jnp.arange(steps_count,...  18.6 us
  transfers between devices with their start and end apart: 7, of which 7 were waited for; matrix products, arithmetic and copies ran while one was open for 18% of the time, Pallas kernels for 0%

commit v1 on v0

v1 whole, which is shorter than its diff:
```python
import functools
import math

import jax
import jax.numpy as jnp
from jax import lax
from jax.experimental import pallas as pl
from jax.experimental.pallas import tpu as pltpu
from jax.sharding import PartitionSpec as P

EPS = 1e-05
HEADS, HEAD, FREQS, USERS = 4, 128, 64, 8
TOK, NBLK, GROUPS = 128, 16, 4
SUB = TOK // GROUPS
WIDTH, D = HEADS * HEAD, 1024
SEQ = TOK * NBLK
QROWS = SUB * NBLK
TILE = 2 * TOK
STEP = 2 * SUB
REACH = 5
TILES = SEQ // TILE
SCALE = 1.0 / math.sqrt(HEAD)
F32, BF16 = jnp.float32, jnp.bfloat16

Q0, G0, K0, V0, PACK = 0, SUB, 2 * SUB, 2 * SUB + TOK, 2 * SUB + 2 * TOK
WROWS = (WIDTH // NBLK) * D // HEAD

NT = (((1,), (1,)), ((), ()))
NN = (((1,), (0,)), ((), ()))
TN = (((0,), (0,)), ((), ()))


def mm(a, b, dims):
    return lax.dot_general(a, b, dims, preferred_element_type=F32)


def lanes(shape):
    return lax.broadcasted_iota(jnp.int32, shape, 1)


def starts_of(lens_ref, pos):
    end = jnp.int32(0)
    start = jnp.zeros_like(pos)
    for u in range(USERS):
        end = end + lens_ref[u]
        start = jnp.where(pos >= end, end, start)
    return start


def cos_sin(angles):
    turns = jnp.floor(angles * (2.0 / math.pi) + 0.5)
    r = angles - turns * 1.5703125
    r = r - turns * 4.837512969970703125e-4
    r = r - turns * 7.54978995489188e-8
    quad = turns.astype(jnp.int32) - jnp.where(lanes(angles.shape) >= FREQS, 1, 0)
    z = r * r
    c = 1.0 - 0.5 * z + z * z * (4.166664568e-2 + z * (-1.388731625e-3 + z * 2.443315712e-5))
    s = r + r * z * (-1.6666654611e-1 + z * (8.3321608736e-3 - z * 1.9515295891e-4))
    odd = (quad & 1) == 1
    value = jnp.where(odd, s, c)
    return jnp.where(((quad + 1) & 2) == 2, -value, value)


def pack_kernel(q_ref, k_ref, v_ref, u_ref, out_ref):
    for h in range(HEADS):
        cols = slice(h * HEAD, (h + 1) * HEAD)
        total = jnp.sum(u_ref[:, cols].astype(F32), axis=1, keepdims=True)
        gate = jnp.broadcast_to(jax.nn.sigmoid(total * SCALE), (TOK, HEAD))
        high = gate.astype(BF16).astype(F32)
        gate = jnp.where(lanes((TOK, HEAD)) < FREQS, high, gate - high).astype(BF16)
        keys, values = k_ref[:, cols], v_ref[:, cols]
        for g in range(GROUPS):
            rows = slice(g * SUB, (g + 1) * SUB)
            out_ref[h * GROUPS + g, Q0:G0, :] = q_ref[rows, cols]
            out_ref[h * GROUPS + g, G0:K0, :] = gate[rows]
            out_ref[h * GROUPS + g, K0:V0, :] = keys
            out_ref[h * GROUPS + g, V0:PACK, :] = values


def stage_rows(recv_ref, lens_ref, group, q_s, gate_s, start_s, pos_s):
    for b in range(NBLK):
        rows = slice(b * SUB, (b + 1) * SUB)
        q_s[rows, :] = recv_ref[b, Q0:G0, :]
        parts = recv_ref[b, G0:K0, :].astype(F32)
        gate_s[rows, :] = jnp.broadcast_to(
            parts[:, 0:1] + parts[:, FREQS : FREQS + 1], (SUB, HEAD)
        )
    row = lax.broadcasted_iota(jnp.int32, (QROWS, HEAD), 0)
    pos = (row >> 5) * TOK + group * SUB + (row & (SUB - 1))
    pos_s[...] = pos
    start_s[...] = starts_of(lens_ref, pos)


def tile_of(recv_ref, c, first, last):
    return jnp.concatenate(
        [recv_ref[2 * c, first:last, :], recv_ref[2 * c + 1, first:last, :]], axis=0
    )


def twice(a):
    return jnp.concatenate([a, a], axis=1)


def allowed_of(start_s, pos_s, rows, c):
    key = c * TILE + lanes((rows.stop - rows.start, TILE))
    return (key >= twice(start_s[rows, :])) & (key <= twice(pos_s[rows, :]))


def forward_kernel(
    lens_ref, idx_ref, recv_ref, freq_ref, mixed_ref, phiq_ref, phik_ref,
    q_s, gate_s, start_s, pos_s, acc_s,
):
    head, group = idx_ref[0] // GROUPS, idx_ref[0] % GROUPS
    stage_rows(recv_ref, lens_ref, group, q_s, gate_s, start_s, pos_s)
    freq = freq_ref[head]
    freq = jnp.concatenate([freq, freq], axis=1)
    pieces = []
    for _ in range(3):
        piece = freq.astype(BF16)
        pieces.append(piece)
        freq = freq - piece.astype(F32)
    pieces = jnp.concatenate(pieces, axis=1)

    def phi_of(x):
        a = mm(x, pieces, NN)
        angles = (a[:, 2 * HEAD :] + a[:, HEAD : 2 * HEAD]) + a[:, :HEAD]
        return (cos_sin(angles) / math.sqrt(FREQS)).astype(BF16)

    for i in range(QROWS // TILE):
        rows = slice(i * TILE, (i + 1) * TILE)
        phiq_ref[rows, :] = phi_of(q_s[rows, :])
    acc_s[...] = jnp.zeros_like(acc_s)
    for c in range(TILES):
        rows = slice(c * STEP, min(c + REACH, TILES) * STEP)
        keys = tile_of(recv_ref, c, K0, V0)
        values = tile_of(recv_ref, c, V0, PACK)
        phik = phi_of(keys)
        phik_ref[c * TILE : (c + 1) * TILE, :] = phik
        half = mm(q_s[rows, :], keys, NT) * (0.5 * SCALE)
        weights = half + half * jnp.tanh(half)
        kern = mm(phiq_ref[rows, :], phik, NT)
        both = weights + twice(gate_s[rows, :]) * kern
        both = jnp.where(allowed_of(start_s, pos_s, rows, c), both, 0.0).astype(BF16)
        acc_s[rows, :] += mm(both, values, NN)
    for b in range(NBLK):
        rows = slice(b * SUB, (b + 1) * SUB)
        count = (pos_s[rows, :] - start_s[rows, :] + 1).astype(F32)
        mixed_ref[b] = acc_s[rows, :] / count


def middle_kernel(
    lens_ref, idx_ref, mixed_ref, u_ref, w_ref, cot_ref, out_ref, send_ref, ghn_ref, hid_s
):
    pos = idx_ref[0] * TOK + lax.broadcasted_iota(jnp.int32, (TOK, HEAD), 0)
    count = (pos - starts_of(lens_ref, pos) + 1).astype(F32)
    count = jnp.concatenate([count] * HEADS, axis=1)
    mixed = jnp.concatenate(
        [
            jnp.concatenate([mixed_ref[h * GROUPS + g] for g in range(GROUPS)], axis=0)
            for h in range(HEADS)
        ],
        axis=1,
    )
    gates = u_ref[...].astype(F32)
    centered = mixed - jnp.mean(mixed, axis=1, keepdims=True)
    rstd = lax.rsqrt(jnp.mean(centered * centered, axis=1, keepdims=True) + EPS)
    normed = centered * rstd
    hidden = (normed * gates).astype(BF16)
    hid_s[...] = hidden
    out_ref[...] = mm(hidden, w_ref[...], NN).astype(BF16)
    grad_hidden = mm(cot_ref[...], w_ref[...], NT)
    ghn_ref[...] = grad_hidden * normed
    grad_normed = grad_hidden * gates
    grad_mixed = rstd * (
        grad_normed
        - jnp.mean(grad_normed, axis=1, keepdims=True)
        - normed * jnp.mean(grad_normed * normed, axis=1, keepdims=True)
    )
    scaled = (grad_mixed / count).astype(BF16)
    for h in range(HEADS):
        for g in range(GROUPS):
            send_ref[h * GROUPS + g, 0:SUB, :] = scaled[
                g * SUB : (g + 1) * SUB, h * HEAD : (h + 1) * HEAD
            ]
    for j in range(D // HEAD):
        part = mm(hid_s[...], cot_ref[:, j * HEAD : (j + 1) * HEAD], TN).astype(BF16)
        for d in range(NBLK):
            send_ref[d, SUB + j * 32 : SUB + (j + 1) * 32, :] = part[d * 32 : (d + 1) * 32]


def backward_kernel(
    lens_ref, idx_ref, recv_ref, phiq_ref, phik_ref, grads_ref, freq_ref, send_ref, gw_ref,
    q_s, gate_s, start_s, pos_s, sc_s, dq_s, dphi_s, term_s,
):
    head, group = idx_ref[0] // GROUPS, idx_ref[0] % GROUPS
    stage_rows(recv_ref, lens_ref, group, q_s, gate_s, start_s, pos_s)
    total = grads_ref[0, SUB:, :].astype(F32)
    for d in range(1, NBLK):
        total = total + grads_ref[d, SUB:, :].astype(F32)
    piece = WROWS // NBLK
    for d in range(NBLK):
        gw_ref[d] = total[d * piece : (d + 1) * piece].astype(BF16)
    for b in range(NBLK):
        sc_s[b * SUB : (b + 1) * SUB, :] = grads_ref[b, 0:SUB, :]
    freq = freq_ref[head].astype(BF16)
    freq = jnp.concatenate([freq, -freq], axis=1)
    dq_s[...] = jnp.zeros_like(dq_s)
    dphi_s[...] = jnp.zeros_like(dphi_s)
    term_s[...] = jnp.zeros_like(term_s)

    def back(phi, grad_phi):
        turned = pltpu.roll(grad_phi, FREQS, 1)
        return mm((phi.astype(F32) * turned).astype(BF16), freq, NT)

    for c in range(TILES):
        rows = slice(c * STEP, min(c + REACH, TILES) * STEP)
        keys = tile_of(recv_ref, c, K0, V0)
        values = tile_of(recv_ref, c, V0, PACK)
        phik = phik_ref[c * TILE : (c + 1) * TILE, :]
        q, phiq, scaled = q_s[rows, :], phiq_ref[rows, :], sc_s[rows, :]
        gate = twice(gate_s[rows, :])
        allowed = allowed_of(start_s, pos_s, rows, c)
        half = mm(q, keys, NT) * (0.5 * SCALE)
        t = jnp.tanh(half)
        weights = half + half * t
        slope = (1.0 + t) + weights * (1.0 - t)
        kern = mm(phiq, phik, NT)
        grad_w = jnp.where(allowed, mm(scaled, values, NT), 0.0)
        both = jnp.where(allowed, weights + gate * kern, 0.0).astype(BF16)
        grad_s = (grad_w * slope * (0.5 * SCALE)).astype(BF16)
        grad_k = (grad_w * gate).astype(BF16)
        term = kern * grad_w
        term_s[rows, :] += term[:, :TOK] + term[:, TOK:]
        dq_s[rows, :] += mm(grad_s, keys, NN)
        dphi_s[rows, :] += mm(grad_k, phik, NN)
        dkey = mm(grad_s, q, TN) + back(phik, mm(grad_k, phiq, TN))
        dval = mm(both, scaled, TN)
        for i in range(2):
            send_ref[2 * c + i, K0:V0, :] = dkey[i * TOK : (i + 1) * TOK].astype(BF16)
            send_ref[2 * c + i, V0:PACK, :] = dval[i * TOK : (i + 1) * TOK].astype(BF16)
    dq = dq_s[...] + back(phiq_ref[...], dphi_s[...])
    gate = gate_s[...]
    term = jnp.sum(term_s[...], axis=1, keepdims=True) * gate * (1.0 - gate) * SCALE
    for b in range(NBLK):
        rows = slice(b * SUB, (b + 1) * SUB)
        send_ref[b, Q0:G0, :] = dq[rows].astype(BF16)
        send_ref[b, G0:K0, :] = term[rows].astype(BF16)


def final_kernel(recv_ref, ghn_ref, gw_ref, dq_ref, dk_ref, dv_ref, dg_ref, dw_ref):
    for h in range(HEADS):
        cols = slice(h * HEAD, (h + 1) * HEAD)
        keys = values = 0.0
        for g in range(GROUPS):
            rows = slice(g * SUB, (g + 1) * SUB)
            d = h * GROUPS + g
            dq_ref[rows, cols] = recv_ref[d, Q0:G0, :]
            dg_ref[rows, cols] = (ghn_ref[rows, cols] + recv_ref[d, G0:K0, :].astype(F32)).astype(
                BF16
            )
            keys = keys + recv_ref[d, K0:V0, :].astype(F32)
            values = values + recv_ref[d, V0:PACK, :].astype(F32)
        dk_ref[:, cols] = keys.astype(BF16)
        dv_ref[:, cols] = values.astype(BF16)
    share = WIDTH // NBLK
    for j in range(D // HEAD):
        for i in range(2):
            rows = gw_ref[2 * j + i].astype(F32)
            dw_ref[i * 16 : (i + 1) * 16, j * HEAD : (j + 1) * HEAD] = rows


VMEM = pl.BlockSpec(memory_space=pltpu.VMEM)
SMEM = pl.BlockSpec(memory_space=pltpu.SMEM)


def call(body, scalars, arrays, outs, scratch=()):
    return pl.pallas_call(
        body,
        in_specs=[SMEM] * len(scalars) + [VMEM] * len(arrays),
        out_specs=[VMEM] * len(outs),
        out_shape=[jax.ShapeDtypeStruct(s, t) for s, t in outs],
        scratch_shapes=[pltpu.VMEM(s, t) for s, t in scratch],
        compiler_params=pltpu.CompilerParams(vmem_limit_bytes=40 * 1024 * 1024),
    )(*scalars, *arrays)


def swap(a, axis):
    return lax.all_to_all(a, axis, 0, 0, tiled=True)


def local(q, k, v, u, freqs, w, lens, cot):
    q, k, v, u, cot, lens = q[0], k[0], v[0], u[0], cot[0], lens[0]
    idx = lax.axis_index("blk").astype(jnp.int32)[None]
    staged = [
        ((QROWS, HEAD), BF16),
        ((QROWS, HEAD), F32),
        ((QROWS, HEAD), jnp.int32),
        ((QROWS, HEAD), jnp.int32),
    ]
    (send1,) = call(pack_kernel, [], [q, k, v, u], [((NBLK, PACK, HEAD), BF16)])
    recv1 = swap(send1, "blk")
    mixed, phiq, phik = call(
        forward_kernel,
        [lens, idx],
        [recv1, freqs],
        [((NBLK, SUB, HEAD), F32), ((QROWS, HEAD), BF16), ((SEQ, HEAD), BF16)],
        staged + [((QROWS, HEAD), F32)],
    )
    recv2 = swap(mixed, "blk")
    layer_out, send3, ghn = call(
        middle_kernel,
        [lens, idx],
        [recv2, u, w, cot],
        [((TOK, D), BF16), ((NBLK, SUB + WROWS, HEAD), BF16), ((TOK, WIDTH), F32)],
        [((TOK, WIDTH), BF16)],
    )
    recv3 = swap(send3, "blk")
    send4, gw = call(
        backward_kernel,
        [lens, idx],
        [recv1, phiq, phik, recv3, freqs],
        [((NBLK, PACK, HEAD), BF16), ((NBLK, WROWS // NBLK, HEAD), BF16)],
        staged + [((QROWS, HEAD), BF16)] + [((QROWS, HEAD), F32)] * 3,
    )
    recv4 = swap(send4, "blk")
    parts = swap(gw, "dp")
    mine = jnp.sum(parts.astype(F32), axis=0).astype(BF16)
    whole = swap(jnp.broadcast_to(mine[None], gw.shape), "dp")
    dq, dk, dv, dg, dw = call(
        final_kernel,
        [],
        [recv4, ghn, whole],
        [((TOK, WIDTH), BF16)] * 4 + [((WIDTH // NBLK, D), F32)],
    )
    return layer_out[None], dq[None], dk[None], dv[None], dg[None], dw


def solution(mesh):
    rows = P("dp", "blk", None)
    return jax.shard_map(
        local,
        mesh=mesh,
        in_specs=(rows, rows, rows, rows, P(), P(), P("dp", None), rows),
        out_specs=(rows, rows, rows, rows, rows, P("blk", None)),
        check_vma=False,
    )
```

time: 705 us -> 134 us (0.19)
  waiting for transfers between devices: 497 us -> 20 us
  local copies, waits for them, and re-layouts: 72 us -> 3.77 us
  blocking collectives: 35.9 us -> 85.5 us
  matrix products: 32.1 us -> 0 us
  other arithmetic: 31.7 us -> 0.02 us
  loops' own time: 17.3 us -> 0 us
  between operations: 16.1 us -> 0.72 us
  Pallas kernels: 0 us -> 15 us
  starting transfers between devices: 0.46 us -> 8.58 us
    psum x1 -> x0, waiting for transfers between devices: 229 us -> none  [local(): total_weight = lax.psum(full_term, ('dp', 'blk'))]
    all_gather x4 -> x0, waiting for transfers between devices: 146 us -> none  [the longest x1 55.2 us: prefix(): lax.all_gather(part.astype(kind), axis)]
    reduce_scatter x2 -> x0, waiting for transfers between devices: 120 us -> none  [the longest x1 80.4 us: local(): lax.psum_scatter(key_term.astype(jnp.float32)[None].astype(jnp.bfloat16),...]
    all_to_all x0 -> x5, blocking collectives: none -> 85.5 us  [swap(): return lax.all_to_all(a, axis, 0, 0, tiled=True)]
    unnamed x1 -> x0, blocking collectives: 35.9 us -> none
    dot_general x43 -> x0, matrix products: 32.1 us -> none  [the longest x4 6.99 us: advance(): jnp.einsum('hts,shd->thd', weights, value_blk, preferred_element_type=jnp...]
    dynamic_slice x38 -> x0, local copies, waits for them, and re-layouts: 30.1 us -> none  [the longest x20 18.6 us: local(): lax.scan(advance, total, (key_split, value_split, jnp.arange(steps_count,...]
    all_to_all x0 -> x1, waiting for transfers between devices: none -> 20 us  [swap(): return lax.all_to_all(a, axis, 0, 0, tiled=True)]
  transfers between devices with their start and end apart: 7 -> 1, of which waited for: 7 -> 1; matrix products, arithmetic and copies ran while one was open for 18% -> 0% of each run, Pallas kernels for 0% -> 0%
where the time goes in v1:
time: 134 us
  blocking collectives  85.5 us (64%)
  waiting for transfers between devices  20 us (15%)
  Pallas kernels  15 us (11%)
  starting transfers between devices  8.58 us (6%)
  local copies, waits for them, and re-layouts  3.77 us (3%)
    all_to_all x5, blocking collectives, swap(): return lax.all_to_all(a, axis, 0, 0, tiled=True)  85.5 us
    all_to_all x1, waiting for transfers between devices, swap(): return lax.all_to_all(a, axis, 0, 0, tiled=True)  20 us
    pallas_call x5, Pallas kernels, call(): pl.pallas_call(body, in_specs=[SMEM] * len(scalars) + [VMEM] * len(arrays...  15 us
    all_to_all x1, starting transfers between devices, swap(): return lax.all_to_all(a, axis, 0, 0, tiled=True)  8.58 us
    unnamed x19, local copies, waits for them, and re-layouts  3.76 us
  transfers between devices with their start and end apart: 1, of which 1 were waited for; matrix products, arithmetic and copies ran while one was open for 0% of the time, Pallas kernels for 0%

profile of v1, /device:TPU:1, one launch (start us, length us, event | category | flops | bytes accessed | tf_op | source)
XLA Modules:
  0.0 133.6 jit_solution(10692129798706610852)
XLA Ops:
  0.6 0.0 copy-start.1
  0.6 0.9 copy-done.1
  1.5 0.9 copy-done.4
  2.4 0.9 copy-done.5
  3.4 0.9 copy-done.6
  4.3 1.3 shard_map.127
  5.6 8.6 %all-to-all-start = ((bf16[16,320,128]{2,1,0:T(8,128)(2,1)}), bf16[16,320,128]{2,1,0:T(8,128)(2,1)S(1)}, u32[]{:S(2)}, u32[]{:S(2)}) async-start(bf16[16,320,128]{2,1,0:T(8,128)(2,1)} %shard_map.127), calls=%async_computation | async-start | bytes 2621440 | tf_op jit(solution)/shard_map/all_to_all | solution.py:288
  14.2 0.0 copy-start.2
  14.2 0.0 copy-start.3
  14.2 0.0 copy-done.8
  14.2 0.1 copy.14.freq_ref
  14.3 20.0 %all-to-all-done.recv_ref = bf16[16,320,128]{2,1,0:T(8,128)(2,1)S(1)} async-done(((bf16[16,320,128]{2,1,0:T(8,128)(2,1)}), bf16[16,320,128]{2,1,0:T(8,128)(2,1)S(1)}, u32[]{:S(2)}, u32[]{:S(2)}) %all-to-all-start) | async-done | bytes 1310752 | tf_op jit(solution)/shard_map/all_to_all | solution.py:288
  34.3 0.0 copy-done.7
  34.3 4.8 %shard_map.128 = (f32[16,32,128]{2,1,0:T(8,128)S(1)}, bf16[512,128]{1,0:T(8,128)(2,1)S(1)}, bf16[2048,128]{1,0:T(8,128)(2,1)S(1)}) custom-call(s32[8]{0:T(128)S(1)} %bitcast.18, s32[1]{0:T(128)} %bitcast.1.idx_ref, bf16[16,320,128]{2,1,0:T(8,128)(2,1)S(1)} %all-to-all-done.recv_ref, f32[4,128,64]{2,1,0:T(8,128)S(1)} %copy.14.freq_ref), custom_call_target="tpu_custom_call" | custom-call | tf_op jit(solution)/shard_map/pallas_call | solution.py:277
  39.1 11.9 %all_to_all.30.mixed_ref = f32[16,32,128]{2,1,0:T(8,128)S(1)} all-to-all(f32[16,32,128]{2,1,0:T(8,128)S(1)} %get-tuple-element.19), channel_id=1, replica_groups=mesh['dp'=16,'blk'=16] {'blk'}, dimensions={0} | all-to-all | bytes 524288 | tf_op jit(solution)/shard_map/all_to_all | solution.py:288
  51.0 0.0 copy-done
  51.0 0.0 copy-done.2
  51.0 2.1 %shard_map.129 = (bf16[128,1024]{1,0:T(8,128)(2,1)}, bf16[16,288,128]{2,1,0:T(8,128)(2,1)S(1)}, f32[128,512]{1,0:T(8,128)S(1)}) custom-call(s32[8]{0:T(128)S(1)} %bitcast.19, s32[1]{0:T(128)} %bitcast.1.idx_ref, f32[16,32,128]{2,1,0:T(8,128)S(1)} %all_to_all.30.mixed_ref, bf16[128,512]{1,0:T(8,128)(2,1)S(1)} %bitcast.13, bf16[512,1024]{1,0:T(8,128)(2,1)S(1)} %copy-done, ...), custom_call_target="tpu_custom_call" | custom-call | tf_op jit(solution)/shard_map/pallas_call | solution.py:277
  53.1 22.1 %all_to_all.31.grads_ref = bf16[16,288,128]{2,1,0:T(8,128)(2,1)S(1)} all-to-all(bf16[16,288,128]{2,1,0:T(8,128)(2,1)S(1)} %get-tuple-element.23), channel_id=1, replica_groups=mesh['dp'=16,'blk'=16] {'blk'}, dimensions={0} | all-to-all | bytes 2359296 | tf_op jit(solution)/shard_map/all_to_all | solution.py:288
  75.2 5.9 %shard_map.130 = (bf16[16,320,128]{2,1,0:T(8,128)(2,1)S(1)}, bf16[16,16,128]{2,1,0:T(8,128)(2,1)S(1)}) custom-call(s32[8]{0:T(128)S(1)} %bitcast.20, s32[1]{0:T(128)} %bitcast.1.idx_ref, bf16[16,320,128]{2,1,0:T(8,128)(2,1)S(1)} %all-to-all-done.recv_ref, bf16[512,128]{1,0:T(8,128)(2,1)S(1)} %get-tuple-element.21.phiq_ref, ...), custom_call_target="tpu_custom_call" | custom-call | tf_op jit(solution)/shard_map/pallas_call | solution.py:277
  81.1 15.6 %all_to_all.32 = bf16[16,16,128]{2,1,0:T(8,128)(2,1)S(1)} all-to-all(bf16[16,16,128]{2,1,0:T(8,128)(2,1)S(1)} %get-tuple-element.26), channel_id=1, replica_groups=mesh['dp'=16,'blk'=16] {'dp'}, dimensions={0} | all-to-all | bytes 131072 | tf_op jit(solution)/shard_map/all_to_all | solution.py:288
  96.7 10.0 %all_to_all.33.gw_ref = bf16[16,16,128]{2,1,0:T(8,128)(2,1)S(1)} all-to-all(bf16[16,16,128]{2,1,0:T(8,128)(2,1)S(1)} %broadcast_in_dim.26), channel_id=1, replica_groups=mesh['dp'=16,'blk'=16] {'dp'}, dimensions={0} | all-to-all | bytes 131072 | tf_op jit(solution)/shard_map/all_to_all | solution.py:288
  106.7 26.0 %all_to_all.34.recv_ref = bf16[16,320,128]{2,1,0:T(8,128)(2,1)S(1)} all-to-all(bf16[16,320,128]{2,1,0:T(8,128)(2,1)S(1)} %get-tuple-element.24), channel_id=1, replica_groups=mesh['dp'=16,'blk'=16] {'blk'}, dimensions={0} | all-to-all | bytes 2621440 | tf_op jit(solution)/shard_map/all_to_all | solution.py:288
  132.6 0.9 shard_map.131
  (9 shorter events, 0.0 us)
Async XLA Ops:
  0.6 0.9 copy-start.1
  1.5 0.9 copy-start.4
  2.4 0.9 copy-start.5
  3.3 0.9 copy-start.6
  5.6 8.6 %copy-start.8 = (f32[4,128,64]{1,2,0:T(8,128)S(1)}, f32[4,128,64]{1,2,0:T(8,128)}, u32[]{:S(2)}) copy-start(f32[4,128,64]{1,2,0:T(8,128)} %param.12) | copy-start | bytes 393220
  5.6 28.8 %copy-start.7 = (s32[1,8]{1,0:T(1,128)S(1)}, s32[1,8]{1,0:T(1,128)}, u32[]{:S(2)}) copy-start(s32[1,8]{1,0:T(1,128)} %param.14) | copy-start | bytes 100
  5.6 28.7 %all-to-all-start = ((bf16[16,320,128]{2,1,0:T(8,128)(2,1)}), bf16[16,320,128]{2,1,0:T(8,128)(2,1)S(1)}, u32[]{:S(2)}, u32[]{:S(2)}) async-start(bf16[16,320,128]{2,1,0:T(8,128)(2,1)} %shard_map.127), calls=%async_computation | async-start | bytes 2621440 | tf_op jit(solution)/shard_map/all_to_all | solution.py:288
  14.2 36.8 %copy-start = (bf16[512,1024]{1,0:T(8,128)(2,1)S(1)}, bf16[512,1024]{1,0:T(8,128)(2,1)}, u32[]{:S(2)}) copy-start(bf16[512,1024]{1,0:T(8,128)(2,1)} %w_ref.1) | copy-start | bytes 3145732
  14.2 36.8 %copy-start.2 = (bf16[1,128,512]{2,1,0:T(8,128)(2,1)S(1)}, bf16[1,128,512]{2,1,0:T(8,128)(2,1)}, u32[]{:S(2)}) copy-start(bf16[1,128,512]{2,1,0:T(8,128)(2,1)} %param.11) | copy-start | bytes 393220
  14.2 36.8 %copy-start.3 = (bf16[1,128,1024]{2,1,0:T(8,128)(2,1)S(1)}, bf16[1,128,1024]{2,1,0:T(8,128)(2,1)}, u32[]{:S(2)}) copy-start(bf16[1,128,1024]{2,1,0:T(8,128)(2,1)} %param.15) | copy-start | bytes 786436

commit v2 on v1

v2 whole, which is shorter than its diff:
```python
import functools
import math

import jax
import jax.numpy as jnp
from jax import lax
from jax.experimental import pallas as pl
from jax.experimental.pallas import tpu as pltpu
from jax.sharding import PartitionSpec as P

EPS = 1e-05
HEADS, HEAD, FREQS, USERS = 4, 128, 64, 8
TOK, NBLK = 128, 16
SUB = TOK // 2
WIDTH, D = HEADS * HEAD, 1024
ROWS = SUB * NBLK
TILE = 2 * SUB
REACH = 5
TILES = ROWS // TILE
SCALE = 1.0 / math.sqrt(HEAD)
F32, BF16 = jnp.float32, jnp.bfloat16

Q0, G0, K0, V0, PACK = 0, SUB, SUB + 16, 2 * SUB + 16, 3 * SUB + 16
WROWS = (WIDTH // NBLK) * D // HEAD


def device(h, gq, gk):
    return 4 * h + 2 * gq + gk


NT = (((1,), (1,)), ((), ()))
NN = (((1,), (0,)), ((), ()))
TN = (((0,), (0,)), ((), ()))


def mm(a, b, dims):
    return lax.dot_general(a, b, dims, preferred_element_type=F32)


def lanes(shape):
    return lax.broadcasted_iota(jnp.int32, shape, 1)


def sublanes(shape):
    return lax.broadcasted_iota(jnp.int32, shape, 0)


def column(row, mine):
    return jnp.sum(jnp.where(mine, row, 0.0), axis=1, keepdims=True)


def starts_of(lens_ref, pos):
    end = jnp.int32(0)
    start = jnp.zeros_like(pos)
    for u in range(USERS):
        end = end + lens_ref[u]
        start = jnp.where(pos >= end, end, start)
    return start


def cos_sin(angles):
    turns = jnp.floor(angles * (2.0 / math.pi) + 0.5)
    r = angles - turns * 1.5703125
    r = r - turns * 4.837512969970703125e-4
    r = r - turns * 7.54978995489188e-8
    quad = turns.astype(jnp.int32) - jnp.where(lanes(angles.shape) >= FREQS, 1, 0)
    z = r * r
    c = 1.0 - 0.5 * z + z * z * (4.166664568e-2 + z * (-1.388731625e-3 + z * 2.443315712e-5))
    s = r + r * z * (-1.6666654611e-1 + z * (8.3321608736e-3 - z * 1.9515295891e-4))
    odd = (quad & 1) == 1
    value = jnp.where(odd, s, c)
    return jnp.where(((quad + 1) & 2) == 2, -value, value)


def pack_kernel(q_hbm, k_hbm, v_hbm, u_hbm, out_ref, q_ref, k_ref, v_ref, u_ref, sems):
    pairs = ((u_hbm, u_ref), (q_hbm, q_ref), (k_hbm, k_ref), (v_hbm, v_ref))
    copies = [pltpu.make_async_copy(src, dst, sems.at[i]) for i, (src, dst) in enumerate(pairs)]
    for copy in copies:
        copy.start()
    ones = jnp.ones((16, HEAD), BF16)
    copies[0].wait()
    for h in range(HEADS):
        total = mm(ones, u_ref[:, h * HEAD : (h + 1) * HEAD], NT)
        gate = jax.nn.sigmoid(total * SCALE)
        high = gate.astype(BF16).astype(F32)
        gate = jnp.where(sublanes((16, TOK)) < 8, high, gate - high).astype(BF16)
        for d in range(device(h, 0, 0), device(h, 1, 1) + 1):
            out_ref[d, G0:K0, :] = gate
    for copy in copies[1:]:
        copy.wait()
    for h in range(HEADS):
        cols = slice(h * HEAD, (h + 1) * HEAD)
        for gq in range(2):
            for gk in range(2):
                d = device(h, gq, gk)
                out_ref[d, Q0:G0, :] = q_ref[gq * SUB : (gq + 1) * SUB, cols]
                out_ref[d, K0:V0, :] = k_ref[gk * SUB : (gk + 1) * SUB, cols]
                out_ref[d, V0:PACK, :] = v_ref[gk * SUB : (gk + 1) * SUB, cols]


def stage_rows(recv_ref, lens_ref, gq, qp_s, gate_s, start_s, pos_s):
    pos = sublanes((NBLK, TOK)) * TOK + lanes((NBLK, TOK))
    starts = starts_of(lens_ref, pos).astype(F32)
    first = (sublanes((SUB, HEAD)) + gq * SUB).astype(F32)
    mine = lanes((SUB, TOK)) == sublanes((SUB, TOK)) + gq * SUB
    for b in range(NBLK):
        rows = slice(b * SUB, (b + 1) * SUB)
        qp_s[rows, :HEAD] = recv_ref[b, Q0:G0, :]
        parts = recv_ref[b, G0:K0, :].astype(F32)
        gate_s[rows, :] = jnp.broadcast_to(column(parts[0:1] + parts[8:9], mine), (SUB, HEAD))
        start_s[rows, :] = jnp.broadcast_to(column(starts[b : b + 1], mine), (SUB, HEAD))
        pos_s[rows, :] = first + float(b * TOK)


def tile_of(recv_ref, c, first, last):
    return jnp.concatenate(
        [recv_ref[2 * c, first:last, :], recv_ref[2 * c + 1, first:last, :]], axis=0
    )


def diagonal(a, b):
    zero = jnp.zeros_like(a)
    return jnp.concatenate(
        [jnp.concatenate([a, zero], axis=1), jnp.concatenate([zero, b], axis=1)], axis=0
    )


def masker(start_s, pos_s, rows, c, gk):
    lane = lanes((1, TILE))
    key = ((2 * c + (lane >> 6)) * TOK + gk * SUB + (lane & (SUB - 1))).astype(F32)
    top = slice(rows.start, rows.start + TILE)
    near = (key >= start_s[top, :]) & (key <= pos_s[top, :])
    if rows.stop == top.stop:
        return lambda x: jnp.where(near, x, 0.0)
    far = key >= start_s[top.stop : rows.stop, :]

    def masked(x):
        return jnp.concatenate(
            [jnp.where(near, x[:TILE], 0.0), jnp.where(far, x[TILE:], 0.0)], axis=0
        )

    return masked


def place(idx_ref):
    return idx_ref[0] // 4, (idx_ref[0] // 2) % 2, idx_ref[0] % 2


def tile_rows(c):
    return slice(c * TILE, min(c + REACH, TILES) * TILE)


def forward_kernel(
    lens_ref, idx_ref, recv_ref, freq_ref, mixed_ref, phiq_ref, phik_ref,
    qp_s, gate_s, start_s, pos_s, acc_s,
):
    head, gq, gk = place(idx_ref)
    stage_rows(recv_ref, lens_ref, gq, qp_s, gate_s, start_s, pos_s)
    freq = freq_ref[head]
    freq = jnp.concatenate([freq, freq], axis=1)
    pieces = []
    for _ in range(3):
        piece = freq.astype(BF16)
        pieces.append(piece)
        freq = freq - piece.astype(F32)
    pieces = jnp.concatenate(pieces, axis=1)

    def phi_of(x):
        a = mm(x, pieces, NN)
        angles = (a[:, 2 * HEAD :] + a[:, HEAD : 2 * HEAD]) + a[:, :HEAD]
        return (cos_sin(angles) / math.sqrt(FREQS)).astype(BF16)

    for i in range(4):
        rows = slice(i * ROWS // 4, (i + 1) * ROWS // 4)
        phiq = phi_of(qp_s[rows, :HEAD])
        phiq_ref[rows, :] = phiq
        qp_s[rows, HEAD:] = phiq
    acc_s[...] = jnp.zeros_like(acc_s)
    for c in range(TILES):
        rows = tile_rows(c)
        keys = tile_of(recv_ref, c, K0, V0)
        values = tile_of(recv_ref, c, V0, PACK)
        phik = phi_of(keys)
        phik_ref[c * TILE : (c + 1) * TILE, :] = phik
        both = mm(qp_s[rows, :], diagonal(keys, phik), NT)
        half, kern = both[:, :TILE] * (0.5 * SCALE), both[:, TILE:]
        both = half + half * jnp.tanh(half) + gate_s[rows, :] * kern
        both = masker(start_s, pos_s, rows, c, gk)(both).astype(BF16)
        acc_s[rows, :] += mm(both, values, NN)
    for b in range(NBLK):
        mixed_ref[b] = acc_s[b * SUB : (b + 1) * SUB, :].astype(BF16)


def hidden_grad_kernel(w_ref, cot_ref, gh_ref):
    gh_ref[...] = mm(cot_ref[...], w_ref[...], NT)


def middle_kernel(
    lens_ref, idx_ref, mixed_ref, u_ref, gh_ref, cot_ref, hid_ref, send_ref, ghn_ref
):
    pos = idx_ref[0] * TOK + sublanes((TOK, HEAD))
    count = (pos - starts_of(lens_ref, pos) + 1).astype(F32)
    inverse = jnp.concatenate([1.0 / count] * HEADS, axis=1)
    mixed = []
    for h in range(HEADS):
        halves = [
            mixed_ref[device(h, gq, 0)].astype(F32) + mixed_ref[device(h, gq, 1)].astype(F32)
            for gq in range(2)
        ]
        mixed.append(jnp.concatenate(halves, axis=0))
    mixed = jnp.concatenate(mixed, axis=1) * inverse
    gates = u_ref[...].astype(F32)
    centered = mixed - jnp.mean(mixed, axis=1, keepdims=True)
    rstd = lax.rsqrt(jnp.mean(centered * centered, axis=1, keepdims=True) + EPS)
    normed = centered * rstd
    hid_ref[...] = (normed * gates).astype(BF16)
    grad_hidden = gh_ref[...]
    ghn_ref[...] = grad_hidden * normed
    grad_normed = grad_hidden * gates
    grad_mixed = rstd * (
        grad_normed
        - jnp.mean(grad_normed, axis=1, keepdims=True)
        - normed * jnp.mean(grad_normed * normed, axis=1, keepdims=True)
    )
    scaled = (grad_mixed * inverse).astype(BF16)
    for h in range(HEADS):
        for gq in range(2):
            for gk in range(2):
                send_ref[device(h, gq, gk), 0:SUB, :] = scaled[
                    gq * SUB : (gq + 1) * SUB, h * HEAD : (h + 1) * HEAD
                ]
    for j in range(D // HEAD):
        part = mm(hid_ref[...], cot_ref[:, j * HEAD : (j + 1) * HEAD], TN).astype(BF16)
        for d in range(NBLK):
            send_ref[d, SUB + j * 32 : SUB + (j + 1) * 32, :] = part[d * 32 : (d + 1) * 32]


def out_kernel(hid_ref, w_ref, out_ref):
    out_ref[...] = mm(hid_ref[...], w_ref[...], NN).astype(BF16)


def sum_kernel(parts_ref, gw_ref):
    total = parts_ref[0, SUB:, :].astype(F32)
    for d in range(1, NBLK):
        total = total + parts_ref[d, SUB:, :].astype(F32)
    gw_ref[...] = total.astype(BF16)


def backward_kernel(
    lens_ref, idx_ref, recv_ref, phiq_ref, phik_ref, grads_ref, freq_ref, send_ref,
    qp_s, gate_s, start_s, pos_s, sc_s, dqp_s, term_s,
):
    head, gq, gk = place(idx_ref)
    stage_rows(recv_ref, lens_ref, gq, qp_s, gate_s, start_s, pos_s)
    qp_s[:, HEAD:] = phiq_ref[...]
    for b in range(NBLK):
        sc_s[b * SUB : (b + 1) * SUB, :] = grads_ref[b, 0:SUB, :]
    freq = freq_ref[head].astype(BF16)
    freq = jnp.concatenate([freq, -freq], axis=1)
    dqp_s[...] = jnp.zeros_like(dqp_s)
    term_s[...] = jnp.zeros_like(term_s)

    def back(phi, grad_phi):
        turned = pltpu.roll(grad_phi, FREQS, 1)
        return mm((phi.astype(F32) * turned).astype(BF16), freq, NT)

    for c in range(TILES):
        rows = tile_rows(c)
        keys = tile_of(recv_ref, c, K0, V0)
        values = tile_of(recv_ref, c, V0, PACK)
        phik = phik_ref[c * TILE : (c + 1) * TILE, :]
        pairs = diagonal(keys, phik)
        scaled, gate = sc_s[rows, :], gate_s[rows, :]
        masked = masker(start_s, pos_s, rows, c, gk)
        both = mm(qp_s[rows, :], pairs, NT)
        half, kern = both[:, :TILE] * (0.5 * SCALE), both[:, TILE:]
        t = jnp.tanh(half)
        weights = half + half * t
        slope = (1.0 + t) + weights * (1.0 - t)
        grad_w = masked(mm(scaled, values, NT))
        both = masked(weights + gate * kern).astype(BF16)
        grad_s = (grad_w * slope * (0.5 * SCALE)).astype(BF16)
        grad_k = (grad_w * gate).astype(BF16)
        term_s[rows, :] += kern * grad_w
        dqp_s[rows, :] += mm(jnp.concatenate([grad_s, grad_k], axis=1), pairs, NN)
        dkey = mm(grad_s, qp_s[rows, :HEAD], TN)
        dkey = dkey + back(phik, mm(grad_k, qp_s[rows, HEAD:], TN))
        dval = mm(both, scaled, TN)
        for i in range(2):
            send_ref[2 * c + i, K0:V0, :] = dkey[i * SUB : (i + 1) * SUB].astype(BF16)
            send_ref[2 * c + i, V0:PACK, :] = dval[i * SUB : (i + 1) * SUB].astype(BF16)
    dq = dqp_s[:, :HEAD] + back(phiq_ref[...], dqp_s[:, HEAD:])
    gate = gate_s[...]
    term = jnp.sum(term_s[...], axis=1, keepdims=True) * gate * (1.0 - gate) * SCALE
    mine = lanes((SUB, HEAD)) == sublanes((SUB, HEAD))
    for b in range(NBLK):
        rows = slice(b * SUB, (b + 1) * SUB)
        send_ref[b, Q0:G0, :] = dq[rows].astype(BF16)
        across = jnp.sum(jnp.where(mine, term[rows], 0.0), axis=0, keepdims=True)
        send_ref[b, G0:K0, :] = jnp.broadcast_to(across, (16, HEAD)).astype(BF16)


def final_kernel(recv_ref, ghn_ref, gw_ref, dq_ref, dk_ref, dv_ref, dg_ref, dw_ref):
    mine = lanes((SUB, HEAD)) == sublanes((SUB, HEAD))

    def pair(one, two, first, last):
        return recv_ref[one, first:last, :].astype(F32) + recv_ref[two, first:last, :].astype(F32)

    for h in range(HEADS):
        cols = slice(h * HEAD, (h + 1) * HEAD)
        for i in range(2):
            rows = slice(i * SUB, (i + 1) * SUB)
            one, two = device(h, i, 0), device(h, i, 1)
            dq_ref[rows, cols] = pair(one, two, Q0, G0).astype(BF16)
            term = column(pair(one, two, G0, K0)[0:1], mine)
            dg_ref[rows, cols] = (ghn_ref[rows, cols] + term).astype(BF16)
            one, two = device(h, 0, i), device(h, 1, i)
            dk_ref[rows, cols] = pair(one, two, K0, V0).astype(BF16)
            dv_ref[rows, cols] = pair(one, two, V0, PACK).astype(BF16)
    for j in range(D // HEAD):
        dw_ref[:, j * HEAD : (j + 1) * HEAD] = gw_ref[j * 32 : (j + 1) * 32]


VMEM = pl.BlockSpec(memory_space=pltpu.VMEM)
SMEM = pl.BlockSpec(memory_space=pltpu.SMEM)
ANY = pl.BlockSpec(memory_space=pl.ANY)


def call(body, scalars, arrays, outs, scratch=(), us=1.0, space=VMEM, mib=16):
    return pl.pallas_call(
        body,
        in_specs=[SMEM] * len(scalars) + [space] * len(arrays),
        out_specs=[VMEM] * len(outs),
        out_shape=[jax.ShapeDtypeStruct(s, t) for s, t in outs],
        scratch_shapes=[pltpu.VMEM(*s) if isinstance(s, tuple) else s for s in scratch],
        compiler_params=pltpu.CompilerParams(vmem_limit_bytes=mib * 1024 * 1024),
        cost_estimate=pl.CostEstimate(
            flops=int(us * 1.1e9), bytes_accessed=1024, transcendentals=0
        ),
    )(*scalars, *arrays)


def swap(a, axis):
    return lax.all_to_all(a, axis, 0, 0, tiled=True)


def local(q, k, v, u, freqs, w, lens, cot):
    q, k, v, u, cot, lens = q[0], k[0], v[0], u[0], cot[0], lens[0]
    idx = lax.axis_index("blk").astype(jnp.int32)[None]
    staged = [
        ((ROWS, 2 * HEAD), BF16),
        ((ROWS, HEAD), F32),
        ((ROWS, HEAD), F32),
        ((ROWS, HEAD), F32),
    ]
    (send1,) = call(
        pack_kernel,
        [],
        [q, k, v, u],
        [((NBLK, PACK, HEAD), BF16)],
        [((TOK, WIDTH), BF16)] * 4 + [pltpu.SemaphoreType.DMA((4,))],
        space=ANY,
        mib=60,
    )
    recv1 = swap(send1, "blk")
    (gh,) = call(hidden_grad_kernel, [], [w, cot], [((TOK, WIDTH), F32)])
    mixed, phiq, phik = call(
        forward_kernel,
        [lens, idx],
        [recv1, freqs],
        [((NBLK, SUB, HEAD), BF16), ((ROWS, HEAD), BF16), ((ROWS, HEAD), BF16)],
        staged + [((ROWS, HEAD), F32)],
        us=4.5,
    )
    recv2 = swap(mixed, "blk")
    hidden, send3, ghn = call(
        middle_kernel,
        [lens, idx],
        [recv2, u, gh, cot],
        [((TOK, WIDTH), BF16), ((NBLK, SUB + WROWS, HEAD), BF16), ((TOK, WIDTH), F32)],
    )
    recv3 = swap(send3, "blk")
    (gw,) = call(sum_kernel, [], [recv3], [((WROWS, HEAD), BF16)])
    (layer_out,) = call(out_kernel, [], [hidden, w], [((TOK, D), BF16)])
    (send4,) = call(
        backward_kernel,
        [lens, idx],
        [recv1, phiq, phik, recv3, freqs],
        [((NBLK, PACK, HEAD), BF16)],
        staged + [((ROWS, HEAD), BF16), ((ROWS, 2 * HEAD), F32), ((ROWS, HEAD), F32)],
        us=5.5,
    )
    for mask in (8, 1, 2, 4):
        other = lax.ppermute(gw, "dp", [(i, i ^ mask) for i in range(16)])
        gw = gw.astype(F32) + other.astype(F32)
        if mask != 4:
            gw = gw.astype(BF16)
        if mask == 8:
            send4, gw = lax.optimization_barrier((send4, gw))
    recv4 = swap(send4, "blk")
    dq, dk, dv, dg, dw = call(
        final_kernel,
        [],
        [recv4, ghn, gw],
        [((TOK, WIDTH), BF16)] * 4 + [((WIDTH // NBLK, D), F32)],
    )
    return layer_out[None], dq[None], dk[None], dv[None], dg[None], dw


def solution(mesh):
    rows = P("dp", "blk", None)
    return jax.shard_map(
        local,
        mesh=mesh,
        in_specs=(rows, rows, rows, rows, P(), P(), P("dp", None), rows),
        out_specs=(rows, rows, rows, rows, rows, P("blk", None)),
        check_vma=False,
    )
```

time: 134 us -> 100 us (0.75)
  blocking collectives: 85.5 us -> 23.2 us
  starting transfers between devices: 8.58 us -> 28 us
  waiting for transfers between devices: 20 us -> 29 us
  local copies, waits for them, and re-layouts: 3.77 us -> 1.94 us
  Pallas kernels: 15 us -> 16.7 us
    all_to_all x5 -> x1, blocking collectives: 85.5 us -> 23.2 us  [swap(): return lax.all_to_all(a, axis, 0, 0, tiled=True)]
    ppermute x0 -> x4, starting transfers between devices: none -> 10.8 us  [local(): other = lax.ppermute(gw, 'dp', [(i, i ^ mask) for i in range(16)])]
    all_to_all x1 -> x3, starting transfers between devices: 8.58 us -> 17.1 us  [swap(): return lax.all_to_all(a, axis, 0, 0, tiled=True)]
    all_to_all x1 -> x3, waiting for transfers between devices: 20 us -> 24.8 us  [swap(): return lax.all_to_all(a, axis, 0, 0, tiled=True)]
    ppermute x0 -> x4, waiting for transfers between devices: none -> 4.15 us  [local(): other = lax.ppermute(gw, 'dp', [(i, i ^ mask) for i in range(16)])]
    unnamed x19, local copies, waits for them, and re-layouts: 3.76 us -> 1.94 us
    pallas_call x5 -> x8, Pallas kernels: 15 us -> 16.7 us  [call(): pl.pallas_call(body, in_specs=[SMEM] * len(scalars) + [space] * len(array...]
  transfers between devices with their start and end apart: 1 -> 7, of which waited for: 1 -> 5; matrix products, arithmetic and copies ran while one was open for 0% -> 0% of each run, Pallas kernels for 0% -> 8%
where the time goes in v2:
time: 100 us; the launch traced here: 99.6 us
  waiting for transfers between devices  29 us (29%)
  starting transfers between devices  28 us (28%)
  blocking collectives  23.2 us (23%)
  Pallas kernels  16.7 us (17%)
  local copies, waits for them, and re-layouts  1.94 us (2%)
    all_to_all x3, waiting for transfers between devices, swap(): return lax.all_to_all(a, axis, 0, 0, tiled=True)  24.8 us
    all_to_all x1, blocking collectives, swap(): return lax.all_to_all(a, axis, 0, 0, tiled=True)  23.2 us
    all_to_all x3, starting transfers between devices, swap(): return lax.all_to_all(a, axis, 0, 0, tiled=True)  17.1 us
    pallas_call x8, Pallas kernels, call(): pl.pallas_call(body, in_specs=[SMEM] * len(scalars) + [space] * len(array...  16.7 us
    ppermute x4, starting transfers between devices, local(): other = lax.ppermute(gw, 'dp', [(i, i ^ mask) for i in range(16)])  10.8 us
    ppermute x4, waiting for transfers between devices, local(): other = lax.ppermute(gw, 'dp', [(i, i ^ mask) for i in range(16)])  4.15 us
  transfers between devices with their start and end apart: 7, of which 5 were waited for; matrix products, arithmetic and copies ran while one was open for 0% of the time, Pallas kernels for 8%

profile of v2, /device:TPU:1, one launch (start us, length us, event | category | flops | bytes accessed | tf_op | source)
XLA Modules:
  0.0 99.6 jit_solution(12303741901511001747)
XLA Ops:
  0.6 2.1 %shard_map.127 = bf16[16,208,128]{2,1,0:T(8,128)(2,1)} custom-call(bf16[128,512]{1,0:T(8,128)(2,1)} %bitcast.19, bf16[128,512]{1,0:T(8,128)(2,1)} %bitcast.20, bf16[128,512]{1,0:T(8,128)(2,1)} %bitcast.21, bf16[128,512]{1,0:T(8,128)(2,1)} %bitcast.14), custom_call_target="tpu_custom_call" | custom-call | flops 1100000000 | bytes 1024 | tf_op jit(solution)/shard_map/pallas_call | solution.py:330
  2.8 8.6 %all-to-all-start = ((bf16[16,208,128]{2,1,0:T(8,128)(2,1)}), bf16[16,208,128]{2,1,0:T(8,128)(2,1)S(1)}, u32[]{:S(2)}, u32[]{:S(2)}) async-start(bf16[16,208,128]{2,1,0:T(8,128)(2,1)} %shard_map.127), calls=%async_computation | async-start | bytes 1703936 | tf_op jit(solution)/shard_map/all_to_all | solution.py:344
  11.5 15.1 %all-to-all-done.recv_ref = bf16[16,208,128]{2,1,0:T(8,128)(2,1)S(1)} async-done(((bf16[16,208,128]{2,1,0:T(8,128)(2,1)}), bf16[16,208,128]{2,1,0:T(8,128)(2,1)S(1)}, u32[]{:S(2)}, u32[]{:S(2)}) %all-to-all-start) | async-done | bytes 852000 | tf_op jit(solution)/shard_map/all_to_all | solution.py:344
  26.7 4.4 %shard_map.128 = (bf16[16,64,128]{2,1,0:T(8,128)(2,1)}, bf16[1024,128]{1,0:T(8,128)(2,1)S(1)}, bf16[1024,128]{1,0:T(8,128)(2,1)S(1)}) custom-call(s32[8]{0:T(128)S(1)} %bitcast.16, s32[1]{0:T(128)} %bitcast.1.idx_ref, bf16[16,208,128]{2,1,0:T(8,128)(2,1)S(1)} %all-to-all-done.recv_ref, f32[4,128,64]{2,1,0:T(8,128)S(1)} %copy.14.freq_ref), custom_call_target="tpu_custom_call" | custom-call | flops 4950000128 | bytes 1024 | tf_op jit(solution)/shard_map/pallas_call | solution.py:330
  31.1 0.7 copy-done.4
  31.8 0.7 copy-done.6
  32.5 4.0 %all-to-all-start.1 = ((bf16[16,64,128]{2,1,0:T(8,128)(2,1)}), bf16[16,64,128]{2,1,0:T(8,128)(2,1)S(1)}, u32[]{:S(2)}, u32[]{:S(2)}) async-start(bf16[16,64,128]{2,1,0:T(8,128)(2,1)} %get-tuple-element.19), calls=%async_computation.1 | async-start | bytes 524288 | tf_op jit(solution)/shard_map/all_to_all | solution.py:344
  36.6 0.5 shard_map.129.gh_ref
  37.1 8.2 %all-to-all-done.1.mixed_ref = bf16[16,64,128]{2,1,0:T(8,128)(2,1)S(1)} async-done(((bf16[16,64,128]{2,1,0:T(8,128)(2,1)}), bf16[16,64,128]{2,1,0:T(8,128)(2,1)S(1)}, u32[]{:S(2)}, u32[]{:S(2)}) %all-to-all-start.1) | async-done | bytes 262176 | tf_op jit(solution)/shard_map/all_to_all | solution.py:344
  45.3 1.3 %shard_map.130 = (bf16[128,512]{1,0:T(8,128)(2,1)S(1)}, bf16[16,320,128]{2,1,0:T(8,128)(2,1)S(1)}, f32[128,512]{1,0:T(8,128)S(1)}) custom-call(s32[8]{0:T(128)S(1)} %bitcast.17, s32[1]{0:T(128)} %bitcast.1.idx_ref, bf16[16,64,128]{2,1,0:T(8,128)(2,1)S(1)} %all-to-all-done.1.mixed_ref, bf16[128,512]{1,0:T(8,128)(2,1)S(1)} %bitcast.15, ...), custom_call_target="tpu_custom_call" | custom-call | flops 1100000000 | bytes 1024 | tf_op jit(solution)/shard_map/pallas_call | solution.py:330
  46.6 23.2 %all_to_all.20.grads_ref.parts_ref = bf16[16,320,128]{2,1,0:T(8,128)(2,1)S(1)} all-to-all(bf16[16,320,128]{2,1,0:T(8,128)(2,1)S(1)} %get-tuple-element.23), channel_id=1, replica_groups=mesh['dp'=16,'blk'=16] {'blk'}, dimensions={0} | all-to-all | bytes 2621440 | tf_op jit(solution)/shard_map/all_to_all | solution.py:344
  69.8 0.1 shard_map.133
  69.9 0.5 collective-permute-start
  70.4 0.3 copy-done.5
  70.8 6.2 %shard_map.132 = bf16[16,208,128]{2,1,0:T(8,128)(2,1)} custom-call(s32[8]{0:T(128)S(1)} %bitcast.18, s32[1]{0:T(128)} %bitcast.1.idx_ref, bf16[16,208,128]{2,1,0:T(8,128)(2,1)S(1)} %all-to-all-done.recv_ref, bf16[1024,128]{1,0:T(8,128)(2,1)S(1)} %copy-done.5, bf16[1024,128]{1,0:T(8,128)(2,1)S(1)} %copy-done.7, ...), custom_call_target="tpu_custom_call" | custom-call | flops 6049999872 | bytes 1024 | tf_op jit(solution)/shard_map/pallas_call | solution.py:330
  77.0 1.7 %collective-permute-start.1 = (bf16[256,128]{1,0:T(8,128)(2,1)S(1)}, bf16[256,128]{1,0:T(8,128)(2,1)S(1)}, u32[]{:S(2)}, u32[]{:S(2)}) collective-permute-start(bf16[256,128]{1,0:T(8,128)(2,1)S(1)} %add_convert_fusion.2), channel_id=1, source_target_pairs={{0,16},{16,0},{32,48},{48,32},{64,80},{80,64},{96,112},{112,96},{1... | collective-permute-start | bytes 196616 | tf_op jit(solution)/shard_map/ppermute | solution.py:394
  78.8 4.5 %all-to-all-start.3 = ((bf16[16,208,128]{2,1,0:T(8,128)(2,1)}), bf16[16,208,128]{2,1,0:T(8,128)(2,1)S(1)}, u32[]{:S(2)}, u32[]{:S(2)}) async-start(bf16[16,208,128]{2,1,0:T(8,128)(2,1)} %shard_map.132), calls=%async_computation.3 | async-start | bytes 1703936 | tf_op jit(solution)/shard_map/all_to_all | solution.py:344
  83.3 3.1 %collective-permute-start.2 = (bf16[256,128]{1,0:T(8,128)(2,1)S(1)}, bf16[256,128]{1,0:T(8,128)(2,1)S(1)}, u32[]{:S(2)}, u32[]{:S(2)}) collective-permute-start(bf16[256,128]{1,0:T(8,128)(2,1)S(1)} %add_convert_fusion.1), channel_id=1, source_target_pairs={{0,32},{16,48},{32,0},{48,16},{64,96},{80,112},{96,64},{112,80},{1... | collective-permute-start | bytes 196616 | tf_op jit(solution)/shard_map/ppermute | solution.py:394
  86.4 3.5 %collective-permute-done.2 = bf16[256,128]{1,0:T(8,128)(2,1)S(1)} collective-permute-done((bf16[256,128]{1,0:T(8,128)(2,1)S(1)}, bf16[256,128]{1,0:T(8,128)(2,1)S(1)}, u32[]{:S(2)}, u32[]{:S(2)}) %collective-permute-start.2) | collective-permute-done | bytes 65568 | tf_op jit(solution)/shard_map/ppermute | solution.py:394
  89.9 5.6 %collective-permute-start.3 = (bf16[256,128]{1,0:T(8,128)(2,1)S(1)}, bf16[256,128]{1,0:T(8,128)(2,1)S(1)}, u32[]{:S(2)}, u32[]{:S(2)}) collective-permute-start(bf16[256,128]{1,0:T(8,128)(2,1)S(1)} %add_convert_fusion), channel_id=1, source_target_pairs={{0,64},{16,80},{32,96},{48,112},{64,0},{80,16},{96,32},{112,48},{1... | collective-permute-start | bytes 196616 | tf_op jit(solution)/shard_map/ppermute | solution.py:394
  95.4 1.0 %shard_map.131 = bf16[128,1024]{1,0:T(8,128)(2,1)} custom-call(bf16[128,512]{1,0:T(8,128)(2,1)S(1)} %get-tuple-element.20.hid_ref, bf16[512,1024]{1,0:T(8,128)(2,1)S(1)} %copy-done), custom_call_target="tpu_custom_call" | custom-call | flops 1100000000 | bytes 1024 | tf_op jit(solution)/shard_map/pallas_call | solution.py:330
  96.5 0.7 collective-permute-done.3
  97.2 1.5 %all-to-all-done.3.recv_ref = bf16[16,208,128]{2,1,0:T(8,128)(2,1)S(1)} async-done(((bf16[16,208,128]{2,1,0:T(8,128)(2,1)}), bf16[16,208,128]{2,1,0:T(8,128)(2,1)S(1)}, u32[]{:S(2)}, u32[]{:S(2)}) %all-to-all-start.3) | async-done | bytes 852000 | tf_op jit(solution)/shard_map/all_to_all | solution.py:344
  98.6 0.9 shard_map.134
  (22 shorter events, 0.3 us)
Async XLA Ops:
  2.8 8.6 %copy-start.8 = (f32[4,128,64]{1,2,0:T(8,128)S(1)}, f32[4,128,64]{1,2,0:T(8,128)}, u32[]{:S(2)}) copy-start(f32[4,128,64]{1,2,0:T(8,128)} %param.12) | copy-start | bytes 393220
  2.8 23.9 %copy-start.3 = (s32[1,8]{1,0:T(1,128)S(1)}, s32[1,8]{1,0:T(1,128)}, u32[]{:S(2)}) copy-start(s32[1,8]{1,0:T(1,128)} %param.14) | copy-start | bytes 100
  2.8 23.8 %all-to-all-start = ((bf16[16,208,128]{2,1,0:T(8,128)(2,1)}), bf16[16,208,128]{2,1,0:T(8,128)(2,1)S(1)}, u32[]{:S(2)}, u32[]{:S(2)}) async-start(bf16[16,208,128]{2,1,0:T(8,128)(2,1)} %shard_map.127), calls=%async_computation | async-start | bytes 1703936 | tf_op jit(solution)/shard_map/all_to_all | solution.py:344
  26.6 9.9 %copy-start = (bf16[512,1024]{1,0:T(8,128)(2,1)S(1)}, bf16[512,1024]{1,0:T(8,128)(2,1)}, u32[]{:S(2)}) copy-start(bf16[512,1024]{1,0:T(8,128)(2,1)} %w_ref.3) | copy-start | bytes 3145732
  26.7 9.9 %copy-start.1 = (bf16[1,128,1024]{2,1,0:T(8,128)(2,1)S(1)}, bf16[1,128,1024]{2,1,0:T(8,128)(2,1)}, u32[]{:S(2)}) copy-start(bf16[1,128,1024]{2,1,0:T(8,128)(2,1)} %param.15) | copy-start | bytes 786436
  31.1 0.7 copy-start.4
  31.8 0.7 copy-start.6
  32.5 12.8 %all-to-all-start.1 = ((bf16[16,64,128]{2,1,0:T(8,128)(2,1)}), bf16[16,64,128]{2,1,0:T(8,128)(2,1)S(1)}, u32[]{:S(2)}, u32[]{:S(2)}) async-start(bf16[16,64,128]{2,1,0:T(8,128)(2,1)} %get-tuple-element.19), calls=%async_computation.1 | async-start | bytes 524288 | tf_op jit(solution)/shard_map/all_to_all | solution.py:344
  36.5 8.7 %copy-start.2 = (bf16[1,128,512]{2,1,0:T(8,128)(2,1)S(1)}, bf16[1,128,512]{2,1,0:T(8,128)(2,1)}, u32[]{:S(2)}) copy-start(bf16[1,128,512]{2,1,0:T(8,128)(2,1)} %param.11) | copy-start | bytes 393220
  69.8 1.0 copy-start.5
  69.8 1.0 %copy-start.7 = (bf16[1024,128]{1,0:T(8,128)(2,1)S(1)}, bf16[1024,128]{1,0:T(8,128)(2,1)}, u32[]{:S(2)}) copy-start(bf16[1024,128]{1,0:T(8,128)(2,1)} %copy-done.6) | copy-start | bytes 786436
  69.9 7.1 %collective-permute-start = (bf16[256,128]{1,0:T(8,128)(2,1)S(1)}, bf16[256,128]{1,0:T(8,128)(2,1)S(1)}, u32[]{:S(2)}, u32[]{:S(2)}) collective-permute-start(bf16[256,128]{1,0:T(8,128)(2,1)S(1)} %shard_map.133), channel_id=1, source_target_pairs={{0,128},{16,144},{32,160},{48,176},{64,192},{80,208},{96,224},{112... | collective-permute-start | bytes 196616 | tf_op jit(solution)/shard_map/ppermute | solution.py:394
  77.0 6.2 %collective-permute-start.1 = (bf16[256,128]{1,0:T(8,128)(2,1)S(1)}, bf16[256,128]{1,0:T(8,128)(2,1)S(1)}, u32[]{:S(2)}, u32[]{:S(2)}) collective-permute-start(bf16[256,128]{1,0:T(8,128)(2,1)S(1)} %add_convert_fusion.2), channel_id=1, source_target_pairs={{0,16},{16,0},{32,48},{48,32},{64,80},{80,64},{96,112},{112,96},{1... | collective-permute-start | bytes 196616 | tf_op jit(solution)/shard_map/ppermute | solution.py:394
  78.8 19.9 %all-to-all-start.3 = ((bf16[16,208,128]{2,1,0:T(8,128)(2,1)}), bf16[16,208,128]{2,1,0:T(8,128)(2,1)S(1)}, u32[]{:S(2)}, u32[]{:S(2)}) async-start(bf16[16,208,128]{2,1,0:T(8,128)(2,1)} %shard_map.132), calls=%async_computation.3 | async-start | bytes 1703936 | tf_op jit(solution)/shard_map/all_to_all | solution.py:344
  83.3 6.5 %collective-permute-start.2 = (bf16[256,128]{1,0:T(8,128)(2,1)S(1)}, bf16[256,128]{1,0:T(8,128)(2,1)S(1)}, u32[]{:S(2)}, u32[]{:S(2)}) collective-permute-start(bf16[256,128]{1,0:T(8,128)(2,1)S(1)} %add_convert_fusion.1), channel_id=1, source_target_pairs={{0,32},{16,48},{32,0},{48,16},{64,96},{80,112},{96,64},{112,80},{1... | collective-permute-start | bytes 196616 | tf_op jit(solution)/shard_map/ppermute | solution.py:394
  89.9 7.3 %collective-permute-start.3 = (bf16[256,128]{1,0:T(8,128)(2,1)S(1)}, bf16[256,128]{1,0:T(8,128)(2,1)S(1)}, u32[]{:S(2)}, u32[]{:S(2)}) collective-permute-start(bf16[256,128]{1,0:T(8,128)(2,1)S(1)} %add_convert_fusion), channel_id=1, source_target_pairs={{0,64},{16,80},{32,96},{48,112},{64,0},{80,16},{96,32},{112,48},{1... | collective-permute-start | bytes 196616 | tf_op jit(solution)/shard_map/ppermute | solution.py:394

commit v3 on v2

--- a/solution.py
+++ b/solution.py
@@ -1,4 +1,3 @@
-import functools
 import math
 
 import jax
@@ -244,6 +243,11 @@
     for d in range(1, NBLK):
         total = total + parts_ref[d, SUB:, :].astype(F32)
     gw_ref[...] = total.astype(BF16)
+
+
+def add_kernel(one_ref, two_ref, out_ref):
+    total = one_ref[...].astype(F32) + two_ref[...].astype(F32)
+    out_ref[...] = total.astype(out_ref.dtype)
 
 
 def backward_kernel(
@@ -326,18 +330,26 @@
 ANY = pl.BlockSpec(memory_space=pl.ANY)
 
 
-def call(body, scalars, arrays, outs, scratch=(), us=1.0, space=VMEM, mib=16):
+def call(body, scalars, arrays, outs, scratch=(), us=1.0, space=VMEM, mib=16, after=()):
+    if after:
+        inner, first = body, len(scalars) + len(arrays)
+
+        def body(*refs):
+            inner(*refs[:first], *refs[first + len(after) :])
+
+    moved = sum(x.size * x.dtype.itemsize for x in arrays)
+    moved += sum(math.prod(s) * jnp.dtype(t).itemsize for s, t in outs)
     return pl.pallas_call(
         body,
-        in_specs=[SMEM] * len(scalars) + [space] * len(arrays),
+        in_specs=[SMEM] * len(scalars) + [space] * len(arrays) + [ANY] * len(after),
         out_specs=[VMEM] * len(outs),
         out_shape=[jax.ShapeDtypeStruct(s, t) for s, t in outs],
         scratch_shapes=[pltpu.VMEM(*s) if isinstance(s, tuple) else s for s in scratch],
         compiler_params=pltpu.CompilerParams(vmem_limit_bytes=mib * 1024 * 1024),
         cost_estimate=pl.CostEstimate(
-            flops=int(us * 1.1e9), bytes_accessed=1024, transcendentals=0
+            flops=int(us * 1.1e9), bytes_accessed=moved, transcendentals=0
         ),
-    )(*scalars, *arrays)
+    )(*scalars, *arrays, *after)
 
 
 def swap(a, axis):
@@ -370,6 +382,7 @@
         [recv1, freqs],
         [((NBLK, SUB, HEAD), BF16), ((ROWS, HEAD), BF16), ((ROWS, HEAD), BF16)],
         staged + [((ROWS, HEAD), F32)],
+        after=[gh],
         us=4.5,
     )
     recv2 = swap(mixed, "blk")
@@ -392,9 +405,8 @@
     )
     for mask in (8, 1, 2, 4):
         other = lax.ppermute(gw, "dp", [(i, i ^ mask) for i in range(16)])
-        gw = gw.astype(F32) + other.astype(F32)
-        if mask != 4:
-            gw = gw.astype(BF16)
+        kind = F32 if mask == 4 else BF16
+        (gw,) = call(add_kernel, [], [gw, other], [((WROWS, HEAD), kind)], us=0.5)
         if mask == 8:
             send4, gw = lax.optimization_barrier((send4, gw))
     recv4 = swap(send4, "blk")

time: 100 us -> 98.9 us (0.989)
  the two profiles are of different devices: /device:TPU:1 before, /device:TPU:24 now
where the time goes in v3:
time: 98.9 us; the launch traced here: 98.6 us
  blocking collectives  35.1 us (35%)
  starting transfers between devices  27.7 us (28%)
  waiting for transfers between devices  18.8 us (19%)
  Pallas kernels  16 us (16%)
    all_to_all x2, blocking collectives, swap(): return lax.all_to_all(a, axis, 0, 0, tiled=True)  35.1 us
    pallas_call x12, Pallas kernels, call(): pl.pallas_call(body, in_specs=[SMEM] * len(scalars) + [space] * len(array...  16 us
    all_to_all x2, starting transfers between devices, swap(): return lax.all_to_all(a, axis, 0, 0, tiled=True)  14.5 us
    ppermute x4, starting transfers between devices, local(): other = lax.ppermute(gw, 'dp', [(i, i ^ mask) for i in range(16)])  13.2 us
    all_to_all x2, waiting for transfers between devices, swap(): return lax.all_to_all(a, axis, 0, 0, tiled=True)  12.3 us
    ppermute x4, waiting for transfers between devices, local(): other = lax.ppermute(gw, 'dp', [(i, i ^ mask) for i in range(16)])  6.5 us
  transfers between devices with their start and end apart: 6, of which 4 were waited for; matrix products, arithmetic and copies ran while one was open for 0% of the time, Pallas kernels for 8%

profile of v3, /device:TPU:24, one launch (start us, length us, event | category | flops | bytes accessed | tf_op | source)
XLA Modules:
  0.0 98.6 jit_solution(655423709715645667)
XLA Ops:
  0.6 2.2 %shard_map.127 = bf16[16,208,128]{2,1,0:T(8,128)(2,1)} custom-call(bf16[128,512]{1,0:T(8,128)(2,1)} %bitcast.19, bf16[128,512]{1,0:T(8,128)(2,1)} %bitcast.20, bf16[128,512]{1,0:T(8,128)(2,1)} %bitcast.21, bf16[128,512]{1,0:T(8,128)(2,1)} %bitcast.14), custom_call_target="tpu_custom_call" | custom-call | flops 1100000000 | bytes 1376256 | tf_op jit(solution)/shard_map/pallas_call | solution.py:342
  2.8 0.0 copy-start.4
  2.8 0.0 copy-start
  2.8 7.4 %all-to-all-start = ((bf16[16,208,128]{2,1,0:T(8,128)(2,1)}), bf16[16,208,128]{2,1,0:T(8,128)(2,1)S(1)}, u32[]{:S(2)}, u32[]{:S(2)}) async-start(bf16[16,208,128]{2,1,0:T(8,128)(2,1)} %shard_map.127), calls=%async_computation | async-start | bytes 1703936 | tf_op jit(solution)/shard_map/all_to_all | solution.py:356
  10.3 0.1 copy.14.refs_3_.freq_ref
  10.4 0.0 copy-start.3
  10.4 0.5 shard_map.128.refs_4_.gh_ref
  10.9 12.3 %all-to-all-done.refs_2_.recv_ref = bf16[16,208,128]{2,1,0:T(8,128)(2,1)S(1)} async-done(((bf16[16,208,128]{2,1,0:T(8,128)(2,1)}), bf16[16,208,128]{2,1,0:T(8,128)(2,1)S(1)}, u32[]{:S(2)}, u32[]{:S(2)}) %all-to-all-start) | async-done | bytes 852000 | tf_op jit(solution)/shard_map/all_to_all | solution.py:356
  23.3 3.7 %shard_map.129 = (bf16[16,64,128]{2,1,0:T(8,128)(2,1)S(1)}, bf16[1024,128]{1,0:T(8,128)(2,1)S(1)}, bf16[1024,128]{1,0:T(8,128)(2,1)S(1)}) custom-call(s32[8]{0:T(128)S(1)} %bitcast.16, s32[1]{0:T(128)} %bitcast.1.refs_1_.idx_ref, bf16[16,208,128]{2,1,0:T(8,128)(2,1)S(1)} %all-to-all-done.refs_2_.recv_ref, f32[4,128,64]{2,1,0:T(8,128)S(1)} %copy.14.refs_3_.freq_ref, ...), custom_call_target="tpu_custom_call" | custom-call | flops 4950000128 | bytes 1769472 | tf_op jit(solution)/shard_map/pallas_call | solution.py:342
  27.0 11.9 %all_to_all.20.mixed_ref = bf16[16,64,128]{2,1,0:T(8,128)(2,1)S(1)} all-to-all(bf16[16,64,128]{2,1,0:T(8,128)(2,1)S(1)} %get-tuple-element.19), channel_id=1, replica_groups=mesh['dp'=16,'blk'=16] {'blk'}, dimensions={0} | all-to-all | bytes 524288 | tf_op jit(solution)/shard_map/all_to_all | solution.py:356
  38.9 1.3 %shard_map.130 = (bf16[128,512]{1,0:T(8,128)(2,1)S(1)}, bf16[16,320,128]{2,1,0:T(8,128)(2,1)S(1)}, f32[128,512]{1,0:T(8,128)S(1)}) custom-call(s32[8]{0:T(128)S(1)} %bitcast.17, s32[1]{0:T(128)} %bitcast.1.refs_1_.idx_ref, bf16[16,64,128]{2,1,0:T(8,128)(2,1)S(1)} %all_to_all.20.mixed_ref, bf16[128,512]{1,0:T(8,128)(2,1)S(1)} %bitcast.15, ...), custom_call_target="tpu_custom_call" | custom-call | flops 1100000000 | bytes 2621440 | tf_op jit(solution)/shard_map/pallas_call | solution.py:342
  40.2 23.2 %all_to_all.21.grads_ref.parts_ref = bf16[16,320,128]{2,1,0:T(8,128)(2,1)S(1)} all-to-all(bf16[16,320,128]{2,1,0:T(8,128)(2,1)S(1)} %get-tuple-element.23), channel_id=1, replica_groups=mesh['dp'=16,'blk'=16] {'blk'}, dimensions={0} | all-to-all | bytes 2621440 | tf_op jit(solution)/shard_map/all_to_all | solution.py:356
  63.4 0.1 shard_map.133.one_ref
  63.5 0.8 collective-permute-start
  64.4 6.2 %shard_map.132 = bf16[16,208,128]{2,1,0:T(8,128)(2,1)} custom-call(s32[8]{0:T(128)S(1)} %bitcast.18, s32[1]{0:T(128)} %bitcast.1.refs_1_.idx_ref, bf16[16,208,128]{2,1,0:T(8,128)(2,1)S(1)} %all-to-all-done.refs_2_.recv_ref, bf16[1024,128]{1,0:T(8,128)(2,1)S(1)} %get-tuple-element.21.phiq_ref, bf16[1024,128]{1,0:T(8,128)(2,1)S(1)} %get-tuple-element.22.phik_ref, ...), custom_call_target="tpu_custom_call" | custom-call | flops 6049999872 | bytes 3670016 | tf_op jit(solution)/shard_map/pallas_call | solution.py:342
  70.6 7.1 %all-to-all-start.3 = ((bf16[16,208,128]{2,1,0:T(8,128)(2,1)}), bf16[16,208,128]{2,1,0:T(8,128)(2,1)S(1)}, u32[]{:S(2)}, u32[]{:S(2)}) async-start(bf16[16,208,128]{2,1,0:T(8,128)(2,1)} %shard_map.132), calls=%async_computation.3 | async-start | bytes 1703936 | tf_op jit(solution)/shard_map/all_to_all | solution.py:356
  77.7 1.9 %collective-permute-start.1 = (bf16[256,128]{1,0:T(8,128)(2,1)S(1)}, bf16[256,128]{1,0:T(8,128)(2,1)S(1)}, u32[]{:S(2)}, u32[]{:S(2)}) collective-permute-start(bf16[256,128]{1,0:T(8,128)(2,1)S(1)} %shard_map.134.one_ref), channel_id=1, source_target_pairs={{0,16},{16,0},{32,48},{48,32},{64,80},{80,64},{96,112},{112,96},{1... | collective-permute-start | bytes 196616 | tf_op jit(solution)/shard_map/ppermute | solution.py:407
  79.6 2.4 %collective-permute-done.1.two_ref = bf16[256,128]{1,0:T(8,128)(2,1)S(1)} collective-permute-done((bf16[256,128]{1,0:T(8,128)(2,1)S(1)}, bf16[256,128]{1,0:T(8,128)(2,1)S(1)}, u32[]{:S(2)}, u32[]{:S(2)}) %collective-permute-start.1) | collective-permute-done | bytes 65568 | tf_op jit(solution)/shard_map/ppermute | solution.py:407
  82.1 3.3 %collective-permute-start.2 = (bf16[256,128]{1,0:T(8,128)(2,1)S(1)}, bf16[256,128]{1,0:T(8,128)(2,1)S(1)}, u32[]{:S(2)}, u32[]{:S(2)}) collective-permute-start(bf16[256,128]{1,0:T(8,128)(2,1)S(1)} %shard_map.135.one_ref), channel_id=1, source_target_pairs={{0,32},{16,48},{32,0},{48,16},{64,96},{80,112},{96,64},{112,80},{1... | collective-permute-start | bytes 196616 | tf_op jit(solution)/shard_map/ppermute | solution.py:407
  85.4 2.9 %collective-permute-done.2.two_ref = bf16[256,128]{1,0:T(8,128)(2,1)S(1)} collective-permute-done((bf16[256,128]{1,0:T(8,128)(2,1)S(1)}, bf16[256,128]{1,0:T(8,128)(2,1)S(1)}, u32[]{:S(2)}, u32[]{:S(2)}) %collective-permute-start.2) | collective-permute-done | bytes 65568 | tf_op jit(solution)/shard_map/ppermute | solution.py:407
  88.3 7.1 %collective-permute-start.3 = (bf16[256,128]{1,0:T(8,128)(2,1)S(1)}, bf16[256,128]{1,0:T(8,128)(2,1)S(1)}, u32[]{:S(2)}, u32[]{:S(2)}) collective-permute-start(bf16[256,128]{1,0:T(8,128)(2,1)S(1)} %shard_map.136.one_ref), channel_id=1, source_target_pairs={{0,64},{16,80},{32,96},{48,112},{64,0},{80,16},{96,32},{112,48},{1... | collective-permute-start | bytes 196616 | tf_op jit(solution)/shard_map/ppermute | solution.py:407
  95.3 1.0 %shard_map.131 = bf16[128,1024]{1,0:T(8,128)(2,1)} custom-call(bf16[128,512]{1,0:T(8,128)(2,1)S(1)} %get-tuple-element.20.hid_ref, bf16[512,1024]{1,0:T(8,128)(2,1)S(1)} %copy-done), custom_call_target="tpu_custom_call" | custom-call | flops 1100000000 | bytes 1441792 | tf_op jit(solution)/shard_map/pallas_call | solution.py:342
  96.4 1.2 %collective-permute-done.3.two_ref = bf16[256,128]{1,0:T(8,128)(2,1)S(1)} collective-permute-done((bf16[256,128]{1,0:T(8,128)(2,1)S(1)}, bf16[256,128]{1,0:T(8,128)(2,1)S(1)}, u32[]{:S(2)}, u32[]{:S(2)}) %collective-permute-start.3) | collective-permute-done | bytes 65568 | tf_op jit(solution)/shard_map/ppermute | solution.py:407
  97.6 0.9 shard_map.138
  (13 shorter events, 0.1 us)
Async XLA Ops:
  2.8 7.5 %copy-start.4 = (f32[4,128,64]{1,2,0:T(8,128)S(1)}, f32[4,128,64]{1,2,0:T(8,128)}, u32[]{:S(2)}) copy-start(f32[4,128,64]{1,2,0:T(8,128)} %param.12) | copy-start | bytes 393220
  2.8 7.6 %copy-start = (bf16[512,1024]{1,0:T(8,128)(2,1)S(1)}, bf16[512,1024]{1,0:T(8,128)(2,1)}, u32[]{:S(2)}) copy-start(bf16[512,1024]{1,0:T(8,128)(2,1)} %w_ref.3) | copy-start | bytes 3145732
  2.8 7.6 %copy-start.1 = (bf16[1,128,1024]{2,1,0:T(8,128)(2,1)S(1)}, bf16[1,128,1024]{2,1,0:T(8,128)(2,1)}, u32[]{:S(2)}) copy-start(bf16[1,128,1024]{2,1,0:T(8,128)(2,1)} %param.15) | copy-start | bytes 786436
  2.8 20.4 %all-to-all-start = ((bf16[16,208,128]{2,1,0:T(8,128)(2,1)}), bf16[16,208,128]{2,1,0:T(8,128)(2,1)S(1)}, u32[]{:S(2)}, u32[]{:S(2)}) async-start(bf16[16,208,128]{2,1,0:T(8,128)(2,1)} %shard_map.127), calls=%async_computation | async-start | bytes 1703936 | tf_op jit(solution)/shard_map/all_to_all | solution.py:356
  10.4 12.8 %copy-start.3 = (s32[1,8]{1,0:T(1,128)S(1)}, s32[1,8]{1,0:T(1,128)}, u32[]{:S(2)}) copy-start(s32[1,8]{1,0:T(1,128)} %param.14) | copy-start | bytes 100
  23.3 15.6 %copy-start.2 = (bf16[1,128,512]{2,1,0:T(8,128)(2,1)S(1)}, bf16[1,128,512]{2,1,0:T(8,128)(2,1)}, u32[]{:S(2)}) copy-start(bf16[1,128,512]{2,1,0:T(8,128)(2,1)} %param.11) | copy-start | bytes 393220
  63.5 7.0 %collective-permute-start = (bf16[256,128]{1,0:T(8,128)(2,1)S(1)}, bf16[256,128]{1,0:T(8,128)(2,1)S(1)}, u32[]{:S(2)}, u32[]{:S(2)}) collective-permute-start(bf16[256,128]{1,0:T(8,128)(2,1)S(1)} %shard_map.133.one_ref), channel_id=1, source_target_pairs={{0,128},{16,144},{32,160},{48,176},{64,192},{80,208},{96,224},{112... | collective-permute-start | bytes 196616 | tf_op jit(solution)/shard_map/ppermute | solution.py:407
  70.6 27.0 %all-to-all-start.3 = ((bf16[16,208,128]{2,1,0:T(8,128)(2,1)}), bf16[16,208,128]{2,1,0:T(8,128)(2,1)S(1)}, u32[]{:S(2)}, u32[]{:S(2)}) async-start(bf16[16,208,128]{2,1,0:T(8,128)(2,1)} %shard_map.132), calls=%async_computation.3 | async-start | bytes 1703936 | tf_op jit(solution)/shard_map/all_to_all | solution.py:356
  77.7 4.3 %collective-permute-start.1 = (bf16[256,128]{1,0:T(8,128)(2,1)S(1)}, bf16[256,128]{1,0:T(8,128)(2,1)S(1)}, u32[]{:S(2)}, u32[]{:S(2)}) collective-permute-start(bf16[256,128]{1,0:T(8,128)(2,1)S(1)} %shard_map.134.one_ref), channel_id=1, source_target_pairs={{0,16},{16,0},{32,48},{48,32},{64,80},{80,64},{96,112},{112,96},{1... | collective-permute-start | bytes 196616 | tf_op jit(solution)/shard_map/ppermute | solution.py:407
  82.1 6.2 %collective-permute-start.2 = (bf16[256,128]{1,0:T(8,128)(2,1)S(1)}, bf16[256,128]{1,0:T(8,128)(2,1)S(1)}, u32[]{:S(2)}, u32[]{:S(2)}) collective-permute-start(bf16[256,128]{1,0:T(8,128)(2,1)S(1)} %shard_map.135.one_ref), channel_id=1, source_target_pairs={{0,32},{16,48},{32,0},{48,16},{64,96},{80,112},{96,64},{112,80},{1... | collective-permute-start | bytes 196616 | tf_op jit(solution)/shard_map/ppermute | solution.py:407
  88.3 9.3 %collective-permute-start.3 = (bf16[256,128]{1,0:T(8,128)(2,1)S(1)}, bf16[256,128]{1,0:T(8,128)(2,1)S(1)}, u32[]{:S(2)}, u32[]{:S(2)}) collective-permute-start(bf16[256,128]{1,0:T(8,128)(2,1)S(1)} %shard_map.136.one_ref), channel_id=1, source_target_pairs={{0,64},{16,80},{32,96},{48,112},{64,0},{80,16},{96,32},{112,48},{1... | collective-permute-start | bytes 196616 | tf_op jit(solution)/shard_map/ppermute | solution.py:407

commit v4 on v3

--- a/solution.py
+++ b/solution.py
@@ -194,9 +194,7 @@
     gh_ref[...] = mm(cot_ref[...], w_ref[...], NT)
 
 
-def middle_kernel(
-    lens_ref, idx_ref, mixed_ref, u_ref, gh_ref, cot_ref, hid_ref, send_ref, ghn_ref
-):
+def norm_kernel(lens_ref, idx_ref, mixed_ref, u_ref, hid_ref, normed_ref, scales_ref):
     pos = idx_ref[0] * TOK + sublanes((TOK, HEAD))
     count = (pos - starts_of(lens_ref, pos) + 1).astype(F32)
     inverse = jnp.concatenate([1.0 / count] * HEADS, axis=1)
@@ -213,7 +211,15 @@
     rstd = lax.rsqrt(jnp.mean(centered * centered, axis=1, keepdims=True) + EPS)
     normed = centered * rstd
     hid_ref[...] = (normed * gates).astype(BF16)
-    grad_hidden = gh_ref[...]
+    normed_ref[...] = normed
+    scales_ref[:, :HEAD] = jnp.broadcast_to(rstd, (TOK, HEAD))
+    scales_ref[:, HEAD:] = inverse[:, :HEAD]
+
+
+def scale_kernel(u_ref, gh_ref, normed_ref, scales_ref, scaled_ref, ghn_ref):
+    gates, normed, grad_hidden = u_ref[...].astype(F32), normed_ref[...], gh_ref[...]
+    rstd = jnp.concatenate([scales_ref[:, :HEAD]] * HEADS, axis=1)
+    inverse = jnp.concatenate([scales_ref[:, HEAD:]] * HEADS, axis=1)
     ghn_ref[...] = grad_hidden * normed
     grad_normed = grad_hidden * gates
     grad_mixed = rstd * (
@@ -221,17 +227,28 @@
         - jnp.mean(grad_normed, axis=1, keepdims=True)
         - normed * jnp.mean(grad_normed * normed, axis=1, keepdims=True)
     )
-    scaled = (grad_mixed * inverse).astype(BF16)
+    scaled_ref[...] = (grad_mixed * inverse).astype(BF16)
+
+
+def weight_kernel(idx_ref, scaled_ref, hid_ref, hid2_ref, cot_ref, cot2_ref, send_ref):
     for h in range(HEADS):
         for gq in range(2):
             for gk in range(2):
-                send_ref[device(h, gq, gk), 0:SUB, :] = scaled[
+                send_ref[device(h, gq, gk), 0:SUB, :] = scaled_ref[
                     gq * SUB : (gq + 1) * SUB, h * HEAD : (h + 1) * HEAD
                 ]
-    for j in range(D // HEAD):
-        part = mm(hid_ref[...], cot_ref[:, j * HEAD : (j + 1) * HEAD], TN).astype(BF16)
-        for d in range(NBLK):
-            send_ref[d, SUB + j * 32 : SUB + (j + 1) * 32, :] = part[d * 32 : (d + 1) * 32]
+    hidden = jnp.concatenate([hid_ref[...], hid2_ref[...]], axis=0)
+    first = (idx_ref[0] % 2) * (D // 2)
+    for j in range(D // 2 // 256):
+        cols = pl.ds(pl.multiple_of(first + j * 256, 256), 256)
+        cots = jnp.concatenate([cot_ref[:, cols], cot2_ref[:, cols]], axis=0)
+        part = mm(hidden, cots, TN).astype(BF16)
+        for i in range(2):
+            top = SUB + (2 * j + i) * 32
+            for d in range(NBLK):
+                send_ref[d, top : top + 32, :] = part[
+                    d * 32 : (d + 1) * 32, i * HEAD : (i + 1) * HEAD
+                ]
 
 
 def out_kernel(hid_ref, w_ref, out_ref):
@@ -239,15 +256,19 @@
 
 
 def sum_kernel(parts_ref, gw_ref):
-    total = parts_ref[0, SUB:, :].astype(F32)
-    for d in range(1, NBLK):
-        total = total + parts_ref[d, SUB:, :].astype(F32)
-    gw_ref[...] = total.astype(BF16)
-
-
-def add_kernel(one_ref, two_ref, out_ref):
-    total = one_ref[...].astype(F32) + two_ref[...].astype(F32)
-    out_ref[...] = total.astype(out_ref.dtype)
+    for half in range(2):
+        total = parts_ref[half, SUB:, :].astype(F32)
+        for d in range(half + 2, NBLK, 2):
+            total = total + parts_ref[d, SUB:, :].astype(F32)
+        gw_ref[half * WROWS // 2 : (half + 1) * WROWS // 2, :] = total.astype(BF16)
+
+
+def add_kernel(*refs):
+    parts = [ref[...].astype(F32) for ref in refs[:-1]]
+    total = parts[0] + parts[1]
+    if len(parts) == 4:
+        total = total + (parts[2] + parts[3])
+    refs[-1][...] = total.astype(refs[-1].dtype)
 
 
 def backward_kernel(
@@ -356,6 +377,14 @@
     return lax.all_to_all(a, axis, 0, 0, tiled=True)
 
 
+def cross(x, mask):
+    return lax.ppermute(x, "dp", [(i, i ^ mask) for i in range(16)])
+
+
+def pair(x):
+    return lax.ppermute(x, "blk", [(i, i ^ 1) for i in range(NBLK)])
+
+
 def local(q, k, v, u, freqs, w, lens, cot):
     q, k, v, u, cot, lens = q[0], k[0], v[0], u[0], cot[0], lens[0]
     idx = lax.axis_index("blk").astype(jnp.int32)[None]
@@ -375,6 +404,7 @@
         mib=60,
     )
     recv1 = swap(send1, "blk")
+    cot2 = pair(cot)
     (gh,) = call(hidden_grad_kernel, [], [w, cot], [((TOK, WIDTH), F32)])
     mixed, phiq, phik = call(
         forward_kernel,
@@ -382,15 +412,28 @@
         [recv1, freqs],
         [((NBLK, SUB, HEAD), BF16), ((ROWS, HEAD), BF16), ((ROWS, HEAD), BF16)],
         staged + [((ROWS, HEAD), F32)],
-        after=[gh],
+        after=[gh, cot2],
         us=4.5,
     )
     recv2 = swap(mixed, "blk")
-    hidden, send3, ghn = call(
-        middle_kernel,
+    wide = ((TOK, WIDTH), F32)
+    hidden, normed, scales = call(
+        norm_kernel,
         [lens, idx],
-        [recv2, u, gh, cot],
-        [((TOK, WIDTH), BF16), ((NBLK, SUB + WROWS, HEAD), BF16), ((TOK, WIDTH), F32)],
+        [recv2, u],
+        [((TOK, WIDTH), BF16), wide, ((TOK, 2 * HEAD), F32)],
+        us=0.7,
+    )
+    hidden2 = pair(hidden)
+    scaled, ghn = call(
+        scale_kernel, [], [u, gh, normed, scales], [((TOK, WIDTH), BF16), wide], us=0.6
+    )
+    (send3,) = call(
+        weight_kernel,
+        [idx],
+        [scaled, hidden, hidden2, cot, cot2],
+        [((NBLK, SUB + WROWS // 2, HEAD), BF16)],
+        us=0.7,
     )
     recv3 = swap(send3, "blk")
     (gw,) = call(sum_kernel, [], [recv3], [((WROWS, HEAD), BF16)])
@@ -403,12 +446,11 @@
         staged + [((ROWS, HEAD), BF16), ((ROWS, 2 * HEAD), F32), ((ROWS, HEAD), F32)],
         us=5.5,
     )
-    for mask in (8, 1, 2, 4):
-        other = lax.ppermute(gw, "dp", [(i, i ^ mask) for i in range(16)])
-        kind = F32 if mask == 4 else BF16
-        (gw,) = call(add_kernel, [], [gw, other], [((WROWS, HEAD), kind)], us=0.5)
-        if mask == 8:
-            send4, gw = lax.optimization_barrier((send4, gw))
+    (gw,) = call(add_kernel, [], [gw, cross(gw, 8)], [((WROWS, HEAD), BF16)], us=0.5)
+    send4, gw = lax.optimization_barrier((send4, gw))
+    parts = [gw] + [cross(gw, mask) for mask in (1, 2, 3)]
+    (gw,) = call(add_kernel, [], parts, [((WROWS, HEAD), BF16)], us=0.5)
+    (gw,) = call(add_kernel, [], [gw, cross(gw, 4)], [((WROWS, HEAD), F32)], us=0.5)
     recv4 = swap(send4, "blk")
     dq, dk, dv, dg, dw = call(
         final_kernel,

time: 98.9 us -> 94.9 us (0.960)
  the two profiles are of different devices: /device:TPU:24 before, /device:TPU:1 now
where the time goes in v4:
time: 94.9 us; the launch traced here: 93.5 us
  blocking collectives  29.2 us (31%)
  starting transfers between devices  26 us (27%)
  waiting for transfers between devices  20.8 us (22%)
  Pallas kernels  15.9 us (17%)
    all_to_all x2, blocking collectives, swap(): return lax.all_to_all(a, axis, 0, 0, tiled=True)  29.2 us
    pallas_call x13, Pallas kernels, call(): pl.pallas_call(body, in_specs=[SMEM] * len(scalars) + [space] * len(array...  15.9 us
    all_to_all x2, waiting for transfers between devices, swap(): return lax.all_to_all(a, axis, 0, 0, tiled=True)  13.6 us
    all_to_all x2, starting transfers between devices, swap(): return lax.all_to_all(a, axis, 0, 0, tiled=True)  13.1 us
    ppermute x5, starting transfers between devices, cross(): return lax.ppermute(x, 'dp', [(i, i ^ mask) for i in range(16)])  11.8 us
    ppermute x5, waiting for transfers between devices, cross(): return lax.ppermute(x, 'dp', [(i, i ^ mask) for i in range(16)])  5.59 us
  transfers between devices with their start and end apart: 9, of which 6 were waited for; matrix products, arithmetic and copies ran while one was open for 0% of the time, Pallas kernels for 8%

profile of v4, /device:TPU:1, one launch (start us, length us, event | category | flops | bytes accessed | tf_op | source)
XLA Modules:
  0.0 93.5 jit_solution(6591525490513617384)
XLA Ops:
  0.6 2.1 %shard_map.127 = bf16[16,208,128]{2,1,0:T(8,128)(2,1)} custom-call(bf16[128,512]{1,0:T(8,128)(2,1)} %bitcast.21, bf16[128,512]{1,0:T(8,128)(2,1)} %bitcast.22, bf16[128,512]{1,0:T(8,128)(2,1)} %bitcast.23, bf16[128,512]{1,0:T(8,128)(2,1)} %bitcast.15), custom_call_target="tpu_custom_call" | custom-call | flops 1100000000 | bytes 1376256 | tf_op jit(solution)/shard_map/pallas_call | solution.py:363
  2.8 8.6 %all-to-all-start = ((bf16[16,208,128]{2,1,0:T(8,128)(2,1)}), bf16[16,208,128]{2,1,0:T(8,128)(2,1)S(1)}, u32[]{:S(2)}, u32[]{:S(2)}) async-start(bf16[16,208,128]{2,1,0:T(8,128)(2,1)} %shard_map.127), calls=%async_computation | async-start | bytes 1703936 | tf_op jit(solution)/shard_map/all_to_all | solution.py:377
  11.8 0.5 shard_map.128.refs_4_.gh_ref
  12.3 0.8 collective-permute-done.refs_5_.cot2_ref
  13.0 13.6 %all-to-all-done.refs_2_.recv_ref = bf16[16,208,128]{2,1,0:T(8,128)(2,1)S(1)} async-done(((bf16[16,208,128]{2,1,0:T(8,128)(2,1)}), bf16[16,208,128]{2,1,0:T(8,128)(2,1)S(1)}, u32[]{:S(2)}, u32[]{:S(2)}) %all-to-all-start) | async-done | bytes 852000 | tf_op jit(solution)/shard_map/all_to_all | solution.py:377
  26.7 0.7 copy-done.3
  27.3 3.7 %shard_map.129 = (bf16[16,64,128]{2,1,0:T(8,128)(2,1)S(1)}, bf16[1024,128]{1,0:T(8,128)(2,1)S(1)}, bf16[1024,128]{1,0:T(8,128)(2,1)S(1)}) custom-call(s32[8]{0:T(128)S(1)} %bitcast.18, s32[1]{0:T(128)} %bitcast.1.refs_1_.idx_ref, bf16[16,208,128]{2,1,0:T(8,128)(2,1)S(1)} %all-to-all-done.refs_2_.recv_ref, f32[4,128,64]{2,1,0:T(8,128)S(1)} %copy.14.refs_3_.freq_ref, ...), custom_call_target="tpu_custom_call" | custom-call | flops 4950000128 | bytes 1769472 | tf_op jit(solution)/shard_map/pallas_call | solution.py:363
  31.1 12.0 %all_to_all.20.mixed_ref = bf16[16,64,128]{2,1,0:T(8,128)(2,1)S(1)} all-to-all(bf16[16,64,128]{2,1,0:T(8,128)(2,1)S(1)} %get-tuple-element.21), channel_id=1, replica_groups=mesh['dp'=16,'blk'=16] {'blk'}, dimensions={0} | all-to-all | bytes 524288 | tf_op jit(solution)/shard_map/all_to_all | solution.py:377
  43.1 0.8 shard_map.130
  43.9 0.9 collective-permute-start.1
  44.9 0.8 collective-permute-done.1.hid2_ref
  45.8 0.3 shard_map.133
  46.1 17.1 %all_to_all.21.grads_ref.parts_ref = bf16[16,192,128]{2,1,0:T(8,128)(2,1)S(1)} all-to-all(bf16[16,192,128]{2,1,0:T(8,128)(2,1)S(1)} %shard_map.133), channel_id=1, replica_groups=mesh['dp'=16,'blk'=16] {'blk'}, dimensions={0} | all-to-all | bytes 1572864 | tf_op jit(solution)/shard_map/all_to_all | solution.py:377
  63.3 0.5 collective-permute-start.2
  63.8 6.2 %shard_map.134 = bf16[16,208,128]{2,1,0:T(8,128)(2,1)} custom-call(s32[8]{0:T(128)S(1)} %bitcast.20, s32[1]{0:T(128)} %bitcast.1.refs_1_.idx_ref, bf16[16,208,128]{2,1,0:T(8,128)(2,1)S(1)} %all-to-all-done.refs_2_.recv_ref, bf16[1024,128]{1,0:T(8,128)(2,1)S(1)} %get-tuple-element.23.phiq_ref, bf16[1024,128]{1,0:T(8,128)(2,1)S(1)} %get-tuple-element.24.phik_ref, ...), custom_call_target="tpu_custom_call" | custom-call | flops 6049999872 | bytes 3145728 | tf_op jit(solution)/shard_map/pallas_call | solution.py:363
  70.1 4.5 %all-to-all-start.3 = ((bf16[16,208,128]{2,1,0:T(8,128)(2,1)}), bf16[16,208,128]{2,1,0:T(8,128)(2,1)S(1)}, u32[]{:S(2)}, u32[]{:S(2)}) async-start(bf16[16,208,128]{2,1,0:T(8,128)(2,1)} %shard_map.134), calls=%async_computation.3 | async-start | bytes 1703936 | tf_op jit(solution)/shard_map/all_to_all | solution.py:377
  74.6 4.3 %collective-permute-start.5 = (bf16[256,128]{1,0:T(8,128)(2,1)S(1)}, bf16[256,128]{1,0:T(8,128)(2,1)S(1)}, u32[]{:S(2)}, u32[]{:S(2)}) collective-permute-start(bf16[256,128]{1,0:T(8,128)(2,1)S(1)} %shard_map.136.refs_0_), channel_id=1, source_target_pairs={{0,48},{16,32},{32,16},{48,0},{64,112},{80,96},{96,80},{112,64},{1... | collective-permute-start | bytes 196616 | tf_op jit(solution)/shard_map/ppermute | solution.py:381
  78.9 0.4 collective-permute-start.3
  79.3 1.8 %collective-permute-done.5.refs_3_ = bf16[256,128]{1,0:T(8,128)(2,1)S(1)} collective-permute-done((bf16[256,128]{1,0:T(8,128)(2,1)S(1)}, bf16[256,128]{1,0:T(8,128)(2,1)S(1)}, u32[]{:S(2)}, u32[]{:S(2)}) %collective-permute-start.5) | collective-permute-done | bytes 65568 | tf_op jit(solution)/shard_map/ppermute | solution.py:381
  81.2 2.7 %collective-permute-done.4.refs_2_ = bf16[256,128]{1,0:T(8,128)(2,1)S(1)} collective-permute-done((bf16[256,128]{1,0:T(8,128)(2,1)S(1)}, bf16[256,128]{1,0:T(8,128)(2,1)S(1)}, u32[]{:S(2)}, u32[]{:S(2)}) %collective-permute-start.4) | collective-permute-done | bytes 65568 | tf_op jit(solution)/shard_map/ppermute | solution.py:381
  83.9 6.5 %collective-permute-start.6 = (bf16[256,128]{1,0:T(8,128)(2,1)S(1)}, bf16[256,128]{1,0:T(8,128)(2,1)S(1)}, u32[]{:S(2)}, u32[]{:S(2)}) collective-permute-start(bf16[256,128]{1,0:T(8,128)(2,1)S(1)} %shard_map.137.refs_0_), channel_id=1, source_target_pairs={{0,64},{16,80},{32,96},{48,112},{64,0},{80,16},{96,32},{112,48},{1... | collective-permute-start | bytes 196616 | tf_op jit(solution)/shard_map/ppermute | solution.py:381
  90.5 1.0 %shard_map.131 = bf16[128,1024]{1,0:T(8,128)(2,1)} custom-call(bf16[128,512]{1,0:T(8,128)(2,1)S(1)} %get-tuple-element.22.hid_ref, bf16[512,1024]{1,0:T(8,128)(2,1)S(1)} %copy-done), custom_call_target="tpu_custom_call" | custom-call | flops 1100000000 | bytes 1441792 | tf_op jit(solution)/shard_map/pallas_call | solution.py:363
  91.5 1.0 %collective-permute-done.6.refs_1_ = bf16[256,128]{1,0:T(8,128)(2,1)S(1)} collective-permute-done((bf16[256,128]{1,0:T(8,128)(2,1)S(1)}, bf16[256,128]{1,0:T(8,128)(2,1)S(1)}, u32[]{:S(2)}, u32[]{:S(2)}) %collective-permute-start.6) | collective-permute-done | bytes 65568 | tf_op jit(solution)/shard_map/ppermute | solution.py:381
  92.5 0.9 %shard_map.139 = (bf16[128,512]{1,0:T(8,128)(2,1)}, bf16[128,512]{1,0:T(8,128)(2,1)}, bf16[128,512]{1,0:T(8,128)(2,1)}, bf16[128,512]{1,0:T(8,128)(2,1)}, f32[32,1024]{1,0:T(8,128)}) custom-call(bf16[16,208,128]{2,1,0:T(8,128)(2,1)S(1)} %all-to-all-done.3.recv_ref, f32[128,512]{1,0:T(8,128)S(1)} %get-tuple-element.29.ghn_ref, f32[256,128]{1,0:T(8,128)S(1)} %shard_map.138.gw_ref), custom_call_target="tpu_custom_call" | custom-call | flops 1100000000 | bytes 1900544 | tf_op jit(solution)/shard_map/pallas_call | solution.py:363
  (20 shorter events, 0.7 us)
Async XLA Ops:
  2.8 8.6 %copy-start.1 = (bf16[1,128,1024]{2,1,0:T(8,128)(2,1)S(1)}, bf16[1,128,1024]{2,1,0:T(8,128)(2,1)}, u32[]{:S(2)}) copy-start(bf16[1,128,1024]{2,1,0:T(8,128)(2,1)} %param.15) | copy-start | bytes 786436
  2.8 8.8 %copy-start.4 = (f32[4,128,64]{1,2,0:T(8,128)S(1)}, f32[4,128,64]{1,2,0:T(8,128)}, u32[]{:S(2)}) copy-start(f32[4,128,64]{1,2,0:T(8,128)} %param.12) | copy-start | bytes 393220
  2.8 8.9 %copy-start = (bf16[512,1024]{1,0:T(8,128)(2,1)S(1)}, bf16[512,1024]{1,0:T(8,128)(2,1)}, u32[]{:S(2)}) copy-start(bf16[512,1024]{1,0:T(8,128)(2,1)} %w_ref.3) | copy-start | bytes 3145732
  2.8 23.8 %all-to-all-start = ((bf16[16,208,128]{2,1,0:T(8,128)(2,1)}), bf16[16,208,128]{2,1,0:T(8,128)(2,1)S(1)}, u32[]{:S(2)}, u32[]{:S(2)}) async-start(bf16[16,208,128]{2,1,0:T(8,128)(2,1)} %shard_map.127), calls=%async_computation | async-start | bytes 1703936 | tf_op jit(solution)/shard_map/all_to_all | solution.py:377
  11.4 1.6 %collective-permute-start = (bf16[128,1024]{1,0:T(8,128)(2,1)S(1)}, bf16[128,1024]{1,0:T(8,128)(2,1)S(1)}, u32[]{:S(2)}, u32[]{:S(2)}) collective-permute-start(bf16[128,1024]{1,0:T(8,128)(2,1)S(1)} %bitcast.12), channel_id=1, source_target_pairs={{0,1},{1,0},{2,3},{3,2},{4,5},{5,4},{6,7},{7,6},{8,9},{9,8},{10,11... | collective-permute-start | bytes 786440 | tf_op jit(solution)/shard_map/ppermute | solution.py:385
  26.7 0.7 copy-start.3
  31.0 12.0 %copy-start.2 = (bf16[1,128,512]{2,1,0:T(8,128)(2,1)S(1)}, bf16[1,128,512]{2,1,0:T(8,128)(2,1)}, u32[]{:S(2)}) copy-start(bf16[1,128,512]{2,1,0:T(8,128)(2,1)} %param.11) | copy-start | bytes 393220
  43.9 1.9 %collective-permute-start.1 = (bf16[128,512]{1,0:T(8,128)(2,1)S(1)}, bf16[128,512]{1,0:T(8,128)(2,1)S(1)}, u32[]{:S(2)}, u32[]{:S(2)}) collective-permute-start(bf16[128,512]{1,0:T(8,128)(2,1)S(1)} %get-tuple-element.22.hid_ref), channel_id=1, source_target_pairs={{0,1},{1,0},{2,3},{3,2},{4,5},{5,4},{6,7},{7,6},{8,9},{9,8},{10,11... | collective-permute-start | bytes 393224 | tf_op jit(solution)/shard_map/ppermute | solution.py:385
  63.3 6.7 %collective-permute-start.2 = (bf16[256,128]{1,0:T(8,128)(2,1)S(1)}, bf16[256,128]{1,0:T(8,128)(2,1)S(1)}, u32[]{:S(2)}, u32[]{:S(2)}) collective-permute-start(bf16[256,128]{1,0:T(8,128)(2,1)S(1)} %shard_map.135.refs_0_), channel_id=1, source_target_pairs={{0,128},{16,144},{32,160},{48,176},{64,192},{80,208},{96,224},{112... | collective-permute-start | bytes 196616 | tf_op jit(solution)/shard_map/ppermute | solution.py:381
  70.1 22.5 %all-to-all-start.3 = ((bf16[16,208,128]{2,1,0:T(8,128)(2,1)}), bf16[16,208,128]{2,1,0:T(8,128)(2,1)S(1)}, u32[]{:S(2)}, u32[]{:S(2)}) async-start(bf16[16,208,128]{2,1,0:T(8,128)(2,1)} %shard_map.134), calls=%async_computation.3 | async-start | bytes 1703936 | tf_op jit(solution)/shard_map/all_to_all | solution.py:377
  74.6 6.6 %collective-permute-start.5 = (bf16[256,128]{1,0:T(8,128)(2,1)S(1)}, bf16[256,128]{1,0:T(8,128)(2,1)S(1)}, u32[]{:S(2)}, u32[]{:S(2)}) collective-permute-start(bf16[256,128]{1,0:T(8,128)(2,1)S(1)} %shard_map.136.refs_0_), channel_id=1, source_target_pairs={{0,48},{16,32},{32,16},{48,0},{64,112},{80,96},{96,80},{112,64},{1... | collective-permute-start | bytes 196616 | tf_op jit(solution)/shard_map/ppermute | solution.py:381
  78.9 4.9 %collective-permute-start.4 = (bf16[256,128]{1,0:T(8,128)(2,1)S(1)}, bf16[256,128]{1,0:T(8,128)(2,1)S(1)}, u32[]{:S(2)}, u32[]{:S(2)}) collective-permute-start(bf16[256,128]{1,0:T(8,128)(2,1)S(1)} %shard_map.136.refs_0_), channel_id=1, source_target_pairs={{0,32},{16,48},{32,0},{48,16},{64,96},{80,112},{96,64},{112,80},{1... | collective-permute-start | bytes 196616 | tf_op jit(solution)/shard_map/ppermute | solution.py:381
  78.9 4.9 %collective-permute-start.3 = (bf16[256,128]{1,0:T(8,128)(2,1)S(1)}, bf16[256,128]{1,0:T(8,128)(2,1)S(1)}, u32[]{:S(2)}, u32[]{:S(2)}) collective-permute-start(bf16[256,128]{1,0:T(8,128)(2,1)S(1)} %shard_map.136.refs_0_), channel_id=1, source_target_pairs={{0,16},{16,0},{32,48},{48,32},{64,80},{80,64},{96,112},{112,96},{1... | collective-permute-start | bytes 196616 | tf_op jit(solution)/shard_map/ppermute | solution.py:381
  83.9 8.6 %collective-permute-start.6 = (bf16[256,128]{1,0:T(8,128)(2,1)S(1)}, bf16[256,128]{1,0:T(8,128)(2,1)S(1)}, u32[]{:S(2)}, u32[]{:S(2)}) collective-permute-start(bf16[256,128]{1,0:T(8,128)(2,1)S(1)} %shard_map.137.refs_0_), channel_id=1, source_target_pairs={{0,64},{16,80},{32,96},{48,112},{64,0},{80,16},{96,32},{112,48},{1... | collective-permute-start | bytes 196616 | tf_op jit(solution)/shard_map/ppermute | solution.py:381

commit v5 on v4

--- a/solution.py
+++ b/solution.py
@@ -16,6 +16,7 @@
 TILE = 2 * SUB
 REACH = 5
 TILES = ROWS // TILE
+EARLY = 3
 SCALE = 1.0 / math.sqrt(HEAD)
 F32, BF16 = jnp.float32, jnp.bfloat16
 
@@ -52,7 +53,7 @@
     end = jnp.int32(0)
     start = jnp.zeros_like(pos)
     for u in range(USERS):
-        end = end + lens_ref[u]
+        end = end + lens_ref[0, u]
         start = jnp.where(pos >= end, end, start)
     return start
 
@@ -97,18 +98,15 @@
                 out_ref[d, V0:PACK, :] = v_ref[gk * SUB : (gk + 1) * SUB, cols]
 
 
-def stage_rows(recv_ref, lens_ref, gq, qp_s, gate_s, start_s, pos_s):
+def stage_rows(recv_ref, lens_ref, gq, gate_s, start_s):
     pos = sublanes((NBLK, TOK)) * TOK + lanes((NBLK, TOK))
     starts = starts_of(lens_ref, pos).astype(F32)
-    first = (sublanes((SUB, HEAD)) + gq * SUB).astype(F32)
     mine = lanes((SUB, TOK)) == sublanes((SUB, TOK)) + gq * SUB
     for b in range(NBLK):
         rows = slice(b * SUB, (b + 1) * SUB)
-        qp_s[rows, :HEAD] = recv_ref[b, Q0:G0, :]
         parts = recv_ref[b, G0:K0, :].astype(F32)
         gate_s[rows, :] = jnp.broadcast_to(column(parts[0:1] + parts[8:9], mine), (SUB, HEAD))
         start_s[rows, :] = jnp.broadcast_to(column(starts[b : b + 1], mine), (SUB, HEAD))
-        pos_s[rows, :] = first + float(b * TOK)
 
 
 def tile_of(recv_ref, c, first, last):
@@ -124,11 +122,13 @@
     )
 
 
-def masker(start_s, pos_s, rows, c, gk):
+def masker(start_s, rows, c, gq, gk):
     lane = lanes((1, TILE))
     key = ((2 * c + (lane >> 6)) * TOK + gk * SUB + (lane & (SUB - 1))).astype(F32)
+    row = sublanes((TILE, TILE))
+    pos = ((2 * c + (row >> 6)) * TOK + gq * SUB + (row & (SUB - 1))).astype(F32)
     top = slice(rows.start, rows.start + TILE)
-    near = (key >= start_s[top, :]) & (key <= pos_s[top, :])
+    near = (key >= start_s[top, :]) & (key <= pos)
     if rows.stop == top.stop:
         return lambda x: jnp.where(near, x, 0.0)
     far = key >= start_s[top.stop : rows.stop, :]
@@ -150,11 +150,12 @@
 
 
 def forward_kernel(
-    lens_ref, idx_ref, recv_ref, freq_ref, mixed_ref, phiq_ref, phik_ref,
-    qp_s, gate_s, start_s, pos_s, acc_s,
+    idx_ref, recv_ref, freq_ref, lens_hbm, mixed_ref, phik_ref, qp_ref, gate_ref, start_ref,
+    acc_s, lens_s, sem,
 ):
+    copy = pltpu.make_async_copy(lens_hbm, lens_s, sem)
+    copy.start()
     head, gq, gk = place(idx_ref)
-    stage_rows(recv_ref, lens_ref, gq, qp_s, gate_s, start_s, pos_s)
     freq = freq_ref[head]
     freq = jnp.concatenate([freq, freq], axis=1)
     pieces = []
@@ -169,11 +170,13 @@
         angles = (a[:, 2 * HEAD :] + a[:, HEAD : 2 * HEAD]) + a[:, :HEAD]
         return (cos_sin(angles) / math.sqrt(FREQS)).astype(BF16)
 
+    for b in range(NBLK):
+        qp_ref[b * SUB : (b + 1) * SUB, :HEAD] = recv_ref[b, Q0:G0, :]
     for i in range(4):
         rows = slice(i * ROWS // 4, (i + 1) * ROWS // 4)
-        phiq = phi_of(qp_s[rows, :HEAD])
-        phiq_ref[rows, :] = phiq
-        qp_s[rows, HEAD:] = phiq
+        qp_ref[rows, HEAD:] = phi_of(qp_ref[rows, :HEAD])
+    copy.wait()
+    stage_rows(recv_ref, lens_s, gq, gate_ref, start_ref)
     acc_s[...] = jnp.zeros_like(acc_s)
     for c in range(TILES):
         rows = tile_rows(c)
@@ -181,10 +184,10 @@
         values = tile_of(recv_ref, c, V0, PACK)
         phik = phi_of(keys)
         phik_ref[c * TILE : (c + 1) * TILE, :] = phik
-        both = mm(qp_s[rows, :], diagonal(keys, phik), NT)
+        both = mm(qp_ref[rows, :], diagonal(keys, phik), NT)
         half, kern = both[:, :TILE] * (0.5 * SCALE), both[:, TILE:]
-        both = half + half * jnp.tanh(half) + gate_s[rows, :] * kern
-        both = masker(start_s, pos_s, rows, c, gk)(both).astype(BF16)
+        both = half + half * jnp.tanh(half) + gate_ref[rows, :] * kern
+        both = masker(start_ref, rows, c, gq, gk)(both).astype(BF16)
         acc_s[rows, :] += mm(both, values, NN)
     for b in range(NBLK):
         mixed_ref[b] = acc_s[b * SUB : (b + 1) * SUB, :].astype(BF16)
@@ -271,33 +274,27 @@
     refs[-1][...] = total.astype(refs[-1].dtype)
 
 
-def backward_kernel(
-    lens_ref, idx_ref, recv_ref, phiq_ref, phik_ref, grads_ref, freq_ref, send_ref,
-    qp_s, gate_s, start_s, pos_s, sc_s, dqp_s, term_s,
+def backward_tiles(
+    tiles, idx_ref, recv_ref, phik_ref, qp_ref, gate_ref, start_ref, sc_ref, freq_ref, out_ref, top,
+    dqp_ref, term_ref,
 ):
     head, gq, gk = place(idx_ref)
-    stage_rows(recv_ref, lens_ref, gq, qp_s, gate_s, start_s, pos_s)
-    qp_s[:, HEAD:] = phiq_ref[...]
-    for b in range(NBLK):
-        sc_s[b * SUB : (b + 1) * SUB, :] = grads_ref[b, 0:SUB, :]
     freq = freq_ref[head].astype(BF16)
     freq = jnp.concatenate([freq, -freq], axis=1)
-    dqp_s[...] = jnp.zeros_like(dqp_s)
-    term_s[...] = jnp.zeros_like(term_s)
-
-    def back(phi, grad_phi):
+
+    def feature_back(phi, grad_phi):
         turned = pltpu.roll(grad_phi, FREQS, 1)
         return mm((phi.astype(F32) * turned).astype(BF16), freq, NT)
 
-    for c in range(TILES):
+    for c in tiles:
         rows = tile_rows(c)
         keys = tile_of(recv_ref, c, K0, V0)
         values = tile_of(recv_ref, c, V0, PACK)
         phik = phik_ref[c * TILE : (c + 1) * TILE, :]
         pairs = diagonal(keys, phik)
-        scaled, gate = sc_s[rows, :], gate_s[rows, :]
-        masked = masker(start_s, pos_s, rows, c, gk)
-        both = mm(qp_s[rows, :], pairs, NT)
+        scaled, gate = sc_ref[rows, :], gate_ref[rows, :]
+        masked = masker(start_ref, rows, c, gq, gk)
+        both = mm(qp_ref[rows, :], pairs, NT)
         half, kern = both[:, :TILE] * (0.5 * SCALE), both[:, TILE:]
         t = jnp.tanh(half)
         weights = half + half * t
@@ -306,16 +303,46 @@
         both = masked(weights + gate * kern).astype(BF16)
         grad_s = (grad_w * slope * (0.5 * SCALE)).astype(BF16)
         grad_k = (grad_w * gate).astype(BF16)
-        term_s[rows, :] += kern * grad_w
-        dqp_s[rows, :] += mm(jnp.concatenate([grad_s, grad_k], axis=1), pairs, NN)
-        dkey = mm(grad_s, qp_s[rows, :HEAD], TN)
-        dkey = dkey + back(phik, mm(grad_k, qp_s[rows, HEAD:], TN))
+        term_ref[rows, :] += kern * grad_w
+        dqp_ref[rows, :] += mm(jnp.concatenate([grad_s, grad_k], axis=1), pairs, NN)
+        dkey = mm(grad_s, qp_ref[rows, :HEAD], TN)
+        dkey = dkey + feature_back(phik, mm(grad_k, qp_ref[rows, HEAD:], TN))
         dval = mm(both, scaled, TN)
         for i in range(2):
-            send_ref[2 * c + i, K0:V0, :] = dkey[i * SUB : (i + 1) * SUB].astype(BF16)
-            send_ref[2 * c + i, V0:PACK, :] = dval[i * SUB : (i + 1) * SUB].astype(BF16)
-    dq = dqp_s[:, :HEAD] + back(phiq_ref[...], dqp_s[:, HEAD:])
-    gate = gate_s[...]
+            half = slice(i * SUB, (i + 1) * SUB)
+            out_ref[2 * c + i, top : top + SUB, :] = dkey[half].astype(BF16)
+            out_ref[2 * c + i, top + SUB : top + 2 * SUB, :] = dval[half].astype(BF16)
+    return feature_back
+
+
+def first_backward_kernel(
+    idx_ref, recv_ref, phik_ref, qp_ref, gate_ref, start_ref, grads_ref, freq_ref,
+    dkv_ref, sc_ref, dqp_ref, term_ref,
+):
+    for b in range(NBLK):
+        sc_ref[b * SUB : (b + 1) * SUB, :] = grads_ref[b, 0:SUB, :]
+    dqp_ref[...] = jnp.zeros_like(dqp_ref)
+    term_ref[...] = jnp.zeros_like(term_ref)
+    backward_tiles(
+        range(EARLY), idx_ref, recv_ref, phik_ref, qp_ref, gate_ref, start_ref, sc_ref, freq_ref,
+        dkv_ref, 0, dqp_ref, term_ref,
+    )
+
+
+def second_backward_kernel(
+    idx_ref, recv_ref, phik_ref, qp_ref, gate_ref, start_ref, sc_ref, dkv_ref, dqp1_ref, term1_ref,
+    freq_ref, send_ref, dqp_s, term_s,
+):
+    dqp_s[...] = dqp1_ref[...]
+    term_s[...] = term1_ref[...]
+    feature_back = backward_tiles(
+        range(EARLY, TILES), idx_ref, recv_ref, phik_ref, qp_ref, gate_ref, start_ref, sc_ref,
+        freq_ref, send_ref, K0, dqp_s, term_s,
+    )
+    for b in range(2 * EARLY):
+        send_ref[b, K0:PACK, :] = dkv_ref[b]
+    dq = dqp_s[:, :HEAD] + feature_back(qp_ref[:, HEAD:], dqp_s[:, HEAD:])
+    gate = gate_ref[...]
     term = jnp.sum(term_s[...], axis=1, keepdims=True) * gate * (1.0 - gate) * SCALE
     mine = lanes((SUB, HEAD)) == sublanes((SUB, HEAD))
     for b in range(NBLK):
@@ -351,7 +378,7 @@
 ANY = pl.BlockSpec(memory_space=pl.ANY)
 
 
-def call(body, scalars, arrays, outs, scratch=(), us=1.0, space=VMEM, mib=16, after=()):
+def call(body, scalars, arrays, outs, scratch=(), us=1.0, space=VMEM, to=VMEM, mib=16, after=(), spaces=None):
     if after:
         inner, first = body, len(scalars) + len(arrays)
 
@@ -362,8 +389,10 @@
     moved += sum(math.prod(s) * jnp.dtype(t).itemsize for s, t in outs)
     return pl.pallas_call(
         body,
-        in_specs=[SMEM] * len(scalars) + [space] * len(arrays) + [ANY] * len(after),
-        out_specs=[VMEM] * len(outs),
+        in_specs=[SMEM] * len(scalars)
+        + (spaces or [space] * len(arrays))
+        + [ANY] * len(after),
+        out_specs=[to] * len(outs),
         out_shape=[jax.ShapeDtypeStruct(s, t) for s, t in outs],
         scratch_shapes=[pltpu.VMEM(*s) if isinstance(s, tuple) else s for s in scratch],
         compiler_params=pltpu.CompilerParams(vmem_limit_bytes=mib * 1024 * 1024),
@@ -386,14 +415,9 @@
 
 
 def local(q, k, v, u, freqs, w, lens, cot):
-    q, k, v, u, cot, lens = q[0], k[0], v[0], u[0], cot[0], lens[0]
+    q, k, v, u, cot, lens = q[0], k[0], v[0], u[0], cot[0], lens
     idx = lax.axis_index("blk").astype(jnp.int32)[None]
-    staged = [
-        ((ROWS, 2 * HEAD), BF16),
-        ((ROWS, HEAD), F32),
-        ((ROWS, HEAD), F32),
-        ((ROWS, HEAD), F32),
-    ]
+    rows, tall = (ROWS, HEAD), (ROWS, 2 * HEAD)
     (send1,) = call(
         pack_kernel,
         [],
@@ -406,14 +430,15 @@
     recv1 = swap(send1, "blk")
     cot2 = pair(cot)
     (gh,) = call(hidden_grad_kernel, [], [w, cot], [((TOK, WIDTH), F32)])
-    mixed, phiq, phik = call(
+    mixed, phik, qp, gate, start = call(
         forward_kernel,
-        [lens, idx],
-        [recv1, freqs],
-        [((NBLK, SUB, HEAD), BF16), ((ROWS, HEAD), BF16), ((ROWS, HEAD), BF16)],
-        staged + [((ROWS, HEAD), F32)],
+        [idx],
+        [recv1, freqs, lens],
+        [((NBLK, SUB, HEAD), BF16), (rows, BF16), (tall, BF16), (rows, F32), (rows, F32)],
+        [(rows, F32), pltpu.SMEM((1, USERS), jnp.int32), pltpu.SemaphoreType.DMA(())],
+        spaces=[VMEM, VMEM, ANY],
         after=[gh, cot2],
-        us=4.5,
+        us=3.5,
     )
     recv2 = swap(mixed, "blk")
     wide = ((TOK, WIDTH), F32)
@@ -438,19 +463,32 @@
     recv3 = swap(send3, "blk")
     (gw,) = call(sum_kernel, [], [recv3], [((WROWS, HEAD), BF16)])
     (layer_out,) = call(out_kernel, [], [hidden, w], [((TOK, D), BF16)])
+    shared = [recv1, phik, qp, gate, start]
+    dkv, scaled, dqp, term = call(
+        first_backward_kernel,
+        [idx],
+        shared + [recv3, freqs],
+        [((2 * EARLY, 2 * SUB, HEAD), BF16), (rows, BF16), (tall, F32), (rows, F32)],
+        us=3.0,
+    )
+    (gw,) = call(
+        add_kernel, [], [gw, cross(gw, 8)], [((WROWS, HEAD), BF16)], us=0.5, after=[dkv]
+    )
     (send4,) = call(
-        backward_kernel,
-        [lens, idx],
-        [recv1, phiq, phik, recv3, freqs],
+        second_backward_kernel,
+        [idx],
+        shared + [scaled, dkv, dqp, term, freqs],
         [((NBLK, PACK, HEAD), BF16)],
-        staged + [((ROWS, HEAD), BF16), ((ROWS, 2 * HEAD), F32), ((ROWS, HEAD), F32)],
-        us=5.5,
-    )
-    (gw,) = call(add_kernel, [], [gw, cross(gw, 8)], [((WROWS, HEAD), BF16)], us=0.5)
+        [(tall, F32), (rows, F32)],
+        us=3.0,
+        after=[gw],
+    )
+    (gw,) = call(
+        add_kernel, [], [gw, cross(gw, 1)], [((WROWS, HEAD), BF16)], us=0.5, after=[send4]
+    )
     send4, gw = lax.optimization_barrier((send4, gw))
-    parts = [gw] + [cross(gw, mask) for mask in (1, 2, 3)]
-    (gw,) = call(add_kernel, [], parts, [((WROWS, HEAD), BF16)], us=0.5)
-    (gw,) = call(add_kernel, [], [gw, cross(gw, 4)], [((WROWS, HEAD), F32)], us=0.5)
+    parts = [gw] + [cross(gw, mask) for mask in (2, 4, 6)]
+    (gw,) = call(add_kernel, [], parts, [((WROWS, HEAD), F32)], us=0.5)
     recv4 = swap(send4, "blk")
     dq, dk, dv, dg, dw = call(
         final_kernel,

time: 94.9 us -> 93.2 us (0.982); the launches traced: 93.5 us -> 92.8 us
  waiting for transfers between devices: 20.8 us -> 22.8 us
  starting transfers between devices: 26 us -> 24.8 us
    all_to_all x2, waiting for transfers between devices: 13.6 us -> 16.3 us  [swap(): return lax.all_to_all(a, axis, 0, 0, tiled=True)]
    ppermute x5, starting transfers between devices: 11.8 us -> 9.41 us  [cross(): return lax.ppermute(x, 'dp', [(i, i ^ mask) for i in range(16)])]
    all_to_all x2, starting transfers between devices: 13.1 us -> 14.3 us  [swap(): return lax.all_to_all(a, axis, 0, 0, tiled=True)]
    pallas_call x13 -> x14, Pallas kernels: 15.9 us -> 15.2 us  [call(): pl.pallas_call(body, in_specs=[SMEM] * len(scalars) + (spaces or [space]...]
  transfers between devices with their start and end apart: 9 -> 9, of which waited for: 6 -> 7; matrix products, arithmetic and copies ran while one was open for 0% -> 0% of each run, Pallas kernels for 8% -> 8%
where the time goes in v5:
time: 93.2 us; the launch traced here: 92.8 us
  blocking collectives  29.2 us (31%)
  starting transfers between devices  24.8 us (27%)
  waiting for transfers between devices  22.8 us (24%)
  Pallas kernels  15.2 us (16%)
    all_to_all x2, blocking collectives, swap(): return lax.all_to_all(a, axis, 0, 0, tiled=True)  29.2 us
    all_to_all x2, waiting for transfers between devices, swap(): return lax.all_to_all(a, axis, 0, 0, tiled=True)  16.3 us
    pallas_call x14, Pallas kernels, call(): pl.pallas_call(body, in_specs=[SMEM] * len(scalars) + (spaces or [space]...  15.2 us
    all_to_all x2, starting transfers between devices, swap(): return lax.all_to_all(a, axis, 0, 0, tiled=True)  14.3 us
    ppermute x5, starting transfers between devices, cross(): return lax.ppermute(x, 'dp', [(i, i ^ mask) for i in range(16)])  9.41 us
    ppermute x5, waiting for transfers between devices, cross(): return lax.ppermute(x, 'dp', [(i, i ^ mask) for i in range(16)])  4.89 us
  transfers between devices with their start and end apart: 9, of which 7 were waited for; matrix products, arithmetic and copies ran while one was open for 0% of the time, Pallas kernels for 8%

profile of v5, /device:TPU:1, one launch (start us, length us, event | category | flops | bytes accessed | tf_op | source)
XLA Modules:
  0.0 92.8 jit_solution(4196852276070262119)
XLA Ops:
  0.6 2.1 %shard_map.127 = bf16[16,208,128]{2,1,0:T(8,128)(2,1)} custom-call(bf16[128,512]{1,0:T(8,128)(2,1)} %bitcast.17, bf16[128,512]{1,0:T(8,128)(2,1)} %bitcast.18, bf16[128,512]{1,0:T(8,128)(2,1)} %bitcast.19, bf16[128,512]{1,0:T(8,128)(2,1)} %bitcast.14), custom_call_target="tpu_custom_call" | custom-call | flops 1100000000 | bytes 1376256 | tf_op jit(solution)/shard_map/pallas_call | solution.py:390
  2.8 8.6 %all-to-all-start = ((bf16[16,208,128]{2,1,0:T(8,128)(2,1)}), bf16[16,208,128]{2,1,0:T(8,128)(2,1)S(1)}, u32[]{:S(2)}, u32[]{:S(2)}) async-start(bf16[16,208,128]{2,1,0:T(8,128)(2,1)} %shard_map.127), calls=%async_computation | async-start | bytes 1703936 | tf_op jit(solution)/shard_map/all_to_all | solution.py:406
  11.8 0.5 shard_map.128.refs_4_.gh_ref
  12.3 0.8 collective-permute-done.refs_5_.cot2_ref
  13.0 13.6 %all-to-all-done.refs_1_.recv_ref = bf16[16,208,128]{2,1,0:T(8,128)(2,1)S(1)} async-done(((bf16[16,208,128]{2,1,0:T(8,128)(2,1)}), bf16[16,208,128]{2,1,0:T(8,128)(2,1)S(1)}, u32[]{:S(2)}, u32[]{:S(2)}) %all-to-all-start) | async-done | bytes 852000 | tf_op jit(solution)/shard_map/all_to_all | solution.py:406
  26.7 3.4 %shard_map.129 = (bf16[16,64,128]{2,1,0:T(8,128)(2,1)S(1)}, bf16[1024,128]{1,0:T(8,128)(2,1)S(1)}, bf16[1024,256]{1,0:T(8,128)(2,1)S(1)}, f32[1024,128]{1,0:T(8,128)S(1)}, f32[1024,128]{1,0:T(8,128)S(1)}) custom-call(s32[1]{0:T(128)} %bitcast.refs_0_.idx_ref, bf16[16,208,128]{2,1,0:T(8,128)(2,1)S(1)} %all-to-all-done.refs_1_.recv_ref, ...), custom_call_target="tpu_custom_call" | custom-call | flops 3849999872 | bytes 3080224 | tf_op jit(solution)/shard_map/pallas_call | solution.py:390
  30.1 12.0 %all_to_all.20.mixed_ref = bf16[16,64,128]{2,1,0:T(8,128)(2,1)S(1)} all-to-all(bf16[16,64,128]{2,1,0:T(8,128)(2,1)S(1)} %get-tuple-element.27), channel_id=1, replica_groups=mesh['dp'=16,'blk'=16] {'blk'}, dimensions={0} | all-to-all | bytes 524288 | tf_op jit(solution)/shard_map/all_to_all | solution.py:406
  42.1 0.8 shard_map.130
  42.9 0.9 collective-permute-start.1
  44.0 0.8 collective-permute-done.1.hid2_ref
  45.1 17.1 %all_to_all.21.grads_ref.parts_ref = bf16[16,192,128]{2,1,0:T(8,128)(2,1)S(1)} all-to-all(bf16[16,192,128]{2,1,0:T(8,128)(2,1)S(1)} %shard_map.133), channel_id=1, replica_groups=mesh['dp'=16,'blk'=16] {'blk'}, dimensions={0} | all-to-all | bytes 1572864 | tf_op jit(solution)/shard_map/all_to_all | solution.py:406
  62.3 0.5 collective-permute-start.2
  62.8 2.3 %shard_map.134 = (bf16[6,128,128]{2,1,0:T(8,128)(2,1)S(1)}, bf16[1024,128]{1,0:T(8,128)(2,1)S(1)}, f32[1024,256]{1,0:T(8,128)S(1)}, f32[1024,128]{1,0:T(8,128)S(1)}) custom-call(s32[1]{0:T(128)} %bitcast.refs_0_.idx_ref, bf16[16,208,128]{2,1,0:T(8,128)(2,1)S(1)} %all-to-all-done.refs_1_.recv_ref, bf16[1024,128]{1,0:T(8,128)(2,1)S(1)} %get-tuple-element.29.phik_ref.refs_2_, ...), custom_call_target="tpu_custom_call" | custom-call | flops 3300000000 | bytes 5636096 | tf_op jit(solution)/shard_map/pallas_call | solution.py:390
  65.1 0.4 collective-permute-done.2.refs_1_
  65.6 1.7 %collective-permute-start.3 = (bf16[256,128]{1,0:T(8,128)(2,1)S(1)}, bf16[256,128]{1,0:T(8,128)(2,1)S(1)}, u32[]{:S(2)}, u32[]{:S(2)}) collective-permute-start(bf16[256,128]{1,0:T(8,128)(2,1)S(1)} %shard_map.136.refs_11_.refs_0_), channel_id=1, source_target_pairs={{0,16},{16,0},{32,48},{48,32},{64,80},{80,64},{96,112},{112,96},{1... | collective-permute-start | bytes 196616 | tf_op jit(solution)/shard_map/ppermute | solution.py:410
  67.3 3.5 %shard_map.137.refs_2_ = bf16[16,208,128]{2,1,0:T(8,128)(2,1)} custom-call(s32[1]{0:T(128)} %bitcast.refs_0_.idx_ref, bf16[16,208,128]{2,1,0:T(8,128)(2,1)S(1)} %all-to-all-done.refs_1_.recv_ref, bf16[1024,128]{1,0:T(8,128)(2,1)S(1)} %get-tuple-element.29.phik_ref.refs_2_, bf16[1024,256]{1,0:T(8,128)(2,1)S(1)} %get-tuple-element.30.qp_ref.refs_3_, ...), custom_call_target="tpu_custom_call" | custom-call | flops 3300000000 | bytes 5701632 | tf_op jit(solution)/shard_map/pallas_call | solution.py:390
  70.9 5.7 %all-to-all-start.3 = ((bf16[16,208,128]{2,1,0:T(8,128)(2,1)}), bf16[16,208,128]{2,1,0:T(8,128)(2,1)S(1)}, u32[]{:S(2)}, u32[]{:S(2)}) async-start(bf16[16,208,128]{2,1,0:T(8,128)(2,1)} %shard_map.137.refs_2_), calls=%async_computation.3 | async-start | bytes 1703936 | tf_op jit(solution)/shard_map/all_to_all | solution.py:406
  76.5 3.0 %collective-permute-start.4 = (bf16[256,128]{1,0:T(8,128)(2,1)S(1)}, bf16[256,128]{1,0:T(8,128)(2,1)S(1)}, u32[]{:S(2)}, u32[]{:S(2)}) collective-permute-start(bf16[256,128]{1,0:T(8,128)(2,1)S(1)} %shard_map.138.refs_0_), channel_id=1, source_target_pairs={{0,32},{16,48},{32,0},{48,16},{64,96},{80,112},{96,64},{112,80},{1... | collective-permute-start | bytes 196616 | tf_op jit(solution)/shard_map/ppermute | solution.py:410
  79.5 4.2 %collective-permute-start.5 = (bf16[256,128]{1,0:T(8,128)(2,1)S(1)}, bf16[256,128]{1,0:T(8,128)(2,1)S(1)}, u32[]{:S(2)}, u32[]{:S(2)}) collective-permute-start(bf16[256,128]{1,0:T(8,128)(2,1)S(1)} %shard_map.138.refs_0_), channel_id=1, source_target_pairs={{0,64},{16,80},{32,96},{48,112},{64,0},{80,16},{96,32},{112,48},{1... | collective-permute-start | bytes 196616 | tf_op jit(solution)/shard_map/ppermute | solution.py:410
  83.7 1.0 %shard_map.131 = bf16[128,1024]{1,0:T(8,128)(2,1)} custom-call(bf16[128,512]{1,0:T(8,128)(2,1)S(1)} %get-tuple-element.28.hid_ref, bf16[512,1024]{1,0:T(8,128)(2,1)S(1)} %copy-done), custom_call_target="tpu_custom_call" | custom-call | flops 1100000000 | bytes 1441792 | tf_op jit(solution)/shard_map/pallas_call | solution.py:390
  84.8 2.4 %collective-permute-done.5.refs_2_ = bf16[256,128]{1,0:T(8,128)(2,1)S(1)} collective-permute-done((bf16[256,128]{1,0:T(8,128)(2,1)S(1)}, bf16[256,128]{1,0:T(8,128)(2,1)S(1)}, u32[]{:S(2)}, u32[]{:S(2)}) %collective-permute-start.5) | collective-permute-done | bytes 65568 | tf_op jit(solution)/shard_map/ppermute | solution.py:410
  87.1 2.1 %collective-permute-done.6.refs_3_ = bf16[256,128]{1,0:T(8,128)(2,1)S(1)} collective-permute-done((bf16[256,128]{1,0:T(8,128)(2,1)S(1)}, bf16[256,128]{1,0:T(8,128)(2,1)S(1)}, u32[]{:S(2)}, u32[]{:S(2)}) %collective-permute-start.6) | collective-permute-done | bytes 65568 | tf_op jit(solution)/shard_map/ppermute | solution.py:410
  89.2 2.6 %all-to-all-done.3.recv_ref = bf16[16,208,128]{2,1,0:T(8,128)(2,1)S(1)} async-done(((bf16[16,208,128]{2,1,0:T(8,128)(2,1)}), bf16[16,208,128]{2,1,0:T(8,128)(2,1)S(1)}, u32[]{:S(2)}, u32[]{:S(2)}) %all-to-all-start.3) | async-done | bytes 852000 | tf_op jit(solution)/shard_map/all_to_all | solution.py:406
  91.9 0.9 %shard_map.140 = (bf16[128,512]{1,0:T(8,128)(2,1)}, bf16[128,512]{1,0:T(8,128)(2,1)}, bf16[128,512]{1,0:T(8,128)(2,1)}, bf16[128,512]{1,0:T(8,128)(2,1)}, f32[32,1024]{1,0:T(8,128)}) custom-call(bf16[16,208,128]{2,1,0:T(8,128)(2,1)S(1)} %all-to-all-done.3.recv_ref, f32[128,512]{1,0:T(8,128)S(1)} %get-tuple-element.41.ghn_ref, f32[256,128]{1,0:T(8,128)S(1)} %shard_map.139.gw_ref), custom_call_target="tpu_custom_call" | custom-call | flops 1100000000 | bytes 1900544 | tf_op jit(solution)/shard_map/pallas_call | solution.py:390
  (21 shorter events, 1.0 us)
Async XLA Ops:
  2.8 8.6 %copy-start.1 = (bf16[1,128,1024]{2,1,0:T(8,128)(2,1)S(1)}, bf16[1,128,1024]{2,1,0:T(8,128)(2,1)}, u32[]{:S(2)}) copy-start(bf16[1,128,1024]{2,1,0:T(8,128)(2,1)} %param.15) | copy-start | bytes 786436
  2.8 8.8 %copy-start.4 = (f32[4,128,64]{1,2,0:T(8,128)S(1)}, f32[4,128,64]{1,2,0:T(8,128)}, u32[]{:S(2)}) copy-start(f32[4,128,64]{1,2,0:T(8,128)} %param.12) | copy-start | bytes 393220
  2.8 8.9 %copy-start = (bf16[512,1024]{1,0:T(8,128)(2,1)S(1)}, bf16[512,1024]{1,0:T(8,128)(2,1)}, u32[]{:S(2)}) copy-start(bf16[512,1024]{1,0:T(8,128)(2,1)} %w_ref.3) | copy-start | bytes 3145732
  2.8 23.8 %all-to-all-start = ((bf16[16,208,128]{2,1,0:T(8,128)(2,1)}), bf16[16,208,128]{2,1,0:T(8,128)(2,1)S(1)}, u32[]{:S(2)}, u32[]{:S(2)}) async-start(bf16[16,208,128]{2,1,0:T(8,128)(2,1)} %shard_map.127), calls=%async_computation | async-start | bytes 1703936 | tf_op jit(solution)/shard_map/all_to_all | solution.py:406
  11.4 1.6 %collective-permute-start = (bf16[128,1024]{1,0:T(8,128)(2,1)S(1)}, bf16[128,1024]{1,0:T(8,128)(2,1)S(1)}, u32[]{:S(2)}, u32[]{:S(2)}) collective-permute-start(bf16[128,1024]{1,0:T(8,128)(2,1)S(1)} %bitcast.11), channel_id=1, source_target_pairs={{0,1},{1,0},{2,3},{3,2},{4,5},{5,4},{6,7},{7,6},{8,9},{9,8},{10,11... | collective-permute-start | bytes 786440 | tf_op jit(solution)/shard_map/ppermute | solution.py:414
  12.2 14.4 %copy-start.3 = (s32[1,8]{1,0:T(1,128)S(1)}, s32[1,8]{1,0:T(1,128)}, u32[]{:S(2)}) copy-start(s32[1,8]{1,0:T(1,128)} %lens_ref.1) | copy-start | bytes 100
  30.1 12.0 %copy-start.2 = (bf16[1,128,512]{2,1,0:T(8,128)(2,1)S(1)}, bf16[1,128,512]{2,1,0:T(8,128)(2,1)}, u32[]{:S(2)}) copy-start(bf16[1,128,512]{2,1,0:T(8,128)(2,1)} %param.11) | copy-start | bytes 393220
  42.9 1.9 %collective-permute-start.1 = (bf16[128,512]{1,0:T(8,128)(2,1)S(1)}, bf16[128,512]{1,0:T(8,128)(2,1)S(1)}, u32[]{:S(2)}, u32[]{:S(2)}) collective-permute-start(bf16[128,512]{1,0:T(8,128)(2,1)S(1)} %get-tuple-element.28.hid_ref), channel_id=1, source_target_pairs={{0,1},{1,0},{2,3},{3,2},{4,5},{5,4},{6,7},{7,6},{8,9},{9,8},{10,11... | collective-permute-start | bytes 393224 | tf_op jit(solution)/shard_map/ppermute | solution.py:414
  62.3 3.2 %collective-permute-start.2 = (bf16[256,128]{1,0:T(8,128)(2,1)S(1)}, bf16[256,128]{1,0:T(8,128)(2,1)S(1)}, u32[]{:S(2)}, u32[]{:S(2)}) collective-permute-start(bf16[256,128]{1,0:T(8,128)(2,1)S(1)} %shard_map.135.refs_0_), channel_id=1, source_target_pairs={{0,128},{16,144},{32,160},{48,176},{64,192},{80,208},{96,224},{112... | collective-permute-start | bytes 196616 | tf_op jit(solution)/shard_map/ppermute | solution.py:410
  65.6 5.3 %collective-permute-start.3 = (bf16[256,128]{1,0:T(8,128)(2,1)S(1)}, bf16[256,128]{1,0:T(8,128)(2,1)S(1)}, u32[]{:S(2)}, u32[]{:S(2)}) collective-permute-start(bf16[256,128]{1,0:T(8,128)(2,1)S(1)} %shard_map.136.refs_11_.refs_0_), channel_id=1, source_target_pairs={{0,16},{16,0},{32,48},{48,32},{64,80},{80,64},{96,112},{112,96},{1... | collective-permute-start | bytes 196616 | tf_op jit(solution)/shard_map/ppermute | solution.py:410
  70.9 21.0 %all-to-all-start.3 = ((bf16[16,208,128]{2,1,0:T(8,128)(2,1)}), bf16[16,208,128]{2,1,0:T(8,128)(2,1)S(1)}, u32[]{:S(2)}, u32[]{:S(2)}) async-start(bf16[16,208,128]{2,1,0:T(8,128)(2,1)} %shard_map.137.refs_2_), calls=%async_computation.3 | async-start | bytes 1703936 | tf_op jit(solution)/shard_map/all_to_all | solution.py:406
  76.5 8.2 %collective-permute-start.4 = (bf16[256,128]{1,0:T(8,128)(2,1)S(1)}, bf16[256,128]{1,0:T(8,128)(2,1)S(1)}, u32[]{:S(2)}, u32[]{:S(2)}) collective-permute-start(bf16[256,128]{1,0:T(8,128)(2,1)S(1)} %shard_map.138.refs_0_), channel_id=1, source_target_pairs={{0,32},{16,48},{32,0},{48,16},{64,96},{80,112},{96,64},{112,80},{1... | collective-permute-start | bytes 196616 | tf_op jit(solution)/shard_map/ppermute | solution.py:410
  79.5 7.6 %collective-permute-start.5 = (bf16[256,128]{1,0:T(8,128)(2,1)S(1)}, bf16[256,128]{1,0:T(8,128)(2,1)S(1)}, u32[]{:S(2)}, u32[]{:S(2)}) collective-permute-start(bf16[256,128]{1,0:T(8,128)(2,1)S(1)} %shard_map.138.refs_0_), channel_id=1, source_target_pairs={{0,64},{16,80},{32,96},{48,112},{64,0},{80,16},{96,32},{112,48},{1... | collective-permute-start | bytes 196616 | tf_op jit(solution)/shard_map/ppermute | solution.py:410
  83.7 5.5 %collective-permute-start.6 = (bf16[256,128]{1,0:T(8,128)(2,1)S(1)}, bf16[256,128]{1,0:T(8,128)(2,1)S(1)}, u32[]{:S(2)}, u32[]{:S(2)}) collective-permute-start(bf16[256,128]{1,0:T(8,128)(2,1)S(1)} %shard_map.138.refs_0_), channel_id=1, source_target_pairs={{0,96},{16,112},{32,64},{48,80},{64,32},{80,48},{96,0},{112,16},{1... | collective-permute-start | bytes 196616 | tf_op jit(solution)/shard_map/ppermute | solution.py:410

commit v6 on v5

--- a/solution.py
+++ b/solution.py
@@ -13,10 +13,11 @@
 SUB = TOK // 2
 WIDTH, D = HEADS * HEAD, 1024
 ROWS = SUB * NBLK
-TILE = 2 * SUB
-REACH = 5
+SPAN = 4
+TILE = SPAN * SUB
+REACH = 3
 TILES = ROWS // TILE
-EARLY = 3
+EARLY = 2
 SCALE = 1.0 / math.sqrt(HEAD)
 F32, BF16 = jnp.float32, jnp.bfloat16
 
@@ -63,13 +64,14 @@
     r = angles - turns * 1.5703125
     r = r - turns * 4.837512969970703125e-4
     r = r - turns * 7.54978995489188e-8
-    quad = turns.astype(jnp.int32) - jnp.where(lanes(angles.shape) >= FREQS, 1, 0)
+    quad = turns.astype(jnp.int32)
     z = r * r
     c = 1.0 - 0.5 * z + z * z * (4.166664568e-2 + z * (-1.388731625e-3 + z * 2.443315712e-5))
     s = r + r * z * (-1.6666654611e-1 + z * (8.3321608736e-3 - z * 1.9515295891e-4))
     odd = (quad & 1) == 1
-    value = jnp.where(odd, s, c)
-    return jnp.where(((quad + 1) & 2) == 2, -value, value)
+    cos, sin = jnp.where(odd, s, c), jnp.where(odd, c, s)
+    cos = jnp.where(((quad + 1) & 2) == 2, -cos, cos)
+    return cos, jnp.where((quad & 2) == 2, -sin, sin)
 
 
 def pack_kernel(q_hbm, k_hbm, v_hbm, u_hbm, out_ref, q_ref, k_ref, v_ref, u_ref, sems):
@@ -111,8 +113,12 @@
 
 def tile_of(recv_ref, c, first, last):
     return jnp.concatenate(
-        [recv_ref[2 * c, first:last, :], recv_ref[2 * c + 1, first:last, :]], axis=0
-    )
+        [recv_ref[SPAN * c + i, first:last, :] for i in range(SPAN)], axis=0
+    )
+
+
+def twice(a):
+    return jnp.concatenate([a, a], axis=1)
 
 
 def diagonal(a, b):
@@ -124,14 +130,14 @@
 
 def masker(start_s, rows, c, gq, gk):
     lane = lanes((1, TILE))
-    key = ((2 * c + (lane >> 6)) * TOK + gk * SUB + (lane & (SUB - 1))).astype(F32)
+    key = ((SPAN * c + (lane >> 6)) * TOK + gk * SUB + (lane & (SUB - 1))).astype(F32)
     row = sublanes((TILE, TILE))
-    pos = ((2 * c + (row >> 6)) * TOK + gq * SUB + (row & (SUB - 1))).astype(F32)
+    pos = ((SPAN * c + (row >> 6)) * TOK + gq * SUB + (row & (SUB - 1))).astype(F32)
     top = slice(rows.start, rows.start + TILE)
-    near = (key >= start_s[top, :]) & (key <= pos)
+    near = (key >= twice(start_s[top, :])) & (key <= pos)
     if rows.stop == top.stop:
         return lambda x: jnp.where(near, x, 0.0)
-    far = key >= start_s[top.stop : rows.stop, :]
+    far = key >= twice(start_s[top.stop : rows.stop, :])
 
     def masked(x):
         return jnp.concatenate(
@@ -157,18 +163,21 @@
     copy.start()
     head, gq, gk = place(idx_ref)
     freq = freq_ref[head]
-    freq = jnp.concatenate([freq, freq], axis=1)
     pieces = []
     for _ in range(3):
         piece = freq.astype(BF16)
-        pieces.append(piece)
+        pieces.append(diagonal(piece, piece))
         freq = freq - piece.astype(F32)
-    pieces = jnp.concatenate(pieces, axis=1)
 
     def phi_of(x):
-        a = mm(x, pieces, NN)
-        angles = (a[:, 2 * HEAD :] + a[:, HEAD : 2 * HEAD]) + a[:, :HEAD]
-        return (cos_sin(angles) / math.sqrt(FREQS)).astype(BF16)
+        n = x.shape[0] // 2
+        x = jnp.concatenate([x[:n], x[n:]], axis=1)
+        angles = (mm(x, pieces[2], NN) + mm(x, pieces[1], NN)) + mm(x, pieces[0], NN)
+        cos, sin = cos_sin(angles)
+        left = lanes((n, HEAD)) < FREQS
+        first = jnp.where(left, cos, pltpu.roll(sin, FREQS, 1))
+        second = jnp.where(left, pltpu.roll(cos, FREQS, 1), sin)
+        return (jnp.concatenate([first, second], axis=0) / math.sqrt(FREQS)).astype(BF16)
 
     for b in range(NBLK):
         qp_ref[b * SUB : (b + 1) * SUB, :HEAD] = recv_ref[b, Q0:G0, :]
@@ -186,7 +195,7 @@
         phik_ref[c * TILE : (c + 1) * TILE, :] = phik
         both = mm(qp_ref[rows, :], diagonal(keys, phik), NT)
         half, kern = both[:, :TILE] * (0.5 * SCALE), both[:, TILE:]
-        both = half + half * jnp.tanh(half) + gate_ref[rows, :] * kern
+        both = half + half * jnp.tanh(half) + twice(gate_ref[rows, :]) * kern
         both = masker(start_ref, rows, c, gq, gk)(both).astype(BF16)
         acc_s[rows, :] += mm(both, values, NN)
     for b in range(NBLK):
@@ -292,7 +301,7 @@
         values = tile_of(recv_ref, c, V0, PACK)
         phik = phik_ref[c * TILE : (c + 1) * TILE, :]
         pairs = diagonal(keys, phik)
-        scaled, gate = sc_ref[rows, :], gate_ref[rows, :]
+        scaled, gate = sc_ref[rows, :], twice(gate_ref[rows, :])
         masked = masker(start_ref, rows, c, gq, gk)
         both = mm(qp_ref[rows, :], pairs, NT)
         half, kern = both[:, :TILE] * (0.5 * SCALE), both[:, TILE:]
@@ -303,15 +312,16 @@
         both = masked(weights + gate * kern).astype(BF16)
         grad_s = (grad_w * slope * (0.5 * SCALE)).astype(BF16)
         grad_k = (grad_w * gate).astype(BF16)
-        term_ref[rows, :] += kern * grad_w
+        term = kern * grad_w
+        term_ref[rows, :] += term[:, :HEAD] + term[:, HEAD:]
         dqp_ref[rows, :] += mm(jnp.concatenate([grad_s, grad_k], axis=1), pairs, NN)
         dkey = mm(grad_s, qp_ref[rows, :HEAD], TN)
         dkey = dkey + feature_back(phik, mm(grad_k, qp_ref[rows, HEAD:], TN))
         dval = mm(both, scaled, TN)
-        for i in range(2):
-            half = slice(i * SUB, (i + 1) * SUB)
-            out_ref[2 * c + i, top : top + SUB, :] = dkey[half].astype(BF16)
-            out_ref[2 * c + i, top + SUB : top + 2 * SUB, :] = dval[half].astype(BF16)
+        for i in range(SPAN):
+            part, b = slice(i * SUB, (i + 1) * SUB), SPAN * c + i
+            out_ref[b, top : top + SUB, :] = dkey[part].astype(BF16)
+            out_ref[b, top + SUB : top + 2 * SUB, :] = dval[part].astype(BF16)
     return feature_back
 
 
@@ -339,7 +349,7 @@
         range(EARLY, TILES), idx_ref, recv_ref, phik_ref, qp_ref, gate_ref, start_ref, sc_ref,
         freq_ref, send_ref, K0, dqp_s, term_s,
     )
-    for b in range(2 * EARLY):
+    for b in range(SPAN * EARLY):
         send_ref[b, K0:PACK, :] = dkv_ref[b]
     dq = dqp_s[:, :HEAD] + feature_back(qp_ref[:, HEAD:], dqp_s[:, HEAD:])
     gate = gate_ref[...]
@@ -468,7 +478,7 @@
         first_backward_kernel,
         [idx],
         shared + [recv3, freqs],
-        [((2 * EARLY, 2 * SUB, HEAD), BF16), (rows, BF16), (tall, F32), (rows, F32)],
+        [((SPAN * EARLY, 2 * SUB, HEAD), BF16), (rows, BF16), (tall, F32), (rows, F32)],
         us=3.0,
     )
     (gw,) = call(

time: 93.2 us -> 92 us (0.987)
  waiting for transfers between devices: 22.8 us -> 21.8 us
  transfers between devices with their start and end apart: 9 -> 9, of which waited for: 7 -> 6; matrix products, arithmetic and copies ran while one was open for 0% -> 0% of each run, Pallas kernels for 8% -> 8%
where the time goes in v6:
time: 92 us; the launch traced here: 91.6 us
  blocking collectives  29.2 us (32%)
  starting transfers between devices  25.1 us (27%)
  waiting for transfers between devices  21.8 us (24%)
  Pallas kernels  14.6 us (16%)
    all_to_all x2, blocking collectives, swap(): return lax.all_to_all(a, axis, 0, 0, tiled=True)  29.2 us
    all_to_all x2, waiting for transfers between devices, swap(): return lax.all_to_all(a, axis, 0, 0, tiled=True)  15.7 us
    pallas_call x14, Pallas kernels, call(): pl.pallas_call(body, in_specs=[SMEM] * len(scalars) + (spaces or [space]...  14.6 us
    all_to_all x2, starting transfers between devices, swap(): return lax.all_to_all(a, axis, 0, 0, tiled=True)  14.1 us
    ppermute x5, starting transfers between devices, cross(): return lax.ppermute(x, 'dp', [(i, i ^ mask) for i in range(16)])  9.92 us
    ppermute x5, waiting for transfers between devices, cross(): return lax.ppermute(x, 'dp', [(i, i ^ mask) for i in range(16)])  4.47 us
  transfers between devices with their start and end apart: 9, of which 6 were waited for; matrix products, arithmetic and copies ran while one was open for 0% of the time, Pallas kernels for 8%

profile of v6, /device:TPU:1, one launch (start us, length us, event | category | flops | bytes accessed | tf_op | source)
XLA Modules:
  0.0 91.6 jit_solution(11744684949612011708)
XLA Ops:
  0.6 2.1 %shard_map.127 = bf16[16,208,128]{2,1,0:T(8,128)(2,1)} custom-call(bf16[128,512]{1,0:T(8,128)(2,1)} %bitcast.17, bf16[128,512]{1,0:T(8,128)(2,1)} %bitcast.18, bf16[128,512]{1,0:T(8,128)(2,1)} %bitcast.19, bf16[128,512]{1,0:T(8,128)(2,1)} %bitcast.14), custom_call_target="tpu_custom_call" | custom-call | flops 1100000000 | bytes 1376256 | tf_op jit(solution)/shard_map/pallas_call | solution.py:400
  2.8 8.6 %all-to-all-start = ((bf16[16,208,128]{2,1,0:T(8,128)(2,1)}), bf16[16,208,128]{2,1,0:T(8,128)(2,1)S(1)}, u32[]{:S(2)}, u32[]{:S(2)}) async-start(bf16[16,208,128]{2,1,0:T(8,128)(2,1)} %shard_map.127), calls=%async_computation | async-start | bytes 1703936 | tf_op jit(solution)/shard_map/all_to_all | solution.py:416
  11.8 0.5 shard_map.128.refs_4_.gh_ref
  12.3 0.8 collective-permute-done.refs_5_.cot2_ref
  13.0 13.6 %all-to-all-done.refs_1_.recv_ref = bf16[16,208,128]{2,1,0:T(8,128)(2,1)S(1)} async-done(((bf16[16,208,128]{2,1,0:T(8,128)(2,1)}), bf16[16,208,128]{2,1,0:T(8,128)(2,1)S(1)}, u32[]{:S(2)}, u32[]{:S(2)}) %all-to-all-start) | async-done | bytes 852000 | tf_op jit(solution)/shard_map/all_to_all | solution.py:416
  26.7 3.0 %shard_map.129 = (bf16[16,64,128]{2,1,0:T(8,128)(2,1)S(1)}, bf16[1024,128]{1,0:T(8,128)(2,1)S(1)}, bf16[1024,256]{1,0:T(8,128)(2,1)S(1)}, f32[1024,128]{1,0:T(8,128)S(1)}, f32[1024,128]{1,0:T(8,128)S(1)}) custom-call(s32[1]{0:T(128)} %bitcast.refs_0_.idx_ref, bf16[16,208,128]{2,1,0:T(8,128)(2,1)S(1)} %all-to-all-done.refs_1_.recv_ref, ...), custom_call_target="tpu_custom_call" | custom-call | flops 3849999872 | bytes 3080224 | tf_op jit(solution)/shard_map/pallas_call | solution.py:400
  29.7 12.0 %all_to_all.20.mixed_ref = bf16[16,64,128]{2,1,0:T(8,128)(2,1)S(1)} all-to-all(bf16[16,64,128]{2,1,0:T(8,128)(2,1)S(1)} %get-tuple-element.27), channel_id=1, replica_groups=mesh['dp'=16,'blk'=16] {'blk'}, dimensions={0} | all-to-all | bytes 524288 | tf_op jit(solution)/shard_map/all_to_all | solution.py:416
  41.7 0.8 shard_map.130
  42.5 0.9 collective-permute-start.1
  43.6 0.8 collective-permute-done.1.hid2_ref
  44.4 0.3 shard_map.133
  44.7 17.1 %all_to_all.21.grads_ref.parts_ref = bf16[16,192,128]{2,1,0:T(8,128)(2,1)S(1)} all-to-all(bf16[16,192,128]{2,1,0:T(8,128)(2,1)S(1)} %shard_map.133), channel_id=1, replica_groups=mesh['dp'=16,'blk'=16] {'blk'}, dimensions={0} | all-to-all | bytes 1572864 | tf_op jit(solution)/shard_map/all_to_all | solution.py:416
  61.9 0.5 collective-permute-start.2
  62.4 2.9 %shard_map.134 = (bf16[8,128,128]{2,1,0:T(8,128)(2,1)S(1)}, bf16[1024,128]{1,0:T(8,128)(2,1)S(1)}, f32[1024,256]{1,0:T(8,128)S(1)}, f32[1024,128]{1,0:T(8,128)S(1)}) custom-call(s32[1]{0:T(128)} %bitcast.refs_0_.idx_ref, bf16[16,208,128]{2,1,0:T(8,128)(2,1)S(1)} %all-to-all-done.refs_1_.recv_ref, bf16[1024,128]{1,0:T(8,128)(2,1)S(1)} %get-tuple-element.29.phik_ref.refs_2_, ...), custom_call_target="tpu_custom_call" | custom-call | flops 3300000000 | bytes 5701632 | tf_op jit(solution)/shard_map/pallas_call | solution.py:400
  65.3 1.7 %collective-permute-start.3 = (bf16[256,128]{1,0:T(8,128)(2,1)S(1)}, bf16[256,128]{1,0:T(8,128)(2,1)S(1)}, u32[]{:S(2)}, u32[]{:S(2)}) collective-permute-start(bf16[256,128]{1,0:T(8,128)(2,1)S(1)} %shard_map.136.refs_11_.refs_0_), channel_id=1, source_target_pairs={{0,16},{16,0},{32,48},{48,32},{64,80},{80,64},{96,112},{112,96},{1... | collective-permute-start | bytes 196616 | tf_op jit(solution)/shard_map/ppermute | solution.py:420
  67.1 2.7 %shard_map.137.refs_2_ = bf16[16,208,128]{2,1,0:T(8,128)(2,1)} custom-call(s32[1]{0:T(128)} %bitcast.refs_0_.idx_ref, bf16[16,208,128]{2,1,0:T(8,128)(2,1)S(1)} %all-to-all-done.refs_1_.recv_ref, bf16[1024,128]{1,0:T(8,128)(2,1)S(1)} %get-tuple-element.29.phik_ref.refs_2_, bf16[1024,256]{1,0:T(8,128)(2,1)S(1)} %get-tuple-element.30.qp_ref.refs_3_, ...), custom_call_target="tpu_custom_call" | custom-call | flops 3300000000 | bytes 5767168 | tf_op jit(solution)/shard_map/pallas_call | solution.py:400
  69.8 5.5 %all-to-all-start.3 = ((bf16[16,208,128]{2,1,0:T(8,128)(2,1)}), bf16[16,208,128]{2,1,0:T(8,128)(2,1)S(1)}, u32[]{:S(2)}, u32[]{:S(2)}) async-start(bf16[16,208,128]{2,1,0:T(8,128)(2,1)} %shard_map.137.refs_2_), calls=%async_computation.3 | async-start | bytes 1703936 | tf_op jit(solution)/shard_map/all_to_all | solution.py:416
  75.3 3.0 %collective-permute-start.4 = (bf16[256,128]{1,0:T(8,128)(2,1)S(1)}, bf16[256,128]{1,0:T(8,128)(2,1)S(1)}, u32[]{:S(2)}, u32[]{:S(2)}) collective-permute-start(bf16[256,128]{1,0:T(8,128)(2,1)S(1)} %shard_map.138.refs_0_), channel_id=1, source_target_pairs={{0,32},{16,48},{32,0},{48,16},{64,96},{80,112},{96,64},{112,80},{1... | collective-permute-start | bytes 196616 | tf_op jit(solution)/shard_map/ppermute | solution.py:420
  78.3 4.7 %collective-permute-start.5 = (bf16[256,128]{1,0:T(8,128)(2,1)S(1)}, bf16[256,128]{1,0:T(8,128)(2,1)S(1)}, u32[]{:S(2)}, u32[]{:S(2)}) collective-permute-start(bf16[256,128]{1,0:T(8,128)(2,1)S(1)} %shard_map.138.refs_0_), channel_id=1, source_target_pairs={{0,64},{16,80},{32,96},{48,112},{64,0},{80,16},{96,32},{112,48},{1... | collective-permute-start | bytes 196616 | tf_op jit(solution)/shard_map/ppermute | solution.py:420
  83.0 1.0 %shard_map.131 = bf16[128,1024]{1,0:T(8,128)(2,1)} custom-call(bf16[128,512]{1,0:T(8,128)(2,1)S(1)} %get-tuple-element.28.hid_ref, bf16[512,1024]{1,0:T(8,128)(2,1)S(1)} %copy-done), custom_call_target="tpu_custom_call" | custom-call | flops 1100000000 | bytes 1441792 | tf_op jit(solution)/shard_map/pallas_call | solution.py:400
  84.1 2.3 %collective-permute-done.5.refs_2_ = bf16[256,128]{1,0:T(8,128)(2,1)S(1)} collective-permute-done((bf16[256,128]{1,0:T(8,128)(2,1)S(1)}, bf16[256,128]{1,0:T(8,128)(2,1)S(1)}, u32[]{:S(2)}, u32[]{:S(2)}) %collective-permute-start.5) | collective-permute-done | bytes 65568 | tf_op jit(solution)/shard_map/ppermute | solution.py:420
  86.4 2.1 %collective-permute-done.6.refs_3_ = bf16[256,128]{1,0:T(8,128)(2,1)S(1)} collective-permute-done((bf16[256,128]{1,0:T(8,128)(2,1)S(1)}, bf16[256,128]{1,0:T(8,128)(2,1)S(1)}, u32[]{:S(2)}, u32[]{:S(2)}) %collective-permute-start.6) | collective-permute-done | bytes 65568 | tf_op jit(solution)/shard_map/ppermute | solution.py:420
  88.6 2.1 %all-to-all-done.3.recv_ref = bf16[16,208,128]{2,1,0:T(8,128)(2,1)S(1)} async-done(((bf16[16,208,128]{2,1,0:T(8,128)(2,1)}), bf16[16,208,128]{2,1,0:T(8,128)(2,1)S(1)}, u32[]{:S(2)}, u32[]{:S(2)}) %all-to-all-start.3) | async-done | bytes 852000 | tf_op jit(solution)/shard_map/all_to_all | solution.py:416
  90.7 0.9 %shard_map.140 = (bf16[128,512]{1,0:T(8,128)(2,1)}, bf16[128,512]{1,0:T(8,128)(2,1)}, bf16[128,512]{1,0:T(8,128)(2,1)}, bf16[128,512]{1,0:T(8,128)(2,1)}, f32[32,1024]{1,0:T(8,128)}) custom-call(bf16[16,208,128]{2,1,0:T(8,128)(2,1)S(1)} %all-to-all-done.3.recv_ref, f32[128,512]{1,0:T(8,128)S(1)} %get-tuple-element.41.ghn_ref, f32[256,128]{1,0:T(8,128)S(1)} %shard_map.139.gw_ref), custom_call_target="tpu_custom_call" | custom-call | flops 1100000000 | bytes 1900544 | tf_op jit(solution)/shard_map/pallas_call | solution.py:400
  (21 shorter events, 0.7 us)
Async XLA Ops:
  2.8 8.6 %copy-start.1 = (bf16[1,128,1024]{2,1,0:T(8,128)(2,1)S(1)}, bf16[1,128,1024]{2,1,0:T(8,128)(2,1)}, u32[]{:S(2)}) copy-start(bf16[1,128,1024]{2,1,0:T(8,128)(2,1)} %param.15) | copy-start | bytes 786436
  2.8 8.8 %copy-start.4 = (f32[4,128,64]{1,2,0:T(8,128)S(1)}, f32[4,128,64]{1,2,0:T(8,128)}, u32[]{:S(2)}) copy-start(f32[4,128,64]{1,2,0:T(8,128)} %param.12) | copy-start | bytes 393220
  2.8 8.9 %copy-start = (bf16[512,1024]{1,0:T(8,128)(2,1)S(1)}, bf16[512,1024]{1,0:T(8,128)(2,1)}, u32[]{:S(2)}) copy-start(bf16[512,1024]{1,0:T(8,128)(2,1)} %w_ref.3) | copy-start | bytes 3145732
  2.8 23.8 %all-to-all-start = ((bf16[16,208,128]{2,1,0:T(8,128)(2,1)}), bf16[16,208,128]{2,1,0:T(8,128)(2,1)S(1)}, u32[]{:S(2)}, u32[]{:S(2)}) async-start(bf16[16,208,128]{2,1,0:T(8,128)(2,1)} %shard_map.127), calls=%async_computation | async-start | bytes 1703936 | tf_op jit(solution)/shard_map/all_to_all | solution.py:416
  11.4 1.6 %collective-permute-start = (bf16[128,1024]{1,0:T(8,128)(2,1)S(1)}, bf16[128,1024]{1,0:T(8,128)(2,1)S(1)}, u32[]{:S(2)}, u32[]{:S(2)}) collective-permute-start(bf16[128,1024]{1,0:T(8,128)(2,1)S(1)} %bitcast.11), channel_id=1, source_target_pairs={{0,1},{1,0},{2,3},{3,2},{4,5},{5,4},{6,7},{7,6},{8,9},{9,8},{10,11... | collective-permute-start | bytes 786440 | tf_op jit(solution)/shard_map/ppermute | solution.py:424
  12.2 14.4 %copy-start.3 = (s32[1,8]{1,0:T(1,128)S(1)}, s32[1,8]{1,0:T(1,128)}, u32[]{:S(2)}) copy-start(s32[1,8]{1,0:T(1,128)} %lens_ref.1) | copy-start | bytes 100
  29.7 12.0 %copy-start.2 = (bf16[1,128,512]{2,1,0:T(8,128)(2,1)S(1)}, bf16[1,128,512]{2,1,0:T(8,128)(2,1)}, u32[]{:S(2)}) copy-start(bf16[1,128,512]{2,1,0:T(8,128)(2,1)} %param.11) | copy-start | bytes 393220
  42.5 1.9 %collective-permute-start.1 = (bf16[128,512]{1,0:T(8,128)(2,1)S(1)}, bf16[128,512]{1,0:T(8,128)(2,1)S(1)}, u32[]{:S(2)}, u32[]{:S(2)}) collective-permute-start(bf16[128,512]{1,0:T(8,128)(2,1)S(1)} %get-tuple-element.28.hid_ref), channel_id=1, source_target_pairs={{0,1},{1,0},{2,3},{3,2},{4,5},{5,4},{6,7},{7,6},{8,9},{9,8},{10,11... | collective-permute-start | bytes 393224 | tf_op jit(solution)/shard_map/ppermute | solution.py:424
  61.9 3.4 %collective-permute-start.2 = (bf16[256,128]{1,0:T(8,128)(2,1)S(1)}, bf16[256,128]{1,0:T(8,128)(2,1)S(1)}, u32[]{:S(2)}, u32[]{:S(2)}) collective-permute-start(bf16[256,128]{1,0:T(8,128)(2,1)S(1)} %shard_map.135.refs_0_), channel_id=1, source_target_pairs={{0,128},{16,144},{32,160},{48,176},{64,192},{80,208},{96,224},{112... | collective-permute-start | bytes 196616 | tf_op jit(solution)/shard_map/ppermute | solution.py:420
  65.3 4.5 %collective-permute-start.3 = (bf16[256,128]{1,0:T(8,128)(2,1)S(1)}, bf16[256,128]{1,0:T(8,128)(2,1)S(1)}, u32[]{:S(2)}, u32[]{:S(2)}) collective-permute-start(bf16[256,128]{1,0:T(8,128)(2,1)S(1)} %shard_map.136.refs_11_.refs_0_), channel_id=1, source_target_pairs={{0,16},{16,0},{32,48},{48,32},{64,80},{80,64},{96,112},{112,96},{1... | collective-permute-start | bytes 196616 | tf_op jit(solution)/shard_map/ppermute | solution.py:420
  69.8 20.9 %all-to-all-start.3 = ((bf16[16,208,128]{2,1,0:T(8,128)(2,1)}), bf16[16,208,128]{2,1,0:T(8,128)(2,1)S(1)}, u32[]{:S(2)}, u32[]{:S(2)}) async-start(bf16[16,208,128]{2,1,0:T(8,128)(2,1)} %shard_map.137.refs_2_), calls=%async_computation.3 | async-start | bytes 1703936 | tf_op jit(solution)/shard_map/all_to_all | solution.py:416
  75.3 8.7 %collective-permute-start.4 = (bf16[256,128]{1,0:T(8,128)(2,1)S(1)}, bf16[256,128]{1,0:T(8,128)(2,1)S(1)}, u32[]{:S(2)}, u32[]{:S(2)}) collective-permute-start(bf16[256,128]{1,0:T(8,128)(2,1)S(1)} %shard_map.138.refs_0_), channel_id=1, source_target_pairs={{0,32},{16,48},{32,0},{48,16},{64,96},{80,112},{96,64},{112,80},{1... | collective-permute-start | bytes 196616 | tf_op jit(solution)/shard_map/ppermute | solution.py:420
  78.3 8.1 %collective-permute-start.5 = (bf16[256,128]{1,0:T(8,128)(2,1)S(1)}, bf16[256,128]{1,0:T(8,128)(2,1)S(1)}, u32[]{:S(2)}, u32[]{:S(2)}) collective-permute-start(bf16[256,128]{1,0:T(8,128)(2,1)S(1)} %shard_map.138.refs_0_), channel_id=1, source_target_pairs={{0,64},{16,80},{32,96},{48,112},{64,0},{80,16},{96,32},{112,48},{1... | collective-permute-start | bytes 196616 | tf_op jit(solution)/shard_map/ppermute | solution.py:420
  83.0 5.5 %collective-permute-start.6 = (bf16[256,128]{1,0:T(8,128)(2,1)S(1)}, bf16[256,128]{1,0:T(8,128)(2,1)S(1)}, u32[]{:S(2)}, u32[]{:S(2)}) collective-permute-start(bf16[256,128]{1,0:T(8,128)(2,1)S(1)} %shard_map.138.refs_0_), channel_id=1, source_target_pairs={{0,96},{16,112},{32,64},{48,80},{64,32},{80,48},{96,0},{112,16},{1... | collective-permute-start | bytes 196616 | tf_op jit(solution)/shard_map/ppermute | solution.py:420

commit v7 on v6

--- a/solution.py
+++ b/solution.py
@@ -181,9 +181,10 @@
 
     for b in range(NBLK):
         qp_ref[b * SUB : (b + 1) * SUB, :HEAD] = recv_ref[b, Q0:G0, :]
-    for i in range(4):
-        rows = slice(i * ROWS // 4, (i + 1) * ROWS // 4)
-        qp_ref[rows, HEAD:] = phi_of(qp_ref[rows, :HEAD])
+    qp_ref[:, HEAD:] = phi_of(qp_ref[:, :HEAD])
+    phik_ref[...] = phi_of(
+        jnp.concatenate([recv_ref[b, K0:V0, :] for b in range(NBLK)], axis=0)
+    )
     copy.wait()
     stage_rows(recv_ref, lens_s, gq, gate_ref, start_ref)
     acc_s[...] = jnp.zeros_like(acc_s)
@@ -191,8 +192,7 @@
         rows = tile_rows(c)
         keys = tile_of(recv_ref, c, K0, V0)
         values = tile_of(recv_ref, c, V0, PACK)
-        phik = phi_of(keys)
-        phik_ref[c * TILE : (c + 1) * TILE, :] = phik
+        phik = phik_ref[c * TILE : (c + 1) * TILE, :]
         both = mm(qp_ref[rows, :], diagonal(keys, phik), NT)
         half, kern = both[:, :TILE] * (0.5 * SCALE), both[:, TILE:]
         both = half + half * jnp.tanh(half) + twice(gate_ref[rows, :]) * kern

time: 92 us -> 91.8 us (level)
  no operation moved by 1% of the time
where the time goes in v7:
time: 91.8 us; the launch traced here: 91.5 us
  blocking collectives  29.2 us (32%)
  starting transfers between devices  25.1 us (27%)
  waiting for transfers between devices  21.8 us (24%)
  Pallas kernels  14.5 us (16%)
    all_to_all x2, blocking collectives, swap(): return lax.all_to_all(a, axis, 0, 0, tiled=True)  29.2 us
    all_to_all x2, waiting for transfers between devices, swap(): return lax.all_to_all(a, axis, 0, 0, tiled=True)  15.7 us
    pallas_call x14, Pallas kernels, call(): pl.pallas_call(body, in_specs=[SMEM] * len(scalars) + (spaces or [space]...  14.5 us
    all_to_all x2, starting transfers between devices, swap(): return lax.all_to_all(a, axis, 0, 0, tiled=True)  14.1 us
    ppermute x5, starting transfers between devices, cross(): return lax.ppermute(x, 'dp', [(i, i ^ mask) for i in range(16)])  9.93 us
    ppermute x5, waiting for transfers between devices, cross(): return lax.ppermute(x, 'dp', [(i, i ^ mask) for i in range(16)])  4.46 us
  transfers between devices with their start and end apart: 9, of which 6 were waited for; matrix products, arithmetic and copies ran while one was open for 0% of the time, Pallas kernels for 8%

profile of v7, /device:TPU:1, one launch (start us, length us, event | category | flops | bytes accessed | tf_op | source)
XLA Modules:
  0.0 91.5 jit_solution(7580037787259067721)
XLA Ops:
  0.6 2.1 %shard_map.127 = bf16[16,208,128]{2,1,0:T(8,128)(2,1)} custom-call(bf16[128,512]{1,0:T(8,128)(2,1)} %bitcast.17, bf16[128,512]{1,0:T(8,128)(2,1)} %bitcast.18, bf16[128,512]{1,0:T(8,128)(2,1)} %bitcast.19, bf16[128,512]{1,0:T(8,128)(2,1)} %bitcast.14), custom_call_target="tpu_custom_call" | custom-call | flops 1100000000 | bytes 1376256 | tf_op jit(solution)/shard_map/pallas_call | solution.py:400
  2.8 8.6 %all-to-all-start = ((bf16[16,208,128]{2,1,0:T(8,128)(2,1)}), bf16[16,208,128]{2,1,0:T(8,128)(2,1)S(1)}, u32[]{:S(2)}, u32[]{:S(2)}) async-start(bf16[16,208,128]{2,1,0:T(8,128)(2,1)} %shard_map.127), calls=%async_computation | async-start | bytes 1703936 | tf_op jit(solution)/shard_map/all_to_all | solution.py:416
  11.8 0.5 shard_map.128.refs_4_.gh_ref
  12.3 0.8 collective-permute-done.refs_5_.cot2_ref
  13.0 13.6 %all-to-all-done.refs_1_.recv_ref = bf16[16,208,128]{2,1,0:T(8,128)(2,1)S(1)} async-done(((bf16[16,208,128]{2,1,0:T(8,128)(2,1)}), bf16[16,208,128]{2,1,0:T(8,128)(2,1)S(1)}, u32[]{:S(2)}, u32[]{:S(2)}) %all-to-all-start) | async-done | bytes 852000 | tf_op jit(solution)/shard_map/all_to_all | solution.py:416
  26.7 2.8 %shard_map.129 = (bf16[16,64,128]{2,1,0:T(8,128)(2,1)S(1)}, bf16[1024,128]{1,0:T(8,128)(2,1)S(1)}, bf16[1024,256]{1,0:T(8,128)(2,1)S(1)}, f32[1024,128]{1,0:T(8,128)S(1)}, f32[1024,128]{1,0:T(8,128)S(1)}) custom-call(s32[1]{0:T(128)} %bitcast.refs_0_.idx_ref, bf16[16,208,128]{2,1,0:T(8,128)(2,1)S(1)} %all-to-all-done.refs_1_.recv_ref, ...), custom_call_target="tpu_custom_call" | custom-call | flops 3849999872 | bytes 3080224 | tf_op jit(solution)/shard_map/pallas_call | solution.py:400
  29.5 12.0 %all_to_all.20.mixed_ref = bf16[16,64,128]{2,1,0:T(8,128)(2,1)S(1)} all-to-all(bf16[16,64,128]{2,1,0:T(8,128)(2,1)S(1)} %get-tuple-element.27), channel_id=1, replica_groups=mesh['dp'=16,'blk'=16] {'blk'}, dimensions={0} | all-to-all | bytes 524288 | tf_op jit(solution)/shard_map/all_to_all | solution.py:416
  41.5 0.8 shard_map.130
  42.3 0.9 collective-permute-start.1
  43.4 0.8 collective-permute-done.1.hid2_ref
  44.2 0.3 shard_map.133
  44.6 17.1 %all_to_all.21.grads_ref.parts_ref = bf16[16,192,128]{2,1,0:T(8,128)(2,1)S(1)} all-to-all(bf16[16,192,128]{2,1,0:T(8,128)(2,1)S(1)} %shard_map.133), channel_id=1, replica_groups=mesh['dp'=16,'blk'=16] {'blk'}, dimensions={0} | all-to-all | bytes 1572864 | tf_op jit(solution)/shard_map/all_to_all | solution.py:416
  61.8 0.5 collective-permute-start.2
  62.3 2.9 %shard_map.134 = (bf16[8,128,128]{2,1,0:T(8,128)(2,1)S(1)}, bf16[1024,128]{1,0:T(8,128)(2,1)S(1)}, f32[1024,256]{1,0:T(8,128)S(1)}, f32[1024,128]{1,0:T(8,128)S(1)}) custom-call(s32[1]{0:T(128)} %bitcast.refs_0_.idx_ref, bf16[16,208,128]{2,1,0:T(8,128)(2,1)S(1)} %all-to-all-done.refs_1_.recv_ref, bf16[1024,128]{1,0:T(8,128)(2,1)S(1)} %get-tuple-element.29.phik_ref.refs_2_, ...), custom_call_target="tpu_custom_call" | custom-call | flops 3300000000 | bytes 5701632 | tf_op jit(solution)/shard_map/pallas_call | solution.py:400
  65.2 1.7 %collective-permute-start.3 = (bf16[256,128]{1,0:T(8,128)(2,1)S(1)}, bf16[256,128]{1,0:T(8,128)(2,1)S(1)}, u32[]{:S(2)}, u32[]{:S(2)}) collective-permute-start(bf16[256,128]{1,0:T(8,128)(2,1)S(1)} %shard_map.136.refs_11_.refs_0_), channel_id=1, source_target_pairs={{0,16},{16,0},{32,48},{48,32},{64,80},{80,64},{96,112},{112,96},{1... | collective-permute-start | bytes 196616 | tf_op jit(solution)/shard_map/ppermute | solution.py:420
  66.9 2.7 %shard_map.137.refs_2_ = bf16[16,208,128]{2,1,0:T(8,128)(2,1)} custom-call(s32[1]{0:T(128)} %bitcast.refs_0_.idx_ref, bf16[16,208,128]{2,1,0:T(8,128)(2,1)S(1)} %all-to-all-done.refs_1_.recv_ref, bf16[1024,128]{1,0:T(8,128)(2,1)S(1)} %get-tuple-element.29.phik_ref.refs_2_, bf16[1024,256]{1,0:T(8,128)(2,1)S(1)} %get-tuple-element.30.qp_ref.refs_3_, ...), custom_call_target="tpu_custom_call" | custom-call | flops 3300000000 | bytes 5767168 | tf_op jit(solution)/shard_map/pallas_call | solution.py:400
  69.7 5.5 %all-to-all-start.3 = ((bf16[16,208,128]{2,1,0:T(8,128)(2,1)}), bf16[16,208,128]{2,1,0:T(8,128)(2,1)S(1)}, u32[]{:S(2)}, u32[]{:S(2)}) async-start(bf16[16,208,128]{2,1,0:T(8,128)(2,1)} %shard_map.137.refs_2_), calls=%async_computation.3 | async-start | bytes 1703936 | tf_op jit(solution)/shard_map/all_to_all | solution.py:416
  75.2 3.0 %collective-permute-start.4 = (bf16[256,128]{1,0:T(8,128)(2,1)S(1)}, bf16[256,128]{1,0:T(8,128)(2,1)S(1)}, u32[]{:S(2)}, u32[]{:S(2)}) collective-permute-start(bf16[256,128]{1,0:T(8,128)(2,1)S(1)} %shard_map.138.refs_0_), channel_id=1, source_target_pairs={{0,32},{16,48},{32,0},{48,16},{64,96},{80,112},{96,64},{112,80},{1... | collective-permute-start | bytes 196616 | tf_op jit(solution)/shard_map/ppermute | solution.py:420
  78.2 4.7 %collective-permute-start.5 = (bf16[256,128]{1,0:T(8,128)(2,1)S(1)}, bf16[256,128]{1,0:T(8,128)(2,1)S(1)}, u32[]{:S(2)}, u32[]{:S(2)}) collective-permute-start(bf16[256,128]{1,0:T(8,128)(2,1)S(1)} %shard_map.138.refs_0_), channel_id=1, source_target_pairs={{0,64},{16,80},{32,96},{48,112},{64,0},{80,16},{96,32},{112,48},{1... | collective-permute-start | bytes 196616 | tf_op jit(solution)/shard_map/ppermute | solution.py:420
  82.9 1.0 %shard_map.131 = bf16[128,1024]{1,0:T(8,128)(2,1)} custom-call(bf16[128,512]{1,0:T(8,128)(2,1)S(1)} %get-tuple-element.28.hid_ref, bf16[512,1024]{1,0:T(8,128)(2,1)S(1)} %copy-done), custom_call_target="tpu_custom_call" | custom-call | flops 1100000000 | bytes 1441792 | tf_op jit(solution)/shard_map/pallas_call | solution.py:400
  83.9 2.3 %collective-permute-done.5.refs_2_ = bf16[256,128]{1,0:T(8,128)(2,1)S(1)} collective-permute-done((bf16[256,128]{1,0:T(8,128)(2,1)S(1)}, bf16[256,128]{1,0:T(8,128)(2,1)S(1)}, u32[]{:S(2)}, u32[]{:S(2)}) %collective-permute-start.5) | collective-permute-done | bytes 65568 | tf_op jit(solution)/shard_map/ppermute | solution.py:420
  86.3 2.1 %collective-permute-done.6.refs_3_ = bf16[256,128]{1,0:T(8,128)(2,1)S(1)} collective-permute-done((bf16[256,128]{1,0:T(8,128)(2,1)S(1)}, bf16[256,128]{1,0:T(8,128)(2,1)S(1)}, u32[]{:S(2)}, u32[]{:S(2)}) %collective-permute-start.6) | collective-permute-done | bytes 65568 | tf_op jit(solution)/shard_map/ppermute | solution.py:420
  88.4 2.1 %all-to-all-done.3.recv_ref = bf16[16,208,128]{2,1,0:T(8,128)(2,1)S(1)} async-done(((bf16[16,208,128]{2,1,0:T(8,128)(2,1)}), bf16[16,208,128]{2,1,0:T(8,128)(2,1)S(1)}, u32[]{:S(2)}, u32[]{:S(2)}) %all-to-all-start.3) | async-done | bytes 852000 | tf_op jit(solution)/shard_map/all_to_all | solution.py:416
  90.5 0.9 %shard_map.140 = (bf16[128,512]{1,0:T(8,128)(2,1)}, bf16[128,512]{1,0:T(8,128)(2,1)}, bf16[128,512]{1,0:T(8,128)(2,1)}, bf16[128,512]{1,0:T(8,128)(2,1)}, f32[32,1024]{1,0:T(8,128)}) custom-call(bf16[16,208,128]{2,1,0:T(8,128)(2,1)S(1)} %all-to-all-done.3.recv_ref, f32[128,512]{1,0:T(8,128)S(1)} %get-tuple-element.41.ghn_ref, f32[256,128]{1,0:T(8,128)S(1)} %shard_map.139.gw_ref), custom_call_target="tpu_custom_call" | custom-call | flops 1100000000 | bytes 1900544 | tf_op jit(solution)/shard_map/pallas_call | solution.py:400
  (21 shorter events, 0.7 us)
Async XLA Ops:
  2.8 8.6 %copy-start.1 = (bf16[1,128,1024]{2,1,0:T(8,128)(2,1)S(1)}, bf16[1,128,1024]{2,1,0:T(8,128)(2,1)}, u32[]{:S(2)}) copy-start(bf16[1,128,1024]{2,1,0:T(8,128)(2,1)} %param.15) | copy-start | bytes 786436
  2.8 8.8 %copy-start.4 = (f32[4,128,64]{1,2,0:T(8,128)S(1)}, f32[4,128,64]{1,2,0:T(8,128)}, u32[]{:S(2)}) copy-start(f32[4,128,64]{1,2,0:T(8,128)} %param.12) | copy-start | bytes 393220
  2.8 8.9 %copy-start = (bf16[512,1024]{1,0:T(8,128)(2,1)S(1)}, bf16[512,1024]{1,0:T(8,128)(2,1)}, u32[]{:S(2)}) copy-start(bf16[512,1024]{1,0:T(8,128)(2,1)} %w_ref.3) | copy-start | bytes 3145732
  2.8 23.8 %all-to-all-start = ((bf16[16,208,128]{2,1,0:T(8,128)(2,1)}), bf16[16,208,128]{2,1,0:T(8,128)(2,1)S(1)}, u32[]{:S(2)}, u32[]{:S(2)}) async-start(bf16[16,208,128]{2,1,0:T(8,128)(2,1)} %shard_map.127), calls=%async_computation | async-start | bytes 1703936 | tf_op jit(solution)/shard_map/all_to_all | solution.py:416
  11.4 1.6 %collective-permute-start = (bf16[128,1024]{1,0:T(8,128)(2,1)S(1)}, bf16[128,1024]{1,0:T(8,128)(2,1)S(1)}, u32[]{:S(2)}, u32[]{:S(2)}) collective-permute-start(bf16[128,1024]{1,0:T(8,128)(2,1)S(1)} %bitcast.11), channel_id=1, source_target_pairs={{0,1},{1,0},{2,3},{3,2},{4,5},{5,4},{6,7},{7,6},{8,9},{9,8},{10,11... | collective-permute-start | bytes 786440 | tf_op jit(solution)/shard_map/ppermute | solution.py:424
  12.2 14.4 %copy-start.3 = (s32[1,8]{1,0:T(1,128)S(1)}, s32[1,8]{1,0:T(1,128)}, u32[]{:S(2)}) copy-start(s32[1,8]{1,0:T(1,128)} %lens_ref.1) | copy-start | bytes 100
  29.5 12.0 %copy-start.2 = (bf16[1,128,512]{2,1,0:T(8,128)(2,1)S(1)}, bf16[1,128,512]{2,1,0:T(8,128)(2,1)}, u32[]{:S(2)}) copy-start(bf16[1,128,512]{2,1,0:T(8,128)(2,1)} %param.11) | copy-start | bytes 393220
  42.3 1.9 %collective-permute-start.1 = (bf16[128,512]{1,0:T(8,128)(2,1)S(1)}, bf16[128,512]{1,0:T(8,128)(2,1)S(1)}, u32[]{:S(2)}, u32[]{:S(2)}) collective-permute-start(bf16[128,512]{1,0:T(8,128)(2,1)S(1)} %get-tuple-element.28.hid_ref), channel_id=1, source_target_pairs={{0,1},{1,0},{2,3},{3,2},{4,5},{5,4},{6,7},{7,6},{8,9},{9,8},{10,11... | collective-permute-start | bytes 393224 | tf_op jit(solution)/shard_map/ppermute | solution.py:424
  61.8 3.4 %collective-permute-start.2 = (bf16[256,128]{1,0:T(8,128)(2,1)S(1)}, bf16[256,128]{1,0:T(8,128)(2,1)S(1)}, u32[]{:S(2)}, u32[]{:S(2)}) collective-permute-start(bf16[256,128]{1,0:T(8,128)(2,1)S(1)} %shard_map.135.refs_0_), channel_id=1, source_target_pairs={{0,128},{16,144},{32,160},{48,176},{64,192},{80,208},{96,224},{112... | collective-permute-start | bytes 196616 | tf_op jit(solution)/shard_map/ppermute | solution.py:420
  65.2 4.5 %collective-permute-start.3 = (bf16[256,128]{1,0:T(8,128)(2,1)S(1)}, bf16[256,128]{1,0:T(8,128)(2,1)S(1)}, u32[]{:S(2)}, u32[]{:S(2)}) collective-permute-start(bf16[256,128]{1,0:T(8,128)(2,1)S(1)} %shard_map.136.refs_11_.refs_0_), channel_id=1, source_target_pairs={{0,16},{16,0},{32,48},{48,32},{64,80},{80,64},{96,112},{112,96},{1... | collective-permute-start | bytes 196616 | tf_op jit(solution)/shard_map/ppermute | solution.py:420
  69.7 20.8 %all-to-all-start.3 = ((bf16[16,208,128]{2,1,0:T(8,128)(2,1)}), bf16[16,208,128]{2,1,0:T(8,128)(2,1)S(1)}, u32[]{:S(2)}, u32[]{:S(2)}) async-start(bf16[16,208,128]{2,1,0:T(8,128)(2,1)} %shard_map.137.refs_2_), calls=%async_computation.3 | async-start | bytes 1703936 | tf_op jit(solution)/shard_map/all_to_all | solution.py:416
  75.2 8.7 %collective-permute-start.4 = (bf16[256,128]{1,0:T(8,128)(2,1)S(1)}, bf16[256,128]{1,0:T(8,128)(2,1)S(1)}, u32[]{:S(2)}, u32[]{:S(2)}) collective-permute-start(bf16[256,128]{1,0:T(8,128)(2,1)S(1)} %shard_map.138.refs_0_), channel_id=1, source_target_pairs={{0,32},{16,48},{32,0},{48,16},{64,96},{80,112},{96,64},{112,80},{1... | collective-permute-start | bytes 196616 | tf_op jit(solution)/shard_map/ppermute | solution.py:420
  78.2 8.1 %collective-permute-start.5 = (bf16[256,128]{1,0:T(8,128)(2,1)S(1)}, bf16[256,128]{1,0:T(8,128)(2,1)S(1)}, u32[]{:S(2)}, u32[]{:S(2)}) collective-permute-start(bf16[256,128]{1,0:T(8,128)(2,1)S(1)} %shard_map.138.refs_0_), channel_id=1, source_target_pairs={{0,64},{16,80},{32,96},{48,112},{64,0},{80,16},{96,32},{112,48},{1... | collective-permute-start | bytes 196616 | tf_op jit(solution)/shard_map/ppermute | solution.py:420
  82.9 5.5 %collective-permute-start.6 = (bf16[256,128]{1,0:T(8,128)(2,1)S(1)}, bf16[256,128]{1,0:T(8,128)(2,1)S(1)}, u32[]{:S(2)}, u32[]{:S(2)}) collective-permute-start(bf16[256,128]{1,0:T(8,128)(2,1)S(1)} %shard_map.138.refs_0_), channel_id=1, source_target_pairs={{0,96},{16,112},{32,64},{48,80},{64,32},{80,48},{96,0},{112,16},{1... | collective-permute-start | bytes 196616 | tf_op jit(solution)/shard_map/ppermute | solution.py:420

commit v8 on v6

--- a/solution.py
+++ b/solution.py
@@ -493,10 +493,9 @@
         us=3.0,
         after=[gw],
     )
-    (gw,) = call(
-        add_kernel, [], [gw, cross(gw, 1)], [((WROWS, HEAD), BF16)], us=0.5, after=[send4]
-    )
-    send4, gw = lax.optimization_barrier((send4, gw))
+    other = cross(gw, 1)
+    send4, other = lax.optimization_barrier((send4, other))
+    (gw,) = call(add_kernel, [], [gw, other], [((WROWS, HEAD), BF16)], us=0.5)
     parts = [gw] + [cross(gw, mask) for mask in (2, 4, 6)]
     (gw,) = call(add_kernel, [], parts, [((WROWS, HEAD), F32)], us=0.5)
     recv4 = swap(send4, "blk")

time: 92 us -> 92 us (level)
  no operation moved by 1% of the time
where the time goes in v8:
time: 92 us; the launch traced here: 91.6 us
  blocking collectives  29.2 us (32%)
  starting transfers between devices  25.2 us (27%)
  waiting for transfers between devices  21.7 us (24%)
  Pallas kernels  14.6 us (16%)
    all_to_all x2, blocking collectives, swap(): return lax.all_to_all(a, axis, 0, 0, tiled=True)  29.2 us
    all_to_all x2, waiting for transfers between devices, swap(): return lax.all_to_all(a, axis, 0, 0, tiled=True)  15.6 us
    pallas_call x14, Pallas kernels, call(): pl.pallas_call(body, in_specs=[SMEM] * len(scalars) + (spaces or [space]...  14.6 us
    all_to_all x2, starting transfers between devices, swap(): return lax.all_to_all(a, axis, 0, 0, tiled=True)  14.1 us
    ppermute x5, starting transfers between devices, cross(): return lax.ppermute(x, 'dp', [(i, i ^ mask) for i in range(16)])  10 us
    ppermute x5, waiting for transfers between devices, cross(): return lax.ppermute(x, 'dp', [(i, i ^ mask) for i in range(16)])  4.49 us
  transfers between devices with their start and end apart: 9, of which 6 were waited for; matrix products, arithmetic and copies ran while one was open for 0% of the time, Pallas kernels for 8%

profile of v8, /device:TPU:1, one launch (start us, length us, event | category | flops | bytes accessed | tf_op | source)
XLA Modules:
  0.0 91.6 jit_solution(9383809157638744216)
XLA Ops:
  0.6 2.1 %shard_map.127 = bf16[16,208,128]{2,1,0:T(8,128)(2,1)} custom-call(bf16[128,512]{1,0:T(8,128)(2,1)} %bitcast.17, bf16[128,512]{1,0:T(8,128)(2,1)} %bitcast.18, bf16[128,512]{1,0:T(8,128)(2,1)} %bitcast.19, bf16[128,512]{1,0:T(8,128)(2,1)} %bitcast.14), custom_call_target="tpu_custom_call" | custom-call | flops 1100000000 | bytes 1376256 | tf_op jit(solution)/shard_map/pallas_call | solution.py:400
  2.8 8.6 %all-to-all-start = ((bf16[16,208,128]{2,1,0:T(8,128)(2,1)}), bf16[16,208,128]{2,1,0:T(8,128)(2,1)S(1)}, u32[]{:S(2)}, u32[]{:S(2)}) async-start(bf16[16,208,128]{2,1,0:T(8,128)(2,1)} %shard_map.127), calls=%async_computation | async-start | bytes 1703936 | tf_op jit(solution)/shard_map/all_to_all | solution.py:416
  11.8 0.5 shard_map.128.refs_4_.gh_ref
  12.3 0.8 collective-permute-done.refs_5_.cot2_ref
  13.0 13.6 %all-to-all-done.refs_1_.recv_ref = bf16[16,208,128]{2,1,0:T(8,128)(2,1)S(1)} async-done(((bf16[16,208,128]{2,1,0:T(8,128)(2,1)}), bf16[16,208,128]{2,1,0:T(8,128)(2,1)S(1)}, u32[]{:S(2)}, u32[]{:S(2)}) %all-to-all-start) | async-done | bytes 852000 | tf_op jit(solution)/shard_map/all_to_all | solution.py:416
  26.7 3.0 %shard_map.129 = (bf16[16,64,128]{2,1,0:T(8,128)(2,1)S(1)}, bf16[1024,128]{1,0:T(8,128)(2,1)S(1)}, bf16[1024,256]{1,0:T(8,128)(2,1)S(1)}, f32[1024,128]{1,0:T(8,128)S(1)}, f32[1024,128]{1,0:T(8,128)S(1)}) custom-call(s32[1]{0:T(128)} %bitcast.refs_0_.idx_ref, bf16[16,208,128]{2,1,0:T(8,128)(2,1)S(1)} %all-to-all-done.refs_1_.recv_ref, ...), custom_call_target="tpu_custom_call" | custom-call | flops 3849999872 | bytes 3080224 | tf_op jit(solution)/shard_map/pallas_call | solution.py:400
  29.7 12.0 %all_to_all.20.mixed_ref = bf16[16,64,128]{2,1,0:T(8,128)(2,1)S(1)} all-to-all(bf16[16,64,128]{2,1,0:T(8,128)(2,1)S(1)} %get-tuple-element.27), channel_id=1, replica_groups=mesh['dp'=16,'blk'=16] {'blk'}, dimensions={0} | all-to-all | bytes 524288 | tf_op jit(solution)/shard_map/all_to_all | solution.py:416
  41.7 0.8 shard_map.130
  42.5 0.9 collective-permute-start.1
  43.6 0.8 collective-permute-done.1.hid2_ref
  44.4 0.3 shard_map.133
  44.7 17.1 %all_to_all.21.grads_ref.parts_ref = bf16[16,192,128]{2,1,0:T(8,128)(2,1)S(1)} all-to-all(bf16[16,192,128]{2,1,0:T(8,128)(2,1)S(1)} %shard_map.133), channel_id=1, replica_groups=mesh['dp'=16,'blk'=16] {'blk'}, dimensions={0} | all-to-all | bytes 1572864 | tf_op jit(solution)/shard_map/all_to_all | solution.py:416
  61.9 0.5 collective-permute-start.2
  62.4 2.9 %shard_map.134 = (bf16[8,128,128]{2,1,0:T(8,128)(2,1)S(1)}, bf16[1024,128]{1,0:T(8,128)(2,1)S(1)}, f32[1024,256]{1,0:T(8,128)S(1)}, f32[1024,128]{1,0:T(8,128)S(1)}) custom-call(s32[1]{0:T(128)} %bitcast.refs_0_.idx_ref, bf16[16,208,128]{2,1,0:T(8,128)(2,1)S(1)} %all-to-all-done.refs_1_.recv_ref, bf16[1024,128]{1,0:T(8,128)(2,1)S(1)} %get-tuple-element.29.phik_ref.refs_2_, ...), custom_call_target="tpu_custom_call" | custom-call | flops 3300000000 | bytes 5701632 | tf_op jit(solution)/shard_map/pallas_call | solution.py:400
  65.3 1.7 %collective-permute-start.3 = (bf16[256,128]{1,0:T(8,128)(2,1)S(1)}, bf16[256,128]{1,0:T(8,128)(2,1)S(1)}, u32[]{:S(2)}, u32[]{:S(2)}) collective-permute-start(bf16[256,128]{1,0:T(8,128)(2,1)S(1)} %shard_map.136.refs_11_.refs_0_), channel_id=1, source_target_pairs={{0,16},{16,0},{32,48},{48,32},{64,80},{80,64},{96,112},{112,96},{1... | collective-permute-start | bytes 196616 | tf_op jit(solution)/shard_map/ppermute | solution.py:420
  67.1 2.7 %shard_map.137 = bf16[16,208,128]{2,1,0:T(8,128)(2,1)} custom-call(s32[1]{0:T(128)} %bitcast.refs_0_.idx_ref, bf16[16,208,128]{2,1,0:T(8,128)(2,1)S(1)} %all-to-all-done.refs_1_.recv_ref, bf16[1024,128]{1,0:T(8,128)(2,1)S(1)} %get-tuple-element.29.phik_ref.refs_2_, bf16[1024,256]{1,0:T(8,128)(2,1)S(1)} %get-tuple-element.30.qp_ref.refs_3_, ...), custom_call_target="tpu_custom_call" | custom-call | flops 3300000000 | bytes 5767168 | tf_op jit(solution)/shard_map/pallas_call | solution.py:400
  69.8 5.5 %all-to-all-start.3 = ((bf16[16,208,128]{2,1,0:T(8,128)(2,1)}), bf16[16,208,128]{2,1,0:T(8,128)(2,1)S(1)}, u32[]{:S(2)}, u32[]{:S(2)}) async-start(bf16[16,208,128]{2,1,0:T(8,128)(2,1)} %shard_map.137), calls=%async_computation.3 | async-start | bytes 1703936 | tf_op jit(solution)/shard_map/all_to_all | solution.py:416
  75.3 3.1 %collective-permute-start.4 = (bf16[256,128]{1,0:T(8,128)(2,1)S(1)}, bf16[256,128]{1,0:T(8,128)(2,1)S(1)}, u32[]{:S(2)}, u32[]{:S(2)}) collective-permute-start(bf16[256,128]{1,0:T(8,128)(2,1)S(1)} %shard_map.138.refs_0_), channel_id=1, source_target_pairs={{0,32},{16,48},{32,0},{48,16},{64,96},{80,112},{96,64},{112,80},{1... | collective-permute-start | bytes 196616 | tf_op jit(solution)/shard_map/ppermute | solution.py:420
  78.4 4.7 %collective-permute-start.5 = (bf16[256,128]{1,0:T(8,128)(2,1)S(1)}, bf16[256,128]{1,0:T(8,128)(2,1)S(1)}, u32[]{:S(2)}, u32[]{:S(2)}) collective-permute-start(bf16[256,128]{1,0:T(8,128)(2,1)S(1)} %shard_map.138.refs_0_), channel_id=1, source_target_pairs={{0,64},{16,80},{32,96},{48,112},{64,0},{80,16},{96,32},{112,48},{1... | collective-permute-start | bytes 196616 | tf_op jit(solution)/shard_map/ppermute | solution.py:420
  83.1 1.0 %shard_map.131 = bf16[128,1024]{1,0:T(8,128)(2,1)} custom-call(bf16[128,512]{1,0:T(8,128)(2,1)S(1)} %get-tuple-element.28.hid_ref, bf16[512,1024]{1,0:T(8,128)(2,1)S(1)} %copy-done), custom_call_target="tpu_custom_call" | custom-call | flops 1100000000 | bytes 1441792 | tf_op jit(solution)/shard_map/pallas_call | solution.py:400
  84.1 2.4 %collective-permute-done.5.refs_2_ = bf16[256,128]{1,0:T(8,128)(2,1)S(1)} collective-permute-done((bf16[256,128]{1,0:T(8,128)(2,1)S(1)}, bf16[256,128]{1,0:T(8,128)(2,1)S(1)}, u32[]{:S(2)}, u32[]{:S(2)}) %collective-permute-start.5) | collective-permute-done | bytes 65568 | tf_op jit(solution)/shard_map/ppermute | solution.py:420
  86.6 2.1 %collective-permute-done.6.refs_3_ = bf16[256,128]{1,0:T(8,128)(2,1)S(1)} collective-permute-done((bf16[256,128]{1,0:T(8,128)(2,1)S(1)}, bf16[256,128]{1,0:T(8,128)(2,1)S(1)}, u32[]{:S(2)}, u32[]{:S(2)}) %collective-permute-start.6) | collective-permute-done | bytes 65568 | tf_op jit(solution)/shard_map/ppermute | solution.py:420
  88.6 2.0 %all-to-all-done.3.recv_ref = bf16[16,208,128]{2,1,0:T(8,128)(2,1)S(1)} async-done(((bf16[16,208,128]{2,1,0:T(8,128)(2,1)}), bf16[16,208,128]{2,1,0:T(8,128)(2,1)S(1)}, u32[]{:S(2)}, u32[]{:S(2)}) %all-to-all-start.3) | async-done | bytes 852000 | tf_op jit(solution)/shard_map/all_to_all | solution.py:416
  90.6 0.9 %shard_map.140 = (bf16[128,512]{1,0:T(8,128)(2,1)}, bf16[128,512]{1,0:T(8,128)(2,1)}, bf16[128,512]{1,0:T(8,128)(2,1)}, bf16[128,512]{1,0:T(8,128)(2,1)}, f32[32,1024]{1,0:T(8,128)}) custom-call(bf16[16,208,128]{2,1,0:T(8,128)(2,1)S(1)} %all-to-all-done.3.recv_ref, f32[128,512]{1,0:T(8,128)S(1)} %get-tuple-element.41.ghn_ref, f32[256,128]{1,0:T(8,128)S(1)} %shard_map.139.gw_ref), custom_call_target="tpu_custom_call" | custom-call | flops 1100000000 | bytes 1900544 | tf_op jit(solution)/shard_map/pallas_call | solution.py:400
  (21 shorter events, 0.7 us)
Async XLA Ops:
  2.8 8.6 %copy-start.1 = (bf16[1,128,1024]{2,1,0:T(8,128)(2,1)S(1)}, bf16[1,128,1024]{2,1,0:T(8,128)(2,1)}, u32[]{:S(2)}) copy-start(bf16[1,128,1024]{2,1,0:T(8,128)(2,1)} %param.15) | copy-start | bytes 786436
  2.8 8.8 %copy-start.4 = (f32[4,128,64]{1,2,0:T(8,128)S(1)}, f32[4,128,64]{1,2,0:T(8,128)}, u32[]{:S(2)}) copy-start(f32[4,128,64]{1,2,0:T(8,128)} %param.12) | copy-start | bytes 393220
  2.8 8.9 %copy-start = (bf16[512,1024]{1,0:T(8,128)(2,1)S(1)}, bf16[512,1024]{1,0:T(8,128)(2,1)}, u32[]{:S(2)}) copy-start(bf16[512,1024]{1,0:T(8,128)(2,1)} %w_ref.3) | copy-start | bytes 3145732
  2.8 23.8 %all-to-all-start = ((bf16[16,208,128]{2,1,0:T(8,128)(2,1)}), bf16[16,208,128]{2,1,0:T(8,128)(2,1)S(1)}, u32[]{:S(2)}, u32[]{:S(2)}) async-start(bf16[16,208,128]{2,1,0:T(8,128)(2,1)} %shard_map.127), calls=%async_computation | async-start | bytes 1703936 | tf_op jit(solution)/shard_map/all_to_all | solution.py:416
  11.4 1.6 %collective-permute-start = (bf16[128,1024]{1,0:T(8,128)(2,1)S(1)}, bf16[128,1024]{1,0:T(8,128)(2,1)S(1)}, u32[]{:S(2)}, u32[]{:S(2)}) collective-permute-start(bf16[128,1024]{1,0:T(8,128)(2,1)S(1)} %bitcast.11), channel_id=1, source_target_pairs={{0,1},{1,0},{2,3},{3,2},{4,5},{5,4},{6,7},{7,6},{8,9},{9,8},{10,11... | collective-permute-start | bytes 786440 | tf_op jit(solution)/shard_map/ppermute | solution.py:424
  12.2 14.4 %copy-start.3 = (s32[1,8]{1,0:T(1,128)S(1)}, s32[1,8]{1,0:T(1,128)}, u32[]{:S(2)}) copy-start(s32[1,8]{1,0:T(1,128)} %lens_ref.1) | copy-start | bytes 100
  29.7 12.0 %copy-start.2 = (bf16[1,128,512]{2,1,0:T(8,128)(2,1)S(1)}, bf16[1,128,512]{2,1,0:T(8,128)(2,1)}, u32[]{:S(2)}) copy-start(bf16[1,128,512]{2,1,0:T(8,128)(2,1)} %param.11) | copy-start | bytes 393220
  42.5 1.9 %collective-permute-start.1 = (bf16[128,512]{1,0:T(8,128)(2,1)S(1)}, bf16[128,512]{1,0:T(8,128)(2,1)S(1)}, u32[]{:S(2)}, u32[]{:S(2)}) collective-permute-start(bf16[128,512]{1,0:T(8,128)(2,1)S(1)} %get-tuple-element.28.hid_ref), channel_id=1, source_target_pairs={{0,1},{1,0},{2,3},{3,2},{4,5},{5,4},{6,7},{7,6},{8,9},{9,8},{10,11... | collective-permute-start | bytes 393224 | tf_op jit(solution)/shard_map/ppermute | solution.py:424
  61.9 3.4 %collective-permute-start.2 = (bf16[256,128]{1,0:T(8,128)(2,1)S(1)}, bf16[256,128]{1,0:T(8,128)(2,1)S(1)}, u32[]{:S(2)}, u32[]{:S(2)}) collective-permute-start(bf16[256,128]{1,0:T(8,128)(2,1)S(1)} %shard_map.135.refs_0_), channel_id=1, source_target_pairs={{0,128},{16,144},{32,160},{48,176},{64,192},{80,208},{96,224},{112... | collective-permute-start | bytes 196616 | tf_op jit(solution)/shard_map/ppermute | solution.py:420
  65.3 4.5 %collective-permute-start.3 = (bf16[256,128]{1,0:T(8,128)(2,1)S(1)}, bf16[256,128]{1,0:T(8,128)(2,1)S(1)}, u32[]{:S(2)}, u32[]{:S(2)}) collective-permute-start(bf16[256,128]{1,0:T(8,128)(2,1)S(1)} %shard_map.136.refs_11_.refs_0_), channel_id=1, source_target_pairs={{0,16},{16,0},{32,48},{48,32},{64,80},{80,64},{96,112},{112,96},{1... | collective-permute-start | bytes 196616 | tf_op jit(solution)/shard_map/ppermute | solution.py:420
  69.8 20.8 %all-to-all-start.3 = ((bf16[16,208,128]{2,1,0:T(8,128)(2,1)}), bf16[16,208,128]{2,1,0:T(8,128)(2,1)S(1)}, u32[]{:S(2)}, u32[]{:S(2)}) async-start(bf16[16,208,128]{2,1,0:T(8,128)(2,1)} %shard_map.137), calls=%async_computation.3 | async-start | bytes 1703936 | tf_op jit(solution)/shard_map/all_to_all | solution.py:416
  75.3 8.8 %collective-permute-start.4 = (bf16[256,128]{1,0:T(8,128)(2,1)S(1)}, bf16[256,128]{1,0:T(8,128)(2,1)S(1)}, u32[]{:S(2)}, u32[]{:S(2)}) collective-permute-start(bf16[256,128]{1,0:T(8,128)(2,1)S(1)} %shard_map.138.refs_0_), channel_id=1, source_target_pairs={{0,32},{16,48},{32,0},{48,16},{64,96},{80,112},{96,64},{112,80},{1... | collective-permute-start | bytes 196616 | tf_op jit(solution)/shard_map/ppermute | solution.py:420
  78.4 8.2 %collective-permute-start.5 = (bf16[256,128]{1,0:T(8,128)(2,1)S(1)}, bf16[256,128]{1,0:T(8,128)(2,1)S(1)}, u32[]{:S(2)}, u32[]{:S(2)}) collective-permute-start(bf16[256,128]{1,0:T(8,128)(2,1)S(1)} %shard_map.138.refs_0_), channel_id=1, source_target_pairs={{0,64},{16,80},{32,96},{48,112},{64,0},{80,16},{96,32},{112,48},{1... | collective-permute-start | bytes 196616 | tf_op jit(solution)/shard_map/ppermute | solution.py:420
  83.1 5.5 %collective-permute-start.6 = (bf16[256,128]{1,0:T(8,128)(2,1)S(1)}, bf16[256,128]{1,0:T(8,128)(2,1)S(1)}, u32[]{:S(2)}, u32[]{:S(2)}) collective-permute-start(bf16[256,128]{1,0:T(8,128)(2,1)S(1)} %shard_map.138.refs_0_), channel_id=1, source_target_pairs={{0,96},{16,112},{32,64},{48,80},{64,32},{80,48},{96,0},{112,16},{1... | collective-permute-start | bytes 196616 | tf_op jit(solution)/shard_map/ppermute | solution.py:420
